TPU v7x, 1024 devices: a whole 4x8x16 slice. The times are simulated.
1024 devices in a mesh: dp: 64 (over x, y, core), fsdp: 16 (over z).
Axes of the slice: x: 4, y: 8, z: 16, core: 2. Of those that a mesh axis runs over, the one named last changes fastest.
Arguments:
- uvqk: bfloat16 [196608, 4096], P(('dp', 'fsdp')), may hold values from -6 to 6
- grad_out: bfloat16 [196608, 1024], P(('dp', 'fsdp')), may hold values from -24 to 24
- w_out: bfloat16 [1024, 1024], P('fsdp'), may hold values from -0.1875 to 0.1875
- kept_segments: int32 [1024, 64], P(('dp', 'fsdp')), may hold values from 0 to 3, never falling along the last dimension, each value on 1 to 32 neighbouring positions
- moved_lengths: int32 [1024, 3], replicated, may hold values from 0 to 128, as said below
- dest_device: int32 [64], replicated, may hold values from 0 to 63, each once
Outputs:
- grad_uvqk: bfloat16 [196608, 4096], P(('dp', 'fsdp'))
- grad_w_out: float32 [1024, 1024], P('fsdp')
Inputs may be any that keep to these rules, and one draw needn't show every extreme that they name: `moved_lengths`: the histories of one row sum to at most 128; in every draw some device's block is one history of 128 events.
All inputs are finite; a program needn't handle non-finite values.
Results may differ from a plain program's by a relative error of at most 0.02.
Values may be sent and summed in bfloat16 or wider, within the bound.
No kernel may reach another device: no remote copies, remote signals or barrier semaphores. Data moves between devices by JAX's collectives and lax.ppermute only.
A program may use at most 32 MiB of HBM per device.

v0:
```python
import math

import jax
import jax.numpy as jnp
from jax import lax
from jax.sharding import PartitionSpec as P

HEADS = 4


EPS = 1e-05


def as_sent(value):

    def short(part):
        return part.astype(jnp.bfloat16) if part.dtype == jnp.float32 else part

    return jax.tree.map(short, value)


def silu_slope(scores):
    sigma = jax.nn.sigmoid(scores)
    return sigma * (1.0 + scores * (1.0 - sigma))


def attend(gate, others, segments):
    length, model_width = gate.shape
    head_dim = model_width // HEADS
    score_scale = 1.0 / math.sqrt(head_dim)
    split_rest = others.reshape(length, 3, HEADS, head_dim)
    values = split_rest[:, 0]
    queries = split_rest[:, 1]
    key_rows = split_rest[:, 2]
    positions = jnp.arange(length, dtype=jnp.int32)
    same_history = segments[:, None] == segments[None, :]
    allowed = same_history & (positions[None, :] <= positions[:, None]) & (segments >= 0)[:, None]
    counts = jnp.sum(same_history.astype(jnp.float32), axis=1)
    scores = (
        jnp.einsum("ihe,jhe->hij", queries, key_rows, preferred_element_type=jnp.float32)
        * score_scale
    )
    weights = (jnp.where(allowed[None], jax.nn.silu(scores), 0.0) / counts[None, :, None]).astype(
        jnp.bfloat16
    )
    mixed = jnp.einsum("hij,jhe->ihe", weights, values, preferred_element_type=jnp.float32)
    mixed = mixed.reshape(length, model_width)
    centered = mixed - jnp.mean(mixed, axis=1, keepdims=True)
    inverse = lax.rsqrt(jnp.mean(centered * centered, axis=1, keepdims=True) + EPS)
    normed = centered * inverse
    gate_float = gate.astype(jnp.float32)
    output_rows = (normed * gate_float).astype(jnp.bfloat16)
    return (
        scores,
        allowed,
        counts,
        weights,
        normed,
        inverse,
        gate_float,
        values,
        queries,
        key_rows,
        output_rows,
    )


def attention_back(stored, grad_y):
    (
        scores,
        allowed,
        counts,
        weights,
        normed,
        inverse,
        gate_float,
        values,
        queries,
        key_rows,
        output_rows,
    ) = stored
    length, model_width = normed.shape
    head_dim = model_width // HEADS
    score_scale = 1.0 / math.sqrt(head_dim)
    grad_gate = (grad_y * normed).astype(jnp.bfloat16)
    grad_normed = grad_y * gate_float
    grad_mixed = inverse * (
        grad_normed
        - jnp.mean(grad_normed, axis=1, keepdims=True)
        - normed * jnp.mean(grad_normed * normed, axis=1, keepdims=True)
    )
    grad_mixed = grad_mixed.astype(jnp.bfloat16).reshape(length, HEADS, head_dim)
    grad_weights = jnp.einsum(
        "ihe,jhe->hij", grad_mixed, values, preferred_element_type=jnp.float32
    )
    grad_values = jnp.einsum(
        "hij,ihe->jhe", weights, grad_mixed, preferred_element_type=jnp.float32
    )
    grad_values = grad_values.astype(jnp.bfloat16)
    grad_scores = (
        jnp.where(allowed[None], grad_weights * silu_slope(scores), 0.0)
        * score_scale
        / counts[None, :, None]
    )
    grad_scores = grad_scores.astype(jnp.bfloat16)
    grad_queries = jnp.einsum(
        "hij,jhe->ihe", grad_scores, key_rows, preferred_element_type=jnp.float32
    )
    grad_keys = jnp.einsum("hij,ihe->jhe", grad_scores, queries, preferred_element_type=jnp.float32)
    return jnp.concatenate(
        [
            grad_gate,
            grad_values.reshape(length, model_width),
            grad_queries.astype(jnp.bfloat16).reshape(length, model_width),
            grad_keys.astype(jnp.bfloat16).reshape(length, model_width),
        ],
        axis=1,
    )


def arrange(pieces, order, groups):
    return tuple(
        (
            piece.reshape((groups, -1) + piece.shape[1:])[order].reshape(piece.shape)
            for piece in pieces
        )
    )


def relocate(blocks, order):
    groups = lax.axis_size("dp")
    shares = (
        lax.all_to_all(blocks[0], "dp", split_axis=1, concat_axis=0, tiled=True),
        lax.all_to_all(blocks[1], "dp", split_axis=1, concat_axis=0, tiled=True),
    )
    return lax.all_to_all(
        as_sent(arrange(shares, order, groups)), "dp", split_axis=0, concat_axis=1, tiled=True
    )


def local(uvqk, grad_out, w_out, kept_segments, moved_lengths, dest_device):
    keep_rows = kept_segments.shape[1]
    model_width = grad_out.shape[1]
    moved_rows = uvqk.shape[0] - keep_rows
    history_count = moved_lengths.shape[1]
    groups = lax.axis_size("dp")
    indices = jnp.arange(groups, dtype=jnp.int32)
    source_of = jnp.sum(
        jnp.where(dest_device[None, :] == indices[:, None], indices[None, :], 0), axis=1
    )
    source_row = source_of[lax.axis_index("dp")] * lax.axis_size("fsdp") + lax.axis_index("fsdp")
    lengths = lax.dynamic_index_in_dim(moved_lengths, source_row, 0, keepdims=False)
    ends = jnp.cumsum(lengths)
    places = jnp.arange(moved_rows, dtype=jnp.int32)
    seg_ids = jnp.sum((places[:, None] >= ends[None, :]).astype(jnp.int32), axis=1)
    recv_segments = jnp.where(seg_ids == history_count, -1, seg_ids)
    received_in, received_grad = relocate((uvqk[keep_rows:], grad_out[keep_rows:]), source_of)
    stored_kept = attend(
        uvqk[:keep_rows, :model_width], uvqk[:keep_rows, model_width:], kept_segments[0]
    )
    stored_recv = attend(received_in[:, :model_width], received_in[:, model_width:], recv_segments)
    grads_all = jnp.concatenate([grad_out[:keep_rows], received_grad], axis=0)
    outputs_all = jnp.concatenate([stored_kept[-1], stored_recv[-1]], axis=0)
    columns = grads_all
    grad_outputs = jnp.dot(
        columns,
        lax.all_gather(w_out, "fsdp", axis=0, tiled=True),
        preferred_element_type=jnp.float32,
    )
    columns = grads_all
    group_sum = lax.psum_scatter(
        lax.dot_general(
            columns, outputs_all, (((0,), (0,)), ((), ())), preferred_element_type=jnp.float32
        ).astype(jnp.bfloat16),
        "fsdp",
        scatter_dimension=0,
        tiled=True,
    ).astype(jnp.float32)
    grad_weight = lax.psum(group_sum, "dp") / (lax.axis_size("dp") * lax.axis_size("fsdp"))
    kept_back = attention_back(stored_kept, grad_outputs[:keep_rows])
    recv_back = attention_back(stored_recv, grad_outputs[keep_rows:])
    return (jnp.concatenate([kept_back, recv_back], axis=0), grad_weight)


def solution(mesh):
    placed = (
        P(("dp", "fsdp"), None),
        P(("dp", "fsdp"), None),
        P("fsdp", None),
        P(("dp", "fsdp"), None),
        P(),
        P(),
    )
    return jax.shard_map(
        local,
        mesh=mesh,
        in_specs=placed,
        out_specs=(P(("dp", "fsdp"), None), P("fsdp", None)),
        check_vma=False,
    )
```

profile of v0, /device:TPU:1, one launch (start us, length us, event | category | flops | bytes accessed | tf_op | source)
XLA Modules:
  0.0 466.2 jit_solution(5799545070055750363)
XLA Ops:
  7.2 1.1 slice.46
  8.3 0.8 copy.114
  9.1 18.2 %all-to-all-start = ((bf16[128,64,16]{0,2,1:T(8,128)(2,1)}), bf16[128,64,16]{0,2,1:T(8,128)(2,1)S(1)}, u32[]{:S(2)}, u32[]{:S(2)}) async-start(bf16[128,64,16]{0,2,1:T(8,128)(2,1)} %bitcast), calls=%async_computation | async-start | bytes 524288 | tf_op jit(solution)/shard_map/all_to_all | solution.py:134
  27.3 1.3 copy.118
  28.7 10.7 %all-to-all-done = bf16[128,64,16]{0,2,1:T(8,128)(2,1)S(1)} async-done(((bf16[128,64,16]{0,2,1:T(8,128)(2,1)}), bf16[128,64,16]{0,2,1:T(8,128)(2,1)S(1)}, u32[]{:S(2)}, u32[]{:S(2)}) %all-to-all-start) | async-done | bytes 262176 | tf_op jit(solution)/shard_map/all_to_all | solution.py:134
  39.3 6.1 %all-to-all-start.2 = ((bf16[128,64,64]{0,2,1:T(8,128)(2,1)}), bf16[128,64,64]{0,2,1:T(8,128)(2,1)S(1)}, u32[]{:S(2)}, u32[]{:S(2)}) async-start(bf16[128,64,64]{0,2,1:T(8,128)(2,1)} %bitcast.14), calls=%async_computation.2 | async-start | bytes 2097152 | tf_op jit(solution)/shard_map/all_to_all | solution.py:133
  45.5 0.7 all-gather.2.cloned.1.call-update
  46.4 0.7 fusion.36
  47.1 1.3 gather_fusion
  48.4 25.6 %all-to-all-done.2 = bf16[128,64,64]{0,2,1:T(8,128)(2,1)S(1)} async-done(((bf16[128,64,64]{0,2,1:T(8,128)(2,1)}), bf16[128,64,64]{0,2,1:T(8,128)(2,1)S(1)}, u32[]{:S(2)}, u32[]{:S(2)}) %all-to-all-start.2) | async-done | bytes 1048608 | tf_op jit(solution)/shard_map/all_to_all | solution.py:133
  74.0 6.4 %all-to-all-start.1 = ((bf16[64,128,16]{1,2,0:T(8,128)(2,1)}), bf16[64,128,16]{1,2,0:T(8,128)(2,1)}, u32[]{:S(2)}, u32[]{:S(2)}) async-start(bf16[64,128,16]{1,2,0:T(8,128)(2,1)} %gather_fusion), calls=%async_computation.1 | async-start | bytes 524288 | tf_op jit(solution)/shard_map/all_to_all | solution.py:136
  80.4 0.7 fusion.35
  81.1 0.3 reshape.277
  81.4 0.8 fusion.40
  82.2 0.8 convolution_multiply_fusion.3
  83.0 1.8 gather_fusion.1
  84.8 7.5 %all-to-all-done.1 = bf16[64,128,16]{1,2,0:T(8,128)(2,1)} async-done(((bf16[64,128,16]{1,2,0:T(8,128)(2,1)}), bf16[64,128,16]{1,2,0:T(8,128)(2,1)}, u32[]{:S(2)}, u32[]{:S(2)}) %all-to-all-start.1) | async-done | bytes 262176 | tf_op jit(solution)/shard_map/all_to_all | solution.py:136
  92.3 6.0 %all-to-all-start.3 = ((bf16[64,128,64]{1,2,0:T(8,128)(2,1)}), bf16[64,128,64]{1,2,0:T(8,128)(2,1)S(1)}, u32[]{:S(2)}, u32[]{:S(2)}) async-start(bf16[64,128,64]{1,2,0:T(8,128)(2,1)} %gather_fusion.1), calls=%async_computation.3 | async-start | bytes 2097152 | tf_op jit(solution)/shard_map/all_to_all | solution.py:136
  98.6 0.9 fusion.42
  99.5 0.6 dynamic_slice.7
  101.0 0.7 reduce-window.8
  101.9 0.8 convert_reduce_fusion
  102.7 0.7 fusion.32
  103.4 0.7 broadcast_multiply_fusion.6
  104.3 0.4 copy-done.23
  104.7 0.7 fusion.33
  105.4 12.7 %all-gather.2.cloned.1.call-done = bf16[1024,1024]{1,0:T(8,128)(2,1)} async-done(((bf16[64,1024]{1,0:T(8,128)(2,1)}), bf16[1024,1024]{1,0:T(8,128)(2,1)}) %all-gather.2.cloned.1.call-update) | async-done | bytes 2097168 | tf_op jit(solution)/shard_map/all_gather | solution.py:167
  118.1 2.4 fusion.17
  120.5 0.9 copy-done.2
  121.4 1.5 fusion.34
  122.9 4.0 all-to-all-done.3
  126.9 0.7 slice.73
  127.7 1.1 copy.121
  128.8 0.3 convolution_multiply_fusion.1
  129.1 1.1 fusion.41
  130.4 0.6 add_rsqrt_fusion
  131.0 1.2 copy.109
  132.3 1.3 fusion.26
  133.6 2.0 multiply_convert_fusion.1
  135.7 3.1 convolution_convert_fusion
  138.9 1.2 multiply_convert_fusion.2
  140.1 1.0 fusion.4
  141.9 0.3 convolution_convert_fusion.3
  142.4 0.2 fusion.3
  143.4 7.0 %maximum_maximum_fusion = bf16[192,4096]{1,0:T(8,128)(2,1)} fusion(bf16[128,1024]{1,0:T(8,128)(2,1)S(1)} %copy.112, bf16[128,1024]{1,0:T(8,128)(2,1)S(1)} %copy.111, bf16[128,1024]{1,0:T(8,128)(2,1)S(1)} %copy.110, bf16[128,1024]{1,0:T(8,128)(2,1)S(1)} %get-tuple-element.7, bf16[64,1024]{1,0:T(8,128)(2,1)S(1)} %bitcast.123, ...), kind=kLoop, calls=%fused_computation.3 | loop fusion | flops 12582912 | bytes 3145728 | tf_op jit(solution)/shard_map/concatenate | solution.py:182
  150.4 56.0 %reduce-scatter.2.cloned.1.call-done = bf16[64,1024]{1,0:T(8,128)(2,1)} async-done(((bf16[1024,1024]{1,0:T(8,128)(2,1)}), bf16[64,1024]{1,0:T(8,128)(2,1)}) %reduce-scatter.2.cloned.1.call-update) | async-done | bytes 131088 | tf_op jit(solution)/shard_map/reduce_scatter | solution.py:171
  206.4 252.3 %all-reduce.1 = f32[64,1024]{1,0:T(8,128)S(1)} all-reduce(bf16[64,1024]{1,0:T(8,128)(2,1)} %reduce-scatter.2.cloned.1.call-done), channel_id=1, replica_groups=mesh['dp'=64,'fsdp'=16] {'dp'}, use_global_device_ids=true, to_apply=%region_14.15 | all-reduce | flops 65536 | bytes 393216 | tf_op jit(solution)/shard_map/psum | solution.py:179
  458.6 0.7 broadcast_multiply_fusion
  (109 shorter events, 2.9 us)
Async XLA Ops:
  7.2 93.6 %copy-start = (s32[1024,3]{0,1:T(4,128)S(1)}, s32[1024,3]{0,1:T(4,128)}, u32[]{:S(2)}) copy-start(s32[1024,3]{0,1:T(4,128)} %param.10) | copy-start | bytes 36868
  7.2 20.1 %slice-start = ((bf16[192,4096]{1,0:T(8,128)(2,1)}), bf16[128,4096]{1,0:T(8,128)(2,1)S(1)}, s32[]{:S(2)}) async-start(bf16[192,4096]{1,0:T(8,128)(2,1)} %param.6), calls=%async_computation.7 | async-start | bytes 2097152 | tf_op jit(solution)/shard_map/slice | solution.py:157
  9.1 30.2 %all-to-all-start = ((bf16[128,64,16]{0,2,1:T(8,128)(2,1)}), bf16[128,64,16]{0,2,1:T(8,128)(2,1)S(1)}, u32[]{:S(2)}, u32[]{:S(2)}) async-start(bf16[128,64,16]{0,2,1:T(8,128)(2,1)} %bitcast), calls=%async_computation | async-start | bytes 524288 | tf_op jit(solution)/shard_map/all_to_all | solution.py:134
  27.3 18.9 %copy-start.32 = (s32[64]{0:T(128)S(1)}, s32[64]{0:T(128)}, u32[]{:S(2)}) copy-start(s32[64]{0:T(128)} %param.11) | copy-start | bytes 772
  27.3 19.0 %copy-start.31 = (s32[1,64]{1,0:T(1,128)S(1)}, s32[1,64]{1,0:T(1,128)}, u32[]{:S(2)}) copy-start(s32[1,64]{1,0:T(1,128)} %param.9) | copy-start | bytes 772
  39.3 34.7 %all-to-all-start.2 = ((bf16[128,64,64]{0,2,1:T(8,128)(2,1)}), bf16[128,64,64]{0,2,1:T(8,128)(2,1)S(1)}, u32[]{:S(2)}, u32[]{:S(2)}) async-start(bf16[128,64,64]{0,2,1:T(8,128)(2,1)} %bitcast.14), calls=%async_computation.2 | async-start | bytes 2097152 | tf_op jit(solution)/shard_map/all_to_all | solution.py:133
  45.5 72.7 %all-gather.2.cloned.1.call-start = ((), (), s32[]{:S(2)}) async-start(), calls=%async_computation.5 | async-start | bytes 2228224 | tf_op jit(solution)/shard_map/all_gather | solution.py:167
  46.3 0.8 copy-start.36
  46.4 2.0 copy-start.22
  47.1 34.0 %copy-start.1 = (bf16[192,4096]{1,0:T(8,128)(2,1)S(1)}, bf16[192,4096]{1,0:T(8,128)(2,1)}, u32[]{:S(2)}) copy-start(bf16[192,4096]{1,0:T(8,128)(2,1)} %param.6) | copy-start | bytes 4718596
  74.0 18.3 %all-to-all-start.1 = ((bf16[64,128,16]{1,2,0:T(8,128)(2,1)}), bf16[64,128,16]{1,2,0:T(8,128)(2,1)}, u32[]{:S(2)}, u32[]{:S(2)}) async-start(bf16[64,128,16]{1,2,0:T(8,128)(2,1)} %gather_fusion), calls=%async_computation.1 | async-start | bytes 524288 | tf_op jit(solution)/shard_map/all_to_all | solution.py:136
  82.2 2.6 copy-start.6
  84.8 13.8 %copy-start.15 = (f32[4,64,64]{2,1,0:T(8,128)S(1)}, f32[4,64,64]{2,1,0:T(8,128)}, u32[]{:S(2)}) copy-start(f32[4,64,64]{2,1,0:T(8,128)} %convolution_multiply_fusion.3) | copy-start | bytes 196612
  84.8 13.8 %copy-start.17 = (bf16[64,1,4,256]{3,2,1,0:T(4,128)(2,1)S(1)}, bf16[64,1,4,256]{3,2,1,0:T(4,128)(2,1)}, u32[]{:S(2)}) copy-start(bf16[64,1,4,256]{3,2,1,0:T(4,128)(2,1)} %get-tuple-element.11) | copy-start | bytes 393220
  84.8 13.8 %copy-start.20 = (pred[64,64]{1,0:T(8,128)(4,1)S(1)}, pred[64,64]{1,0:T(8,128)(4,1)}, u32[]{:S(2)}) copy-start(pred[64,64]{1,0:T(8,128)(4,1)} %fusion.36) | copy-start | bytes 12292
  84.8 13.8 %copy-start.33 = (f32[64]{0:T(128)S(1)}, f32[64]{0:T(128)}, u32[]{:S(2)}) copy-start(f32[64]{0:T(128)} %fusion.35) | copy-start | bytes 772
  84.8 14.8 %copy-start.37 = (s32[64]{0:T(128)S(1)}, s32[64]{0:T(128)}, u32[]{:S(2)}) copy-start(s32[64]{0:T(128)} %copy-done.36) | copy-start | bytes 772
  84.8 16.9 %slice-start.1 = ((bf16[192,1024]{1,0:T(8,128)(2,1)}), bf16[64,1024]{1,0:T(8,128)(2,1)S(1)}, s32[]{:S(2)}) async-start(bf16[192,1024]{1,0:T(8,128)(2,1)} %param.7), calls=%async_computation.8 | async-start | bytes 262144 | tf_op jit(solution)/shard_map/slice | solution.py:162
  92.3 34.6 %all-to-all-start.3 = ((bf16[64,128,64]{1,2,0:T(8,128)(2,1)}), bf16[64,128,64]{1,2,0:T(8,128)(2,1)S(1)}, u32[]{:S(2)}, u32[]{:S(2)}) async-start(bf16[64,128,64]{1,2,0:T(8,128)(2,1)} %gather_fusion.1), calls=%async_computation.3 | async-start | bytes 2097152 | tf_op jit(solution)/shard_map/all_to_all | solution.py:136
  98.4 108.0 %reduce-scatter.2.cloned.1.call-start = ((), (), s32[]{:S(2)}) async-start(), calls=%async_computation.6 | async-start | bytes 2228224 | tf_op jit(solution)/shard_map/reduce_scatter | solution.py:171
  101.9 18.7 %copy-start.8 = (bf16[64,1024]{0,1:T(8,128)(2,1)}, bf16[64,1024]{0,1:T(8,128)(2,1)S(1)}, u32[]{:S(2)}) copy-start(bf16[64,1024]{0,1:T(8,128)(2,1)S(1)} %copy.113) | copy-start | bytes 393220
  101.9 21.0 %copy-start.3 = (f32[4,8,8,256]{3,2,0,1:T(8,128)}, f32[4,8,8,256]{3,2,0,1:T(8,128)S(1)}, u32[]{:S(2)}) copy-start(f32[4,8,8,256]{3,2,0,1:T(8,128)S(1)} %copy.124) | copy-start | bytes 786436
  104.1 0.6 copy-start.23
  104.6 16.8 %copy-start.24 = (f32[64]{0:T(128)S(1)}, f32[64]{0:T(128)}, u32[]{:S(2)}) copy-start(f32[64]{0:T(128)} %copy-done.23) | copy-start | bytes 772
  104.7 18.3 %copy-start.27 = (f32[64]{0:T(128)}, f32[64]{0:T(128)S(1)}, u32[]{:S(2)}) copy-start(f32[64]{0:T(128)S(1)} %add_rsqrt_fusion.1) | copy-start | bytes 772
  120.5 0.9 copy-start.2
  129.1 3.2 copy-start.12
  130.2 0.8 copy-start.5
  130.2 0.8 copy-start.26
  132.3 3.4 copy-start.9
  132.3 3.4 copy-start.11
  135.7 3.2 copy-start.29
  135.7 3.2 copy-start.30
  135.7 3.2 copy-start.4
  135.7 3.2 copy-start.25
  135.7 3.2 copy-start.28
  138.8 1.3 copy-start.16
  138.8 2.4 copy-start.18
  138.8 2.4 copy-start.21
  138.8 2.4 copy-start.34
  138.8 2.6 copy-start.7
  140.1 1.8 copy-start.13
  140.1 1.8 copy-start.14
  140.1 1.8 copy-start.19
  140.1 1.8 copy-start.35
  142.4 1.0 copy-start.10
Sparse Core Ops, SparseCore 0:
  49.0 69.1 all-gather.1
  138.9 67.3 reduce-scatter.1
where the time goes:
time: 470 us; the launch traced here: 466 us
  blocking collectives  252 us (54%)
  waiting for transfers between devices  117 us (25%)
  starting transfers between devices  37 us (8%)
  other arithmetic  19.7 us (4%)
  between operations  15.4 us (3%)
  local copies, waits for them, and re-layouts  13.4 us (3%)
  matrix products  11.2 us (2%)
    psum x1, blocking collectives, local(): lax.psum(group_sum, 'dp') / (lax.axis_size('dp') * lax.axis_size('fsdp'))  252 us
    reduce_scatter x1, waiting for transfers between devices, local(): lax.psum_scatter(lax.dot_general(columns, outputs_all, (((0,), (0,)), (()...  56 us
    all_to_all x1, waiting for transfers between devices, relocate(): lax.all_to_all(blocks[0], 'dp', split_axis=1, concat_axis=0, tiled=True)  25.6 us
    all_to_all x1, starting transfers between devices, relocate(): lax.all_to_all(blocks[1], 'dp', split_axis=1, concat_axis=0, tiled=True)  18.2 us
    all_gather x1, waiting for transfers between devices, local(): lax.all_gather(w_out, 'fsdp', axis=0, tiled=True)  12.7 us
    all_to_all x2, starting transfers between devices, relocate(): lax.all_to_all(as_sent(arrange(shares, order, groups)), 'dp', split_axis=...  12.4 us
    all_to_all x2, waiting for transfers between devices, relocate(): lax.all_to_all(as_sent(arrange(shares, order, groups)), 'dp', split_axis=...  11.5 us
    all_to_all x1, waiting for transfers between devices, relocate(): lax.all_to_all(blocks[1], 'dp', split_axis=1, concat_axis=0, tiled=True)  10.7 us
  transfers between devices with their start and end apart: 6, of which 6 were waited for; matrix products, arithmetic and copies ran while one was open for 6% of the time, Pallas kernels for 0%

commit v1 on v0

v1 whole, which is shorter than its diff:
```python
import functools
import math

import jax
import jax.numpy as jnp
from jax import lax
from jax.experimental import pallas as pl
from jax.experimental.pallas import tpu as pltpu
from jax.sharding import Mesh
from jax.sharding import PartitionSpec as P

HEADS = 4
EPS = 1e-05
GROUP_ROWS = 16
BF16 = jnp.bfloat16
F32 = jnp.float32
DP = ("x", "y", "core")


def dot(a, b, dims):
    return lax.dot_general(a, b, (dims, ((), ())), preferred_element_type=F32)


def segments_of(ends, shape, dim):
    places = lax.broadcasted_iota(jnp.int32, shape, dim)
    passed = jnp.zeros(shape, jnp.int32)
    for end in ends:
        passed = passed + (places >= end).astype(jnp.int32)
    return jnp.where(passed == len(ends), -1, passed)


def masks(seg_column, seg_row):
    length = seg_column.shape[0]
    square = (length, length)
    same = seg_column == seg_row
    earlier = lax.broadcasted_iota(jnp.int32, square, 1) <= lax.broadcasted_iota(jnp.int32, square, 0)
    allowed = same & earlier & (seg_column >= 0)
    counts = jnp.sum(same.astype(F32), axis=1, keepdims=True)
    return allowed, counts


def forward(values, queries, key_rows, allowed, counts):
    width = values.shape[1]
    head_dim = width // HEADS
    scale = 1.0 / math.sqrt(head_dim)
    scores, sigmas, weights, mixed = [], [], [], []
    for h in range(HEADS):
        cols = slice(h * head_dim, (h + 1) * head_dim)
        s = dot(queries[:, cols], key_rows[:, cols], ((1,), (1,))) * scale
        sigma = jax.nn.sigmoid(s)
        w = (jnp.where(allowed, s * sigma, 0.0) / counts).astype(BF16)
        scores.append(s)
        sigmas.append(sigma)
        weights.append(w)
        mixed.append(dot(w, values[:, cols], ((1,), (0,))))
    mixed = jnp.concatenate(mixed, axis=1)
    centered = mixed - jnp.mean(mixed, axis=1, keepdims=True)
    inverse = lax.rsqrt(jnp.mean(centered * centered, axis=1, keepdims=True) + EPS)
    return scores, sigmas, weights, centered * inverse, inverse


def backward(gate, values, queries, key_rows, grad_y, allowed, counts, put):
    width = values.shape[1]
    head_dim = width // HEADS
    scale = 1.0 / math.sqrt(head_dim)
    scores, sigmas, weights, normed, inverse = forward(values, queries, key_rows, allowed, counts)
    put(0, slice(0, width), grad_y * normed)
    grad_normed = grad_y * gate.astype(F32)
    grad_mixed = inverse * (
        grad_normed
        - jnp.mean(grad_normed, axis=1, keepdims=True)
        - normed * jnp.mean(grad_normed * normed, axis=1, keepdims=True)
    )
    grad_mixed = grad_mixed.astype(BF16)
    factor = scale / counts
    for h in range(HEADS):
        cols = slice(h * head_dim, (h + 1) * head_dim)
        s, sigma = scores[h], sigmas[h]
        grad_weights = dot(grad_mixed[:, cols], values[:, cols], ((1,), (1,)))
        put(1, cols, dot(weights[h], grad_mixed[:, cols], ((0,), (0,))))
        slope = sigma * (1.0 + s * (1.0 - sigma))
        grad_scores = (jnp.where(allowed, grad_weights * slope, 0.0) * factor).astype(BF16)
        put(2, cols, dot(grad_scores, key_rows[:, cols], ((1,), (0,))))
        put(3, cols, dot(grad_scores, queries[:, cols], ((0,), (0,))))


def shares(row_groups, col_groups, share_cols):
    for r in range(row_groups):
        for c in range(col_groups):
            yield r * col_groups + c, r * GROUP_ROWS, c * share_cols


def pack_kernel(keep, x_ref, g_ref, out_ref):
    width, joint = x_ref.shape[1], x_ref.shape[1] + g_ref.shape[1]
    row_groups = (x_ref.shape[0] - keep) // GROUP_ROWS
    share_cols = out_ref.shape[2]
    for share, row, start in shares(row_groups, joint // share_cols, share_cols):
        rows = pl.ds(keep + row, GROUP_ROWS)
        split = min(max(width - start, 0), share_cols)
        if split > 0:
            out_ref[share, :, pl.ds(0, split)] = x_ref[rows, pl.ds(start, split)]
        if split < share_cols:
            out_ref[share, :, pl.ds(split, share_cols - split)] = g_ref[
                rows, pl.ds(start + split - width, share_cols - split)
            ]


def term_kernel(keep, lengths_ref, x_ref, g_ref, seg_col_ref, seg_row_ref, term_ref, y_ref):
    width = g_ref.shape[1]
    rows_all = x_ref.shape[0]

    def rows_of(rows, allowed, counts):
        values, queries, key_rows = (x_ref[rows, pl.ds((1 + i) * width, width)] for i in range(3))
        normed = forward(values, queries, key_rows, allowed, counts)[3]
        y_ref[rows, :] = (normed * x_ref[rows, pl.ds(0, width)].astype(F32)).astype(BF16)

    moved = rows_all - keep
    total, ends = 0, []
    for i in range(lengths_ref.shape[1]):
        total = total + lengths_ref[0, i]
        ends.append(total)
    rows_of(pl.ds(keep, moved), *masks(segments_of(ends, (moved, 1), 0), segments_of(ends, (1, moved), 1)))
    rows_of(pl.ds(0, keep), *masks(seg_col_ref[...], seg_row_ref[...]))
    blocks, _, block_cols = term_ref.shape
    joined = max(1, 256 // block_cols)
    for b in range(0, blocks, joined):
        found = dot(g_ref[...], y_ref[:, pl.ds(b * block_cols, joined * block_cols)], ((0,), (0,)))
        for i in range(joined):
            term_ref[b + i] = found[:, i * block_cols : (i + 1) * block_cols].astype(BF16)


def back_kernel(keep, lengths_ref, x_ref, g_ref, came_ref, w_ref, seg_col_ref, seg_row_ref, out_ref, block_ref):
    width = g_ref.shape[1]
    moved, joint = block_ref.shape
    share_cols = came_ref.shape[2]
    for share, row, start in shares(moved // GROUP_ROWS, joint // share_cols, share_cols):
        block_ref[pl.ds(row, GROUP_ROWS), pl.ds(start, share_cols)] = came_ref[share]

    def put_in(rows):
        def put(part, cols, found):
            out_ref[rows, pl.ds(part * width + cols.start, cols.stop - cols.start)] = found.astype(BF16)

        return put

    total, ends = 0, []
    for i in range(lengths_ref.shape[1]):
        total = total + lengths_ref[0, i]
        ends.append(total)
    kept_grad_y = dot(g_ref[pl.ds(0, keep), :], w_ref[...], ((1,), (0,)))
    parts = [x_ref[pl.ds(0, keep), pl.ds(i * width, width)] for i in range(4)]
    backward(*parts, kept_grad_y, *masks(seg_col_ref[...], seg_row_ref[...]), put_in(pl.ds(0, keep)))
    *parts, grads = [block_ref[:, pl.ds(i * width, width)] for i in range(5)]
    grad_y = dot(grads, w_ref[...], ((1,), (0,)))
    backward(
        *parts,
        grad_y,
        *masks(segments_of(ends, (moved, 1), 0), segments_of(ends, (1, moved), 1)),
        put_in(pl.ds(keep, moved)),
    )


VMEM = pl.BlockSpec(memory_space=pltpu.VMEM)
SMEM = pl.BlockSpec(memory_space=pltpu.SMEM)
PARAMS = pltpu.CompilerParams(vmem_limit_bytes=40 * 2**20)


def cost(flops, nbytes):
    return pl.CostEstimate(flops=flops, bytes_accessed=nbytes, transcendentals=0)


def permuted(value, axis, target):
    size = lax.axis_size(axis)
    return lax.ppermute(value, axis, [(i, target(i)) for i in range(size)])


def pick(value, index, dim=0):
    return lax.dynamic_index_in_dim(value, index, dim, keepdims=False)


def added(*values):
    return functools.reduce(jnp.add, [value.astype(F32) for value in values])


def scatter_sum(value, axis):
    size, me = lax.axis_size(axis), lax.axis_index(axis)
    came = [
        permuted(pick(value, (me + step) & (size - 1)), axis, lambda i, step=step: (i + step) % size)
        for step in range(1, size)
    ]
    return added(pick(value, me), *came).astype(BF16)


def halving_sum(value, axis):
    size, me = lax.axis_size(axis), lax.axis_index(axis)
    steps = size.bit_length() - 1
    for step in range(steps):
        pairs = value.reshape((value.shape[0] // 2, 2) + value.shape[1:])
        mine = (me >> step) & 1
        came = permuted(pick(pairs, 1 - mine, 1), axis, lambda i, step=step: i ^ (1 << step))
        value = added(pick(pairs, mine, 1), came)
        if step < steps - 1:
            value = value.astype(BF16)
    return value[0]


def doubling_sum(value, axis):
    for step in range(lax.axis_size(axis).bit_length() - 1):
        value = value + permuted(value, axis, lambda i, step=step: i ^ (1 << step))
    return value


def doubling_gather(value, axis):
    me = lax.axis_index(axis)
    for step in range(lax.axis_size(axis).bit_length() - 1):
        came = permuted(value, axis, lambda i, step=step: i ^ (1 << step))
        low = ((me >> step) & 1) == 0
        value = jnp.concatenate([jnp.where(low, value, came), jnp.where(low, came, value)], axis=1)
    return value


def exchange(value):
    return lax.all_to_all(value, DP, split_axis=0, concat_axis=0, tiled=True)


def local(uvqk, grad_out, w_out, kept_segments, moved_lengths, dest_device):
    keep = kept_segments.shape[1]
    rows, width = grad_out.shape
    moved = rows - keep
    n_x, n_y, n_core, n_z = (lax.axis_size(a) for a in ("x", "y", "core", "z"))
    groups = n_x * n_y * n_core
    dp_index, z_index = lax.axis_index(DP), lax.axis_index("z")
    indices = jnp.arange(groups, dtype=jnp.int32)
    source_of = jnp.sum(jnp.where(dest_device[None, :] == indices[:, None], indices[None, :], 0), axis=1)
    own_source = jnp.sum(jnp.where(dest_device == dp_index, indices, 0))
    own_lengths = lax.dynamic_slice_in_dim(moved_lengths, dp_index * n_z + z_index, 1, 0)
    recv_lengths = lax.dynamic_slice_in_dim(moved_lengths, own_source * n_z + z_index, 1, 0)
    seg_col, seg_row = kept_segments.reshape(keep, 1), kept_segments

    w_all = lax.all_gather(w_out, "z", axis=0, tiled=True)
    share_cols = 5 * width * (moved // GROUP_ROWS) // groups
    block = pl.pallas_call(
        functools.partial(pack_kernel, keep),
        out_shape=jax.ShapeDtypeStruct((groups, GROUP_ROWS, share_cols), BF16),
        in_specs=[VMEM, VMEM],
        out_specs=VMEM,
        compiler_params=PARAMS,
        cost_estimate=cost(0, 10 * moved * 5 * width),
        name="pack",
    )(uvqk, grad_out)
    uvqk, grad_out, block = lax.optimization_barrier((uvqk, grad_out, block))
    block = exchange(block)

    blocks = n_core * n_x
    block_cols = width // blocks
    term = pl.pallas_call(
        functools.partial(term_kernel, keep),
        out_shape=jax.ShapeDtypeStruct((blocks, width, block_cols), BF16),
        in_specs=[SMEM, VMEM, VMEM, VMEM, VMEM],
        out_specs=VMEM,
        scratch_shapes=[pltpu.VMEM((rows, width), BF16)],
        compiler_params=PARAMS,
        cost_estimate=cost(4 * rows * width * width, 8 * width * width),
        name="term",
    )(own_lengths, uvqk, grad_out, seg_col, seg_row)
    part = scatter_sum(term.reshape(n_core, n_x, width, block_cols), "core")
    part = scatter_sum(part, "x")
    own_rows = width // n_z
    part = halving_sum(part.reshape(n_z, own_rows, block_cols), "z")
    part = doubling_sum(part, "y") * (1.0 / (groups * n_z))
    grad_weight = doubling_gather(doubling_gather(part, "x"), "core")

    block = exchange(block[source_of])
    grad_rows = pl.pallas_call(
        functools.partial(back_kernel, keep),
        out_shape=jax.ShapeDtypeStruct(uvqk.shape, BF16),
        in_specs=[SMEM] + [VMEM] * 6,
        out_specs=VMEM,
        scratch_shapes=[pltpu.VMEM((moved, 5 * width), BF16)],
        compiler_params=PARAMS,
        cost_estimate=cost(8 * rows * width * width, 8 * width * width),
        name="back",
    )(recv_lengths, uvqk, grad_out, block, w_all, seg_col, seg_row)
    return grad_rows, grad_weight


def fine_mesh(mesh):
    n_dp, n_z = mesh.devices.shape
    n_core = 2
    n_x = min(4, n_dp // 4)
    shape = (n_x, n_dp // (n_x * n_core), n_core, n_z)
    return Mesh(mesh.devices.reshape(shape), ("x", "y", "core", "z"))


def solution(mesh):
    everyone = P(("x", "y", "core", "z"), None)
    placed = (everyone, everyone, P("z", None), everyone, P(), P())
    return jax.shard_map(
        local,
        mesh=fine_mesh(mesh),
        in_specs=placed,
        out_specs=(everyone, P("z", None)),
        check_vma=False,
    )
```

time: 470 us -> 184 us (0.39)
  blocking collectives: 252 us -> 0 us
  waiting for transfers between devices: 117 us -> 38.2 us
  starting transfers between devices: 37 us -> 101 us
  matrix products: 11.2 us -> 0 us
  other arithmetic: 19.7 us -> 8.68 us
  Pallas kernels: 0 us -> 8.32 us
    psum x1 -> x0, blocking collectives: 252 us -> none  [local(): lax.psum(group_sum, 'dp') / (lax.axis_size('dp') * lax.axis_size('fsdp'))]
    ppermute x0 -> x14, starting transfers between devices: none -> 83.8 us  [permuted(): return lax.ppermute(value, axis, [(i, target(i)) for i in range(size)])]
    reduce_scatter x1 -> x0, waiting for transfers between devices: 56 us -> none  [local(): lax.psum_scatter(lax.dot_general(columns, outputs_all, (((0,), (0,)), (()...]
    all_to_all x4 -> x2, waiting for transfers between devices: 47.8 us -> 0.01 us  [exchange(): return lax.all_to_all(value, DP, split_axis=0, concat_axis=0, tiled=True)]
    ppermute x0 -> x14, waiting for transfers between devices: none -> 37.5 us  [permuted(): return lax.ppermute(value, axis, [(i, target(i)) for i in range(size)])]
    all_to_all x4 -> x2, starting transfers between devices: 36.7 us -> 17.1 us  [exchange(): return lax.all_to_all(value, DP, split_axis=0, concat_axis=0, tiled=True)]
    all_gather x1, waiting for transfers between devices: 12.7 us -> 0.01 us  [local(): w_all = lax.all_gather(w_out, 'z', axis=0, tiled=True)]
    dot_general x14 -> x0, matrix products: 11.2 us -> none  [the longest x1 3.07 us: local(): lax.dot_general(columns, outputs_all, (((0,), (0,)), ((), ())), preferred...]
  transfers between devices with their start and end apart: 6 -> 17, of which waited for: 6 -> 12; matrix products, arithmetic and copies ran while one was open for 6% -> 6% of each run, Pallas kernels for 0% -> 0%
where the time goes in v1:
time: 184 us; the launch traced here: 183 us
  starting transfers between devices  101 us (55%)
  waiting for transfers between devices  38.2 us (21%)
  between operations  15 us (8%)
  local copies, waits for them, and re-layouts  11.9 us (6%)
  other arithmetic  8.68 us (5%)
  Pallas kernels  8.32 us (5%)
    ppermute x14, starting transfers between devices, permuted(): return lax.ppermute(value, axis, [(i, target(i)) for i in range(size)])  83.8 us
    ppermute x14, waiting for transfers between devices, permuted(): return lax.ppermute(value, axis, [(i, target(i)) for i in range(size)])  37.5 us
    all_to_all x2, starting transfers between devices, exchange(): return lax.all_to_all(value, DP, split_axis=0, concat_axis=0, tiled=True)  17.1 us
    unnamed x20, local copies, waits for them, and re-layouts  7.16 us
    pallas_call x1, Pallas kernels, local(): pl.pallas_call(functools.partial(back_kernel, keep), out_shape=jax.ShapeD...  5.02 us
  transfers between devices with their start and end apart: 17, of which 12 were waited for; matrix products, arithmetic and copies ran while one was open for 6% of the time, Pallas kernels for 0%

profile of v1, /device:TPU:1, one launch (start us, length us, event | category | flops | bytes accessed | tf_op | source)
XLA Modules:
  0.0 183.1 jit_solution(14412818176156489296)
XLA Ops:
  7.2 1.3 fusion.7
  9.1 0.8 constant_dynamic-slice_fusion
  10.1 1.4 copy-done
  11.5 1.0 copy-done.3
  12.5 1.2 pack.1
  14.4 2.1 %term.1 = bf16[8,1024,128]{2,1,0:T(8,128)(2,1)S(1)} custom-call(s32[1,3]{1,0:T(1,128)S(1)} %copy.29.lengths_ref, bf16[192,4096]{1,0:T(8,128)(2,1)S(1)} %copy-done.1, bf16[192,1024]{1,0:T(8,128)(2,1)S(1)} %copy-done.4, s32[64,1]{1,0:T(8,128)S(1)} %copy.25.seg_col_ref, s32[1,64]{1,0:T(1,128)S(1)} %copy-done.6), custom_call_target="tpu_custom_call" | custom-call | flops 805306368 | bytes 8388608 | tf_op jit(solution)/shard_map/term/pallas_call | solution.py:255
  16.6 1.3 copy-done.2
  17.9 1.1 dynamic-slice_bitcast_fusion
  18.9 16.0 %collective-permute-start = (bf16[4,1024,128]{2,1,0:T(8,128)(2,1)}, bf16[4,1024,128]{2,1,0:T(8,128)(2,1)}, u32[]{:S(2)}, u32[]{:S(2)}) collective-permute-start(bf16[4,1024,128]{2,1,0:T(8,128)(2,1)} %dynamic-slice_bitcast_fusion), channel_id=1, source_target_pairs={{0,16},{16,0},{1,17},{17,1},{2,18},{18,2},{3,19},{19,3},{4,20},{20... | collective-permute-start | bytes 3145736 | tf_op jit(solution)/shard_map/ppermute | solution.py:173
  34.9 4.2 %all-to-all-start = ((bf16[64,16,640]{2,1,0:T(8,128)(2,1)}), bf16[64,16,640]{2,1,0:T(8,128)(2,1)S(1)}, u32[]{:S(2)}, u32[]{:S(2)}) async-start(bf16[64,16,640]{2,1,0:T(8,128)(2,1)} %pack.1), calls=%async_computation | async-start | bytes 2621440 | tf_op jit(solution)/shard_map/all_to_all | solution.py:222
  39.2 0.7 all-gather.2.cloned.1.call-update
  39.9 1.8 fusion
  41.8 1.0 copy-done.7
  42.8 0.9 dynamic-slice_bitcast_fusion.3
  43.6 3.3 %collective-permute-start.1 = (bf16[1024,128]{1,0:T(8,128)(2,1)}, bf16[1024,128]{1,0:T(8,128)(2,1)}, u32[]{:S(2)}, u32[]{:S(2)}) collective-permute-start(bf16[1024,128]{1,0:T(8,128)(2,1)} %get-tuple-element.8), channel_id=1, source_target_pairs={{0,256},{256,512},{512,768},{768,0},{1,257},{257,513},{513,769},{7... | collective-permute-start | bytes 786440 | tf_op jit(solution)/shard_map/ppermute | solution.py:173
  46.9 4.5 %collective-permute-start.2 = (bf16[1024,128]{1,0:T(8,128)(2,1)}, bf16[1024,128]{1,0:T(8,128)(2,1)}, u32[]{:S(2)}, u32[]{:S(2)}) collective-permute-start(bf16[1024,128]{1,0:T(8,128)(2,1)} %get-tuple-element.10), channel_id=1, source_target_pairs={{0,512},{256,768},{512,0},{768,256},{1,513},{257,769},{513,1},{769... | collective-permute-start | bytes 786440 | tf_op jit(solution)/shard_map/ppermute | solution.py:173
  51.4 3.0 %collective-permute-start.3 = (bf16[1024,128]{1,0:T(8,128)(2,1)}, bf16[1024,128]{1,0:T(8,128)(2,1)}, u32[]{:S(2)}, u32[]{:S(2)}) collective-permute-start(bf16[1024,128]{1,0:T(8,128)(2,1)} %get-tuple-element.9), channel_id=1, source_target_pairs={{0,768},{256,0},{512,256},{768,512},{1,769},{257,1},{513,257},{769... | collective-permute-start | bytes 786440 | tf_op jit(solution)/shard_map/ppermute | solution.py:173
  54.6 4.9 %collective-permute-done.1 = bf16[1024,128]{1,0:T(8,128)(2,1)} collective-permute-done((bf16[1024,128]{1,0:T(8,128)(2,1)}, bf16[1024,128]{1,0:T(8,128)(2,1)}, u32[]{:S(2)}, u32[]{:S(2)}) %collective-permute-start.1) | collective-permute-done | bytes 262176 | tf_op jit(solution)/shard_map/ppermute | solution.py:173
  59.5 11.1 %collective-permute-done.2 = bf16[1024,128]{1,0:T(8,128)(2,1)} collective-permute-done((bf16[1024,128]{1,0:T(8,128)(2,1)}, bf16[1024,128]{1,0:T(8,128)(2,1)}, u32[]{:S(2)}, u32[]{:S(2)}) %collective-permute-start.2) | collective-permute-done | bytes 262176 | tf_op jit(solution)/shard_map/ppermute | solution.py:173
  70.6 1.0 collective-permute-done.3
  71.5 1.3 fusion.3
  72.9 1.9 %collective-permute-start.4 = (bf16[8,64,128]{2,1,0:T(8,128)(2,1)S(1)}, bf16[8,64,128]{2,1,0:T(8,128)(2,1)S(1)}, u32[]{:S(2)}, u32[]{:S(2)}) collective-permute-start(bf16[8,64,128]{2,1,0:T(8,128)(2,1)S(1)} %dynamic-slice_bitcast_fusion.4), channel_id=1, source_target_pairs={{0,1},{1,0},{2,3},{3,2},{4,5},{5,4},{6,7},{7,6},{8,9},{9,8},{10,11... | collective-permute-start | bytes 393224 | tf_op jit(solution)/shard_map/ppermute | solution.py:173
  74.8 5.4 %collective-permute-done.4 = bf16[8,64,128]{2,1,0:T(8,128)(2,1)S(1)} collective-permute-done((bf16[8,64,128]{2,1,0:T(8,128)(2,1)S(1)}, bf16[8,64,128]{2,1,0:T(8,128)(2,1)S(1)}, u32[]{:S(2)}, u32[]{:S(2)}) %collective-permute-start.4) | collective-permute-done | bytes 131104 | tf_op jit(solution)/shard_map/ppermute | solution.py:173
  80.3 1.9 %collective-permute-start.5 = (bf16[4,64,128]{2,1,0:T(8,128)(2,1)S(1)}, bf16[4,64,128]{2,1,0:T(8,128)(2,1)}, u32[]{:S(2)}, u32[]{:S(2)}) collective-permute-start(bf16[4,64,128]{2,1,0:T(8,128)(2,1)S(1)} %dynamic-slice_bitcast_fusion.5), channel_id=1, source_target_pairs={{0,2},{1,3},{2,0},{3,1},{4,6},{5,7},{6,4},{7,5},{8,10},{9,11},{10,... | collective-permute-start | bytes 196616 | tf_op jit(solution)/shard_map/ppermute | solution.py:173
  82.2 1.8 gather_fusion
  84.0 12.9 %all-to-all-start.1 = ((bf16[64,16,640]{2,1,0:T(8,128)(2,1)}), bf16[64,16,640]{2,1,0:T(8,128)(2,1)S(1)}, u32[]{:S(2)}, u32[]{:S(2)}) async-start(bf16[64,16,640]{2,1,0:T(8,128)(2,1)} %gather_fusion), calls=%async_computation.1 | async-start | bytes 2621440 | tf_op jit(solution)/shard_map/all_to_all | solution.py:222
  96.9 0.9 fusion.5
  97.8 9.6 %collective-permute-start.6 = (bf16[2,64,128]{2,1,0:T(8,128)(2,1)S(1)}, bf16[2,64,128]{2,1,0:T(8,128)(2,1)S(1)}, u32[]{:S(2)}, u32[]{:S(2)}) collective-permute-start(bf16[2,64,128]{2,1,0:T(8,128)(2,1)S(1)} %dynamic-slice_bitcast_fusion.6), channel_id=1, source_target_pairs={{0,4},{1,5},{2,6},{3,7},{4,0},{5,1},{6,2},{7,3},{8,12},{9,13},{10,... | collective-permute-start | bytes 98312 | tf_op jit(solution)/shard_map/ppermute | solution.py:173
  107.4 4.6 %collective-permute-done.6 = bf16[2,64,128]{2,1,0:T(8,128)(2,1)S(1)} collective-permute-done((bf16[2,64,128]{2,1,0:T(8,128)(2,1)S(1)}, bf16[2,64,128]{2,1,0:T(8,128)(2,1)S(1)}, u32[]{:S(2)}, u32[]{:S(2)}) %collective-permute-start.6) | collective-permute-done | bytes 32800 | tf_op jit(solution)/shard_map/ppermute | solution.py:173
  112.0 12.8 %collective-permute-start.7 = (bf16[1,64,128]{2,1,0:T(8,128)(2,1)S(1)}, bf16[1,64,128]{2,1,0:T(8,128)(2,1)S(1)}, u32[]{:S(2)}, u32[]{:S(2)}) collective-permute-start(bf16[1,64,128]{2,1,0:T(8,128)(2,1)S(1)} %constant_dynamic-slice_fusion.1), channel_id=1, source_target_pairs={{0,8},{1,9},{2,10},{3,11},{4,12},{5,13},{6,14},{7,15},{8,0},{9,1},... | collective-permute-start | bytes 49160 | tf_op jit(solution)/shard_map/ppermute | solution.py:173
  124.8 1.1 collective-permute-done.7
  125.9 2.8 %collective-permute-start.8 = (f32[64,128]{1,0:T(8,128)S(1)}, f32[64,128]{1,0:T(8,128)S(1)}, u32[]{:S(2)}, u32[]{:S(2)}) collective-permute-start(f32[64,128]{1,0:T(8,128)S(1)} %add_bitcast_fusion), channel_id=1, source_target_pairs={{0,32},{32,0},{64,96},{96,64},{128,160},{160,128},{192,224},{224,1... | collective-permute-start | bytes 98312 | tf_op jit(solution)/shard_map/ppermute | solution.py:173
  128.7 1.9 %collective-permute-done.8 = f32[64,128]{1,0:T(8,128)S(1)} collective-permute-done((f32[64,128]{1,0:T(8,128)S(1)}, f32[64,128]{1,0:T(8,128)S(1)}, u32[]{:S(2)}, u32[]{:S(2)}) %collective-permute-start.8) | collective-permute-done | bytes 32800 | tf_op jit(solution)/shard_map/ppermute | solution.py:173
  130.6 3.8 %collective-permute-start.9 = (f32[64,128]{1,0:T(8,128)S(1)}, f32[64,128]{1,0:T(8,128)S(1)}, u32[]{:S(2)}, u32[]{:S(2)}) collective-permute-start(f32[64,128]{1,0:T(8,128)S(1)} %add.162), channel_id=1, source_target_pairs={{0,64},{32,96},{64,0},{96,32},{128,192},{160,224},{192,128},{224,1... | collective-permute-start | bytes 98312 | tf_op jit(solution)/shard_map/ppermute | solution.py:173
  134.4 1.7 collective-permute-done.9
  136.2 7.3 %collective-permute-start.10 = (f32[64,128]{1,0:T(8,128)S(1)}, f32[64,128]{1,0:T(8,128)S(1)}, u32[]{:S(2)}, u32[]{:S(2)}) collective-permute-start(f32[64,128]{1,0:T(8,128)S(1)} %add.163), channel_id=1, source_target_pairs={{0,128},{32,160},{64,192},{96,224},{128,0},{160,32},{192,64},{224,... | collective-permute-start | bytes 98312 | tf_op jit(solution)/shard_map/ppermute | solution.py:173
  143.5 1.4 collective-permute-done.10
  144.9 3.4 %collective-permute-start.11 = (f32[64,128]{1,0:T(8,128)S(1)}, f32[64,128]{1,0:T(8,128)S(1)}, u32[]{:S(2)}, u32[]{:S(2)}) collective-permute-start(f32[64,128]{1,0:T(8,128)S(1)} %add_multiply_fusion), channel_id=1, source_target_pairs={{0,256},{256,0},{512,768},{768,512},{1,257},{257,1},{513,769},{769... | collective-permute-start | bytes 98312 | tf_op jit(solution)/shard_map/ppermute | solution.py:173
  148.3 1.3 collective-permute-done.11
  149.6 4.6 %collective-permute-start.12 = (f32[64,256]{1,0:T(8,128)S(1)}, f32[64,256]{1,0:T(8,128)}, u32[]{:S(2)}, u32[]{:S(2)}) collective-permute-start(f32[64,256]{1,0:T(8,128)S(1)} %pad_maximum_fusion.2), channel_id=1, source_target_pairs={{0,512},{256,768},{512,0},{768,256},{1,513},{257,769},{513,1},{769... | collective-permute-start | bytes 196616 | tf_op jit(solution)/shard_map/ppermute | solution.py:173
  154.3 2.0 %collective-permute-done.12 = f32[64,256]{1,0:T(8,128)} collective-permute-done((f32[64,256]{1,0:T(8,128)S(1)}, f32[64,256]{1,0:T(8,128)}, u32[]{:S(2)}, u32[]{:S(2)}) %collective-permute-start.12) | collective-permute-done | bytes 65568 | tf_op jit(solution)/shard_map/ppermute | solution.py:173
  156.3 0.9 broadcast_select_fusion.3
  157.8 8.9 %collective-permute-start.13 = (f32[64,512]{1,0:T(8,128)}, f32[64,512]{1,0:T(8,128)}, u32[]{:S(2)}, u32[]{:S(2)}) collective-permute-start(f32[64,512]{1,0:T(8,128)} %pad_maximum_fusion.1), channel_id=1, source_target_pairs={{0,16},{16,0},{1,17},{17,1},{2,18},{18,2},{3,19},{19,3},{4,20},{20... | collective-permute-start | bytes 393224 | tf_op jit(solution)/shard_map/ppermute | solution.py:173
  166.8 1.2 collective-permute-done.13
  168.0 0.9 broadcast_select_fusion.1
  168.9 0.7 pad_maximum_fusion
  169.6 1.6 copy-done.5
  171.2 5.0 %back.1 = bf16[192,4096]{1,0:T(8,128)(2,1)} custom-call(s32[1,3]{1,0:T(1,128)S(1)} %copy.28.lengths_ref, bf16[192,4096]{1,0:T(8,128)(2,1)S(1)} %copy-done.1, bf16[192,1024]{1,0:T(8,128)(2,1)S(1)} %copy-done.4, bf16[64,16,640]{2,1,0:T(8,128)(2,1)S(1)} %all-to-all-done.1.came_ref, bf16[1024,1024]{1,0:T(8,128)(2,1)S(1)} %copy-done.5, ...), custom_call_target="tpu_custom_call" | custom-call | flops 1610612736 | bytes 8388608 | tf_op jit(solution)/shard_map/back/pallas_call | solution.py:273
  (38 shorter events, 2.0 us)
Async XLA Ops:
  10.1 1.4 copy-start
  11.5 1.0 copy-start.3
  12.5 1.2 copy-start.6
  12.5 1.9 %copy-start.1 = (bf16[192,4096]{1,0:T(8,128)(2,1)S(1)}, bf16[192,4096]{1,0:T(8,128)(2,1)}, u32[]{:S(2)}) copy-start(bf16[192,4096]{1,0:T(8,128)(2,1)} %x_ref.3) | copy-start | bytes 4718596
  12.5 2.0 %copy-start.4 = (bf16[192,1024]{1,0:T(8,128)(2,1)S(1)}, bf16[192,1024]{1,0:T(8,128)(2,1)}, u32[]{:S(2)}) copy-start(bf16[192,1024]{1,0:T(8,128)(2,1)} %g_ref.3) | copy-start | bytes 1179652
  16.6 1.3 copy-start.2
  18.9 21.0 %collective-permute-start = (bf16[4,1024,128]{2,1,0:T(8,128)(2,1)}, bf16[4,1024,128]{2,1,0:T(8,128)(2,1)}, u32[]{:S(2)}, u32[]{:S(2)}) collective-permute-start(bf16[4,1024,128]{2,1,0:T(8,128)(2,1)} %dynamic-slice_bitcast_fusion), channel_id=1, source_target_pairs={{0,16},{16,0},{1,17},{17,1},{2,18},{18,2},{3,19},{19,3},{4,20},{20... | collective-permute-start | bytes 3145736 | tf_op jit(solution)/shard_map/ppermute | solution.py:173
  34.9 47.3 %all-to-all-start = ((bf16[64,16,640]{2,1,0:T(8,128)(2,1)}), bf16[64,16,640]{2,1,0:T(8,128)(2,1)S(1)}, u32[]{:S(2)}, u32[]{:S(2)}) async-start(bf16[64,16,640]{2,1,0:T(8,128)(2,1)} %pack.1), calls=%async_computation | async-start | bytes 2621440 | tf_op jit(solution)/shard_map/all_to_all | solution.py:222
  39.2 130.4 %all-gather.2.cloned.1.call-start = ((), (), s32[]{:S(2)}) async-start(), calls=%async_computation.2 | async-start | bytes 2228224 | tf_op jit(solution)/shard_map/all_gather | solution.py:239
  41.8 1.0 copy-start.7
  42.8 11.7 %copy-start.8 = (s32[64]{0:T(128)S(1)}, s32[64]{0:T(128)}, u32[]{:S(2)}) copy-start(s32[64]{0:T(128)} %param.11) | copy-start | bytes 772
  43.6 15.8 %collective-permute-start.1 = (bf16[1024,128]{1,0:T(8,128)(2,1)}, bf16[1024,128]{1,0:T(8,128)(2,1)}, u32[]{:S(2)}, u32[]{:S(2)}) collective-permute-start(bf16[1024,128]{1,0:T(8,128)(2,1)} %get-tuple-element.8), channel_id=1, source_target_pairs={{0,256},{256,512},{512,768},{768,0},{1,257},{257,513},{513,769},{7... | collective-permute-start | bytes 786440 | tf_op jit(solution)/shard_map/ppermute | solution.py:173
  46.9 23.6 %collective-permute-start.2 = (bf16[1024,128]{1,0:T(8,128)(2,1)}, bf16[1024,128]{1,0:T(8,128)(2,1)}, u32[]{:S(2)}, u32[]{:S(2)}) collective-permute-start(bf16[1024,128]{1,0:T(8,128)(2,1)} %get-tuple-element.10), channel_id=1, source_target_pairs={{0,512},{256,768},{512,0},{768,256},{1,513},{257,769},{513,1},{769... | collective-permute-start | bytes 786440 | tf_op jit(solution)/shard_map/ppermute | solution.py:173
  51.4 20.1 %collective-permute-start.3 = (bf16[1024,128]{1,0:T(8,128)(2,1)}, bf16[1024,128]{1,0:T(8,128)(2,1)}, u32[]{:S(2)}, u32[]{:S(2)}) collective-permute-start(bf16[1024,128]{1,0:T(8,128)(2,1)} %get-tuple-element.9), channel_id=1, source_target_pairs={{0,768},{256,0},{512,256},{768,512},{1,769},{257,1},{513,257},{769... | collective-permute-start | bytes 786440 | tf_op jit(solution)/shard_map/ppermute | solution.py:173
  72.9 7.3 %collective-permute-start.4 = (bf16[8,64,128]{2,1,0:T(8,128)(2,1)S(1)}, bf16[8,64,128]{2,1,0:T(8,128)(2,1)S(1)}, u32[]{:S(2)}, u32[]{:S(2)}) collective-permute-start(bf16[8,64,128]{2,1,0:T(8,128)(2,1)S(1)} %dynamic-slice_bitcast_fusion.4), channel_id=1, source_target_pairs={{0,1},{1,0},{2,3},{3,2},{4,5},{5,4},{6,7},{7,6},{8,9},{9,8},{10,11... | collective-permute-start | bytes 393224 | tf_op jit(solution)/shard_map/ppermute | solution.py:173
  80.3 16.6 %collective-permute-start.5 = (bf16[4,64,128]{2,1,0:T(8,128)(2,1)S(1)}, bf16[4,64,128]{2,1,0:T(8,128)(2,1)}, u32[]{:S(2)}, u32[]{:S(2)}) collective-permute-start(bf16[4,64,128]{2,1,0:T(8,128)(2,1)S(1)} %dynamic-slice_bitcast_fusion.5), channel_id=1, source_target_pairs={{0,2},{1,3},{2,0},{3,1},{4,6},{5,7},{6,4},{7,5},{8,10},{9,11},{10,... | collective-permute-start | bytes 196616 | tf_op jit(solution)/shard_map/ppermute | solution.py:173
  84.0 85.6 %all-to-all-start.1 = ((bf16[64,16,640]{2,1,0:T(8,128)(2,1)}), bf16[64,16,640]{2,1,0:T(8,128)(2,1)S(1)}, u32[]{:S(2)}, u32[]{:S(2)}) async-start(bf16[64,16,640]{2,1,0:T(8,128)(2,1)} %gather_fusion), calls=%async_computation.1 | async-start | bytes 2621440 | tf_op jit(solution)/shard_map/all_to_all | solution.py:222
  97.8 14.1 %collective-permute-start.6 = (bf16[2,64,128]{2,1,0:T(8,128)(2,1)S(1)}, bf16[2,64,128]{2,1,0:T(8,128)(2,1)S(1)}, u32[]{:S(2)}, u32[]{:S(2)}) collective-permute-start(bf16[2,64,128]{2,1,0:T(8,128)(2,1)S(1)} %dynamic-slice_bitcast_fusion.6), channel_id=1, source_target_pairs={{0,4},{1,5},{2,6},{3,7},{4,0},{5,1},{6,2},{7,3},{8,12},{9,13},{10,... | collective-permute-start | bytes 98312 | tf_op jit(solution)/shard_map/ppermute | solution.py:173
  112.0 13.9 %collective-permute-start.7 = (bf16[1,64,128]{2,1,0:T(8,128)(2,1)S(1)}, bf16[1,64,128]{2,1,0:T(8,128)(2,1)S(1)}, u32[]{:S(2)}, u32[]{:S(2)}) collective-permute-start(bf16[1,64,128]{2,1,0:T(8,128)(2,1)S(1)} %constant_dynamic-slice_fusion.1), channel_id=1, source_target_pairs={{0,8},{1,9},{2,10},{3,11},{4,12},{5,13},{6,14},{7,15},{8,0},{9,1},... | collective-permute-start | bytes 49160 | tf_op jit(solution)/shard_map/ppermute | solution.py:173
  125.9 4.7 %collective-permute-start.8 = (f32[64,128]{1,0:T(8,128)S(1)}, f32[64,128]{1,0:T(8,128)S(1)}, u32[]{:S(2)}, u32[]{:S(2)}) collective-permute-start(f32[64,128]{1,0:T(8,128)S(1)} %add_bitcast_fusion), channel_id=1, source_target_pairs={{0,32},{32,0},{64,96},{96,64},{128,160},{160,128},{192,224},{224,1... | collective-permute-start | bytes 98312 | tf_op jit(solution)/shard_map/ppermute | solution.py:173
  130.6 5.5 %collective-permute-start.9 = (f32[64,128]{1,0:T(8,128)S(1)}, f32[64,128]{1,0:T(8,128)S(1)}, u32[]{:S(2)}, u32[]{:S(2)}) collective-permute-start(f32[64,128]{1,0:T(8,128)S(1)} %add.162), channel_id=1, source_target_pairs={{0,64},{32,96},{64,0},{96,32},{128,192},{160,224},{192,128},{224,1... | collective-permute-start | bytes 98312 | tf_op jit(solution)/shard_map/ppermute | solution.py:173
  136.2 8.7 %collective-permute-start.10 = (f32[64,128]{1,0:T(8,128)S(1)}, f32[64,128]{1,0:T(8,128)S(1)}, u32[]{:S(2)}, u32[]{:S(2)}) collective-permute-start(f32[64,128]{1,0:T(8,128)S(1)} %add.163), channel_id=1, source_target_pairs={{0,128},{32,160},{64,192},{96,224},{128,0},{160,32},{192,64},{224,... | collective-permute-start | bytes 98312 | tf_op jit(solution)/shard_map/ppermute | solution.py:173
  144.9 4.7 %collective-permute-start.11 = (f32[64,128]{1,0:T(8,128)S(1)}, f32[64,128]{1,0:T(8,128)S(1)}, u32[]{:S(2)}, u32[]{:S(2)}) collective-permute-start(f32[64,128]{1,0:T(8,128)S(1)} %add_multiply_fusion), channel_id=1, source_target_pairs={{0,256},{256,0},{512,768},{768,512},{1,257},{257,1},{513,769},{769... | collective-permute-start | bytes 98312 | tf_op jit(solution)/shard_map/ppermute | solution.py:173
  149.6 6.6 %collective-permute-start.12 = (f32[64,256]{1,0:T(8,128)S(1)}, f32[64,256]{1,0:T(8,128)}, u32[]{:S(2)}, u32[]{:S(2)}) collective-permute-start(f32[64,256]{1,0:T(8,128)S(1)} %pad_maximum_fusion.2), channel_id=1, source_target_pairs={{0,512},{256,768},{512,0},{768,256},{1,513},{257,769},{513,1},{769... | collective-permute-start | bytes 196616 | tf_op jit(solution)/shard_map/ppermute | solution.py:173
  157.8 10.2 %collective-permute-start.13 = (f32[64,512]{1,0:T(8,128)}, f32[64,512]{1,0:T(8,128)}, u32[]{:S(2)}, u32[]{:S(2)}) collective-permute-start(f32[64,512]{1,0:T(8,128)} %pad_maximum_fusion.1), channel_id=1, source_target_pairs={{0,16},{16,0},{1,17},{17,1},{2,18},{18,2},{3,19},{19,3},{4,20},{20... | collective-permute-start | bytes 393224 | tf_op jit(solution)/shard_map/ppermute | solution.py:173
  169.6 1.6 copy-start.5
Sparse Core Ops, SparseCore 0:
  42.7 70.4 all-gather.1

commit v2 on v1

--- a/solution.py
+++ b/solution.py
@@ -190,36 +190,29 @@
     return added(pick(value, me), *came).astype(BF16)
 
 
-def halving_sum(value, axis):
+def ring_of_rings_sum(value, axis, inner):
     size, me = lax.axis_size(axis), lax.axis_index(axis)
-    steps = size.bit_length() - 1
-    for step in range(steps):
-        pairs = value.reshape((value.shape[0] // 2, 2) + value.shape[1:])
-        mine = (me >> step) & 1
-        came = permuted(pick(pairs, 1 - mine, 1), axis, lambda i, step=step: i ^ (1 << step))
-        value = added(pick(pairs, mine, 1), came)
-        if step < steps - 1:
-            value = value.astype(BF16)
-    return value[0]
-
-
-def doubling_sum(value, axis):
-    for step in range(lax.axis_size(axis).bit_length() - 1):
-        value = value + permuted(value, axis, lambda i, step=step: i ^ (1 << step))
-    return value
-
-
-def doubling_gather(value, axis):
-    me = lax.axis_index(axis)
-    for step in range(lax.axis_size(axis).bit_length() - 1):
-        came = permuted(value, axis, lambda i, step=step: i ^ (1 << step))
-        low = ((me >> step) & 1) == 0
-        value = jnp.concatenate([jnp.where(low, value, came), jnp.where(low, came, value)], axis=1)
-    return value
-
-
-def exchange(value):
-    return lax.all_to_all(value, DP, split_axis=0, concat_axis=0, tiled=True)
+    outer = size // inner
+    value = value.reshape((outer, inner) + value.shape[1:])
+    low, high = me & (inner - 1), me >> (inner.bit_length() - 1)
+    came = [
+        permuted(
+            pick(value, (low + step) & (inner - 1), 1),
+            axis,
+            lambda i, step=step: i // inner * inner + (i + step) % inner,
+        )
+        for step in range(1, inner)
+    ]
+    value = added(pick(value, low, 1), *came).astype(BF16)
+    came = [
+        permuted(pick(value, (high + step) & (outer - 1)), axis, lambda i, step=step: (i + step * inner) % size)
+        for step in range(1, outer)
+    ]
+    return added(pick(value, high), *came)
+
+
+def exchange(value, axes=DP):
+    return lax.all_to_all(value, axes, split_axis=0, concat_axis=0, tiled=True)
 
 
 def local(uvqk, grad_out, w_out, kept_segments, moved_lengths, dest_device):
@@ -244,7 +237,7 @@
         in_specs=[VMEM, VMEM],
         out_specs=VMEM,
         compiler_params=PARAMS,
-        cost_estimate=cost(0, 10 * moved * 5 * width),
+        cost_estimate=cost(0, 8 * width),
         name="pack",
     )(uvqk, grad_out)
     uvqk, grad_out, block = lax.optimization_barrier((uvqk, grad_out, block))
@@ -259,17 +252,22 @@
         out_specs=VMEM,
         scratch_shapes=[pltpu.VMEM((rows, width), BF16)],
         compiler_params=PARAMS,
-        cost_estimate=cost(4 * rows * width * width, 8 * width * width),
+        cost_estimate=cost(0, 8 * width),
         name="term",
     )(own_lengths, uvqk, grad_out, seg_col, seg_row)
     part = scatter_sum(term.reshape(n_core, n_x, width, block_cols), "core")
     part = scatter_sum(part, "x")
     own_rows = width // n_z
-    part = halving_sum(part.reshape(n_z, own_rows, block_cols), "z")
-    part = doubling_sum(part, "y") * (1.0 / (groups * n_z))
-    grad_weight = doubling_gather(doubling_gather(part, "x"), "core")
-
+    part, block = lax.optimization_barrier((part, block))
     block = exchange(block[source_of])
+    part = ring_of_rings_sum(part.reshape(n_z, own_rows, block_cols), "z", min(4, n_z))
+    part = lax.optimization_barrier((part, block))[0]
+    part = exchange(part.reshape(n_y, own_rows // n_y, block_cols), "y")
+    part = (jnp.sum(part, axis=0) * (1.0 / (groups * n_z))).astype(BF16)
+    spread = exchange(jnp.broadcast_to(part[None], (groups,) + part.shape))
+    spread = spread.astype(F32).reshape(n_x, n_y, n_core, own_rows // n_y, block_cols)
+    grad_weight = spread.transpose(1, 3, 2, 0, 4).reshape(own_rows, width)
+
     grad_rows = pl.pallas_call(
         functools.partial(back_kernel, keep),
         out_shape=jax.ShapeDtypeStruct(uvqk.shape, BF16),

time: 184 us -> 163 us (0.89)
  starting transfers between devices: 101 us -> 77.7 us
  blocking collectives: 0 us -> 13.5 us
  waiting for transfers between devices: 38.2 us -> 30.5 us
  other arithmetic: 8.68 us -> 4.37 us
    ppermute x14 -> x10, starting transfers between devices: 83.8 us -> 42 us  [permuted(): return lax.ppermute(value, axis, [(i, target(i)) for i in range(size)])]
    all_to_all x2 -> x3, starting transfers between devices: 17.1 us -> 35.7 us  [exchange(): return lax.all_to_all(value, axes, split_axis=0, concat_axis=0, tiled=True)]
    all_to_all x0 -> x1, blocking collectives: none -> 13.5 us  [exchange(): return lax.all_to_all(value, axes, split_axis=0, concat_axis=0, tiled=True)]
    ppermute x14 -> x10, waiting for transfers between devices: 37.5 us -> 26.8 us  [permuted(): return lax.ppermute(value, axis, [(i, target(i)) for i in range(size)])]
    all_to_all x2 -> x3, waiting for transfers between devices: 0.01 us -> 3.65 us  [exchange(): return lax.all_to_all(value, axes, split_axis=0, concat_axis=0, tiled=True)]
    unnamed x20 -> x18, local copies, waits for them, and re-layouts: 7.16 us -> 5.48 us
  transfers between devices with their start and end apart: 17 -> 14, of which waited for: 12 -> 7; matrix products, arithmetic and copies ran while one was open for 6% -> 7% of each run, Pallas kernels for 0% -> 4%
where the time goes in v2:
time: 163 us; the launch traced here: 162 us
  starting transfers between devices  77.7 us (48%)
  waiting for transfers between devices  30.5 us (19%)
  between operations  15 us (9%)
  blocking collectives  13.5 us (8%)
  local copies, waits for them, and re-layouts  12.6 us (8%)
  Pallas kernels  8.33 us (5%)
  other arithmetic  4.37 us (3%)
    ppermute x10, starting transfers between devices, permuted(): return lax.ppermute(value, axis, [(i, target(i)) for i in range(size)])  42 us
    all_to_all x3, starting transfers between devices, exchange(): return lax.all_to_all(value, axes, split_axis=0, concat_axis=0, tiled=True)  35.7 us
    ppermute x10, waiting for transfers between devices, permuted(): return lax.ppermute(value, axis, [(i, target(i)) for i in range(size)])  26.8 us
    all_to_all x1, blocking collectives, exchange(): return lax.all_to_all(value, axes, split_axis=0, concat_axis=0, tiled=True)  13.5 us
    unnamed x18, local copies, waits for them, and re-layouts  5.48 us
    pallas_call x1, Pallas kernels, local(): pl.pallas_call(functools.partial(back_kernel, keep), out_shape=jax.ShapeD...  5.03 us
    all_to_all x3, waiting for transfers between devices, exchange(): return lax.all_to_all(value, axes, split_axis=0, concat_axis=0, tiled=True)  3.65 us
  transfers between devices with their start and end apart: 14, of which 7 were waited for; matrix products, arithmetic and copies ran while one was open for 7% of the time, Pallas kernels for 4%

profile of v2, /device:TPU:1, one launch (start us, length us, event | category | flops | bytes accessed | tf_op | source)
XLA Modules:
  0.0 162.0 jit_solution(4032103286074425946)
XLA Ops:
  7.2 0.0 copy-start
  7.2 1.4 copy-done
  8.6 1.0 copy-done.3
  9.6 1.2 pack.1
  10.7 19.2 %all-to-all-start = ((bf16[64,16,640]{2,1,0:T(8,128)(2,1)}), bf16[64,16,640]{2,1,0:T(8,128)(2,1)}, u32[]{:S(2)}, u32[]{:S(2)}) async-start(bf16[64,16,640]{2,1,0:T(8,128)(2,1)} %pack.1), calls=%async_computation | async-start | bytes 2621440 | tf_op jit(solution)/shard_map/all_to_all | solution.py:215
  29.9 0.0 all-gather.2.cloned.1.call-start
  30.0 0.6 fusion.9
  31.3 0.8 constant_dynamic-slice_fusion
  32.1 0.1 copy.27.lengths_ref
  32.2 0.1 copy.23.seg_col_ref
  32.3 2.1 %term.1 = bf16[8,1024,128]{2,1,0:T(8,128)(2,1)S(1)} custom-call(s32[1,3]{1,0:T(1,128)S(1)} %copy.27.lengths_ref, bf16[192,4096]{1,0:T(8,128)(2,1)S(1)} %copy-done.1, bf16[192,1024]{1,0:T(8,128)(2,1)S(1)} %copy-done.4, s32[64,1]{1,0:T(8,128)S(1)} %copy.23.seg_col_ref, s32[1,64]{1,0:T(1,128)S(1)} %copy-done.6), custom_call_target="tpu_custom_call" | custom-call | bytes 8192 | tf_op jit(solution)/shard_map/term/pallas_call | solution.py:248
  34.4 1.3 copy-done.2
  35.7 0.1 dynamic-slice_bitcast_fusion
  35.8 2.6 %collective-permute-start = (bf16[4,1024,128]{2,1,0:T(8,128)(2,1)S(1)}, bf16[4,1024,128]{2,1,0:T(8,128)(2,1)}, u32[]{:S(2)}, u32[]{:S(2)}) collective-permute-start(bf16[4,1024,128]{2,1,0:T(8,128)(2,1)S(1)} %dynamic-slice_bitcast_fusion), channel_id=1, source_target_pairs={{0,16},{16,0},{1,17},{17,1},{2,18},{18,2},{3,19},{19,3},{4,20},{20... | collective-permute-start | bytes 3145736 | tf_op jit(solution)/shard_map/ppermute | solution.py:173
  38.4 0.0 all-gather.2.cloned.1.call-update
  38.4 0.1 select_reduce_fusion
  38.5 2.3 %collective-permute-done = bf16[4,1024,128]{2,1,0:T(8,128)(2,1)} collective-permute-done((bf16[4,1024,128]{2,1,0:T(8,128)(2,1)S(1)}, bf16[4,1024,128]{2,1,0:T(8,128)(2,1)}, u32[]{:S(2)}, u32[]{:S(2)}) %collective-permute-start) | collective-permute-done | bytes 1048608 | tf_op jit(solution)/shard_map/ppermute | solution.py:173
  40.8 1.8 %fusion = bf16[4,1024,128]{2,1,0:T(8,128)(2,1)S(1)} fusion(bf16[4,1024,128]{2,1,0:T(8,128)(2,1)} %collective-permute-done, bf16[2,4,1024,128]{3,2,1,0:T(8,128)(2,1)} %bitcast.46, s32[]{:T(128)S(6)} %select_n.73), kind=kLoop, calls=%fused_computation.2 | loop fusion | flops 2097152 | bytes 3145732 | tf_op jit(solution)/shard_map/convert_element_type | solution.py:190
  42.6 0.1 dynamic-slice_bitcast_fusion.3
  42.7 4.5 %collective-permute-start.3 = (bf16[1024,128]{1,0:T(8,128)(2,1)S(1)}, bf16[1024,128]{1,0:T(8,128)(2,1)S(1)}, u32[]{:S(2)}, u32[]{:S(2)}) collective-permute-start(bf16[1024,128]{1,0:T(8,128)(2,1)S(1)} %get-tuple-element.15), channel_id=1, source_target_pairs={{0,768},{256,0},{512,256},{768,512},{1,769},{257,1},{513,257},{769... | collective-permute-start | bytes 786440 | tf_op jit(solution)/shard_map/ppermute | solution.py:173
  47.2 2.3 %collective-permute-start.2 = (bf16[1024,128]{1,0:T(8,128)(2,1)S(1)}, bf16[1024,128]{1,0:T(8,128)(2,1)S(1)}, u32[]{:S(2)}, u32[]{:S(2)}) collective-permute-start(bf16[1024,128]{1,0:T(8,128)(2,1)S(1)} %get-tuple-element.16), channel_id=1, source_target_pairs={{0,512},{256,768},{512,0},{768,256},{1,513},{257,769},{513,1},{769... | collective-permute-start | bytes 786440 | tf_op jit(solution)/shard_map/ppermute | solution.py:173
  49.5 2.6 %collective-permute-start.1 = (bf16[1024,128]{1,0:T(8,128)(2,1)S(1)}, bf16[1024,128]{1,0:T(8,128)(2,1)S(1)}, u32[]{:S(2)}, u32[]{:S(2)}) collective-permute-start(bf16[1024,128]{1,0:T(8,128)(2,1)S(1)} %get-tuple-element.14), channel_id=1, source_target_pairs={{0,256},{256,512},{512,768},{768,0},{1,257},{257,513},{513,769},{7... | collective-permute-start | bytes 786440 | tf_op jit(solution)/shard_map/ppermute | solution.py:173
  52.1 12.3 %collective-permute-done.3 = bf16[1024,128]{1,0:T(8,128)(2,1)S(1)} collective-permute-done((bf16[1024,128]{1,0:T(8,128)(2,1)S(1)}, bf16[1024,128]{1,0:T(8,128)(2,1)S(1)}, u32[]{:S(2)}, u32[]{:S(2)}) %collective-permute-start.3) | collective-permute-done | bytes 262176 | tf_op jit(solution)/shard_map/ppermute | solution.py:173
  64.4 0.0 collective-permute-done.2
  64.4 4.4 %collective-permute-done.1 = bf16[1024,128]{1,0:T(8,128)(2,1)S(1)} collective-permute-done((bf16[1024,128]{1,0:T(8,128)(2,1)S(1)}, bf16[1024,128]{1,0:T(8,128)(2,1)S(1)}, u32[]{:S(2)}, u32[]{:S(2)}) %collective-permute-start.1) | collective-permute-done | bytes 262176 | tf_op jit(solution)/shard_map/ppermute | solution.py:173
  68.9 0.8 fusion.3
  69.7 3.1 %gather_fusion = bf16[64,16,640]{2,1,0:T(8,128)(2,1)} fusion(bf16[64,16,640]{2,1,0:T(8,128)(2,1)} %all-to-all-done, s32[1024]{0:T(1024)S(1)} %pad_clamp_fusion), kind=kCustom, calls=%fused_computation | custom fusion | bytes 2621696 | tf_op jit(solution)/shard_map/gather | solution.py:262
  72.8 6.7 %all-to-all-start.1 = ((bf16[64,16,640]{2,1,0:T(8,128)(2,1)}), bf16[64,16,640]{2,1,0:T(8,128)(2,1)S(1)}, u32[]{:S(2)}, u32[]{:S(2)}) async-start(bf16[64,16,640]{2,1,0:T(8,128)(2,1)} %gather_fusion), calls=%async_computation.1 | async-start | bytes 2621440 | tf_op jit(solution)/shard_map/all_to_all | solution.py:215
  79.5 1.6 dynamic-slice_bitcast_fusion.6
  81.1 1.9 %collective-permute-start.6 = (bf16[4,64,128]{2,1,0:T(8,128)(2,1)}, bf16[4,64,128]{2,1,0:T(8,128)(2,1)S(1)}, u32[]{:S(2)}, u32[]{:S(2)}) collective-permute-start(bf16[4,64,128]{2,1,0:T(8,128)(2,1)} %get-tuple-element.18), channel_id=1, source_target_pairs={{0,3},{1,0},{2,1},{3,2},{4,7},{5,4},{6,5},{7,6},{8,11},{9,8},{10,9... | collective-permute-start | bytes 196616 | tf_op jit(solution)/shard_map/ppermute | solution.py:173
  83.0 1.9 %collective-permute-start.5 = (bf16[4,64,128]{2,1,0:T(8,128)(2,1)}, bf16[4,64,128]{2,1,0:T(8,128)(2,1)S(1)}, u32[]{:S(2)}, u32[]{:S(2)}) collective-permute-start(bf16[4,64,128]{2,1,0:T(8,128)(2,1)} %get-tuple-element.19), channel_id=1, source_target_pairs={{0,2},{1,3},{2,0},{3,1},{4,6},{5,7},{6,4},{7,5},{8,10},{9,11},{10,... | collective-permute-start | bytes 196616 | tf_op jit(solution)/shard_map/ppermute | solution.py:173
  84.9 3.4 %collective-permute-start.4 = (bf16[4,64,128]{2,1,0:T(8,128)(2,1)S(1)}, bf16[4,64,128]{2,1,0:T(8,128)(2,1)}, u32[]{:S(2)}, u32[]{:S(2)}) collective-permute-start(bf16[4,64,128]{2,1,0:T(8,128)(2,1)S(1)} %get-tuple-element.17), channel_id=1, source_target_pairs={{0,1},{1,2},{2,3},{3,0},{4,5},{5,6},{6,7},{7,4},{8,9},{9,10},{10,1... | collective-permute-start | bytes 196616 | tf_op jit(solution)/shard_map/ppermute | solution.py:173
  88.3 4.8 %collective-permute-done.5 = bf16[4,64,128]{2,1,0:T(8,128)(2,1)S(1)} collective-permute-done((bf16[4,64,128]{2,1,0:T(8,128)(2,1)}, bf16[4,64,128]{2,1,0:T(8,128)(2,1)S(1)}, u32[]{:S(2)}, u32[]{:S(2)}) %collective-permute-start.5) | collective-permute-done | bytes 65568 | tf_op jit(solution)/shard_map/ppermute | solution.py:173
  93.1 0.9 collective-permute-done.4
  94.0 0.9 fusion.6
  95.0 11.7 %collective-permute-start.9 = (bf16[64,128]{1,0:T(8,128)(2,1)S(1)}, bf16[64,128]{1,0:T(8,128)(2,1)S(1)}, u32[]{:S(2)}, u32[]{:S(2)}) collective-permute-start(bf16[64,128]{1,0:T(8,128)(2,1)S(1)} %get-tuple-element.21), channel_id=1, source_target_pairs={{0,12},{1,13},{2,14},{3,15},{4,0},{5,1},{6,2},{7,3},{8,4},{9,5},{1... | collective-permute-start | bytes 49160 | tf_op jit(solution)/shard_map/ppermute | solution.py:173
  106.7 3.9 %collective-permute-start.8 = (bf16[64,128]{1,0:T(8,128)(2,1)S(1)}, bf16[64,128]{1,0:T(8,128)(2,1)S(1)}, u32[]{:S(2)}, u32[]{:S(2)}) collective-permute-start(bf16[64,128]{1,0:T(8,128)(2,1)S(1)} %get-tuple-element.22), channel_id=1, source_target_pairs={{0,8},{1,9},{2,10},{3,11},{4,12},{5,13},{6,14},{7,15},{8,0},{9,1},... | collective-permute-start | bytes 49160 | tf_op jit(solution)/shard_map/ppermute | solution.py:173
  110.5 7.3 %collective-permute-start.7 = (bf16[64,128]{1,0:T(8,128)(2,1)S(1)}, bf16[64,128]{1,0:T(8,128)(2,1)S(1)}, u32[]{:S(2)}, u32[]{:S(2)}) collective-permute-start(bf16[64,128]{1,0:T(8,128)(2,1)S(1)} %get-tuple-element.20), channel_id=1, source_target_pairs={{0,4},{1,5},{2,6},{3,7},{4,8},{5,9},{6,10},{7,11},{8,12},{9,13},{1... | collective-permute-start | bytes 49160 | tf_op jit(solution)/shard_map/ppermute | solution.py:173
  117.8 2.1 %collective-permute-done.8 = bf16[64,128]{1,0:T(8,128)(2,1)S(1)} collective-permute-done((bf16[64,128]{1,0:T(8,128)(2,1)S(1)}, bf16[64,128]{1,0:T(8,128)(2,1)S(1)}, u32[]{:S(2)}, u32[]{:S(2)}) %collective-permute-start.8) | collective-permute-done | bytes 16416 | tf_op jit(solution)/shard_map/ppermute | solution.py:173
  119.9 0.0 all-to-all-done.1.came_ref
  119.9 13.5 %all_to_all.20 = f32[8,8,128]{2,1,0:T(8,128)S(1)} all-to-all(f32[8,8,128]{2,1,0:T(8,128)S(1)} %bitcast.52), channel_id=1, replica_groups=mesh['x'=4,'y'=8,'core'=2,'z'=16] {'y'}, dimensions={0} | all-to-all | bytes 65536 | tf_op jit(solution)/shard_map/all_to_all | solution.py:215
  133.4 0.7 broadcast_in_dim.32
  134.1 9.9 %all-to-all-start.3 = ((bf16[64,8,128]{2,1,0:T(8,128)(2,1)}), bf16[64,8,128]{2,1,0:T(8,128)(2,1)S(1)}, u32[]{:S(2)}, u32[]{:S(2)}) async-start(bf16[64,8,128]{2,1,0:T(8,128)(2,1)} %broadcast_in_dim.32), calls=%async_computation.3 | async-start | bytes 262144 | tf_op jit(solution)/shard_map/all_to_all | solution.py:215
  144.0 0.1 copy.26.lengths_ref
  144.1 1.6 copy-done.5
  145.7 5.0 %back.1 = bf16[192,4096]{1,0:T(8,128)(2,1)} custom-call(s32[1,3]{1,0:T(1,128)S(1)} %copy.26.lengths_ref, bf16[192,4096]{1,0:T(8,128)(2,1)S(1)} %copy-done.1, bf16[192,1024]{1,0:T(8,128)(2,1)S(1)} %copy-done.4, bf16[64,16,640]{2,1,0:T(8,128)(2,1)S(1)} %all-to-all-done.1.came_ref, bf16[1024,1024]{1,0:T(8,128)(2,1)S(1)} %copy-done.5, ...), custom_call_target="tpu_custom_call" | custom-call | flops 1610612736 | bytes 8388608 | tf_op jit(solution)/shard_map/back/pallas_call | solution.py:271
  150.7 3.6 %all-to-all-done.3 = bf16[64,8,128]{2,1,0:T(8,128)(2,1)S(1)} async-done(((bf16[64,8,128]{2,1,0:T(8,128)(2,1)}), bf16[64,8,128]{2,1,0:T(8,128)(2,1)S(1)}, u32[]{:S(2)}, u32[]{:S(2)}) %all-to-all-start.3) | async-done | bytes 131104 | tf_op jit(solution)/shard_map/all_to_all | solution.py:215
  154.4 0.7 copy.25
  (23 shorter events, 0.1 us)
Async XLA Ops:
  7.2 1.4 copy-start
  8.6 1.0 copy-start.3
  10.7 19.2 %copy-start.7 = (s32[64]{0:T(128)S(1)}, s32[64]{0:T(128)}, u32[]{:S(2)}) copy-start(s32[64]{0:T(128)} %param.11) | copy-start | bytes 772
  10.7 21.4 %copy-start.6 = (s32[1,64]{1,0:T(1,128)S(1)}, s32[1,64]{1,0:T(1,128)}, u32[]{:S(2)}) copy-start(s32[1,64]{1,0:T(1,128)} %seg_row_ref.3) | copy-start | bytes 772
  10.7 21.5 %copy-start.1 = (bf16[192,4096]{1,0:T(8,128)(2,1)S(1)}, bf16[192,4096]{1,0:T(8,128)(2,1)}, u32[]{:S(2)}) copy-start(bf16[192,4096]{1,0:T(8,128)(2,1)} %x_ref.3) | copy-start | bytes 4718596
  10.7 21.5 %copy-start.4 = (bf16[192,1024]{1,0:T(8,128)(2,1)S(1)}, bf16[192,1024]{1,0:T(8,128)(2,1)}, u32[]{:S(2)}) copy-start(bf16[192,1024]{1,0:T(8,128)(2,1)} %g_ref.3) | copy-start | bytes 1179652
  10.7 59.0 %all-to-all-start = ((bf16[64,16,640]{2,1,0:T(8,128)(2,1)}), bf16[64,16,640]{2,1,0:T(8,128)(2,1)}, u32[]{:S(2)}, u32[]{:S(2)}) async-start(bf16[64,16,640]{2,1,0:T(8,128)(2,1)} %pack.1), calls=%async_computation | async-start | bytes 2621440 | tf_op jit(solution)/shard_map/all_to_all | solution.py:215
  29.9 114.2 %all-gather.2.cloned.1.call-start = ((), (), s32[]{:S(2)}) async-start(), calls=%async_computation.4 | async-start | bytes 2228224 | tf_op jit(solution)/shard_map/all_gather | solution.py:232
  34.4 1.3 copy-start.2
  35.8 5.0 %collective-permute-start = (bf16[4,1024,128]{2,1,0:T(8,128)(2,1)S(1)}, bf16[4,1024,128]{2,1,0:T(8,128)(2,1)}, u32[]{:S(2)}, u32[]{:S(2)}) collective-permute-start(bf16[4,1024,128]{2,1,0:T(8,128)(2,1)S(1)} %dynamic-slice_bitcast_fusion), channel_id=1, source_target_pairs={{0,16},{16,0},{1,17},{17,1},{2,18},{18,2},{3,19},{19,3},{4,20},{20... | collective-permute-start | bytes 3145736 | tf_op jit(solution)/shard_map/ppermute | solution.py:173
  42.7 21.8 %collective-permute-start.3 = (bf16[1024,128]{1,0:T(8,128)(2,1)S(1)}, bf16[1024,128]{1,0:T(8,128)(2,1)S(1)}, u32[]{:S(2)}, u32[]{:S(2)}) collective-permute-start(bf16[1024,128]{1,0:T(8,128)(2,1)S(1)} %get-tuple-element.15), channel_id=1, source_target_pairs={{0,768},{256,0},{512,256},{768,512},{1,769},{257,1},{513,257},{769... | collective-permute-start | bytes 786440 | tf_op jit(solution)/shard_map/ppermute | solution.py:173
  47.2 17.2 %collective-permute-start.2 = (bf16[1024,128]{1,0:T(8,128)(2,1)S(1)}, bf16[1024,128]{1,0:T(8,128)(2,1)S(1)}, u32[]{:S(2)}, u32[]{:S(2)}) collective-permute-start(bf16[1024,128]{1,0:T(8,128)(2,1)S(1)} %get-tuple-element.16), channel_id=1, source_target_pairs={{0,512},{256,768},{512,0},{768,256},{1,513},{257,769},{513,1},{769... | collective-permute-start | bytes 786440 | tf_op jit(solution)/shard_map/ppermute | solution.py:173
  49.5 19.4 %collective-permute-start.1 = (bf16[1024,128]{1,0:T(8,128)(2,1)S(1)}, bf16[1024,128]{1,0:T(8,128)(2,1)S(1)}, u32[]{:S(2)}, u32[]{:S(2)}) collective-permute-start(bf16[1024,128]{1,0:T(8,128)(2,1)S(1)} %get-tuple-element.14), channel_id=1, source_target_pairs={{0,256},{256,512},{512,768},{768,0},{1,257},{257,513},{513,769},{7... | collective-permute-start | bytes 786440 | tf_op jit(solution)/shard_map/ppermute | solution.py:173
  72.8 47.1 %all-to-all-start.1 = ((bf16[64,16,640]{2,1,0:T(8,128)(2,1)}), bf16[64,16,640]{2,1,0:T(8,128)(2,1)S(1)}, u32[]{:S(2)}, u32[]{:S(2)}) async-start(bf16[64,16,640]{2,1,0:T(8,128)(2,1)} %gather_fusion), calls=%async_computation.1 | async-start | bytes 2621440 | tf_op jit(solution)/shard_map/all_to_all | solution.py:215
  81.1 7.2 %collective-permute-start.6 = (bf16[4,64,128]{2,1,0:T(8,128)(2,1)}, bf16[4,64,128]{2,1,0:T(8,128)(2,1)S(1)}, u32[]{:S(2)}, u32[]{:S(2)}) collective-permute-start(bf16[4,64,128]{2,1,0:T(8,128)(2,1)} %get-tuple-element.18), channel_id=1, source_target_pairs={{0,3},{1,0},{2,1},{3,2},{4,7},{5,4},{6,5},{7,6},{8,11},{9,8},{10,9... | collective-permute-start | bytes 196616 | tf_op jit(solution)/shard_map/ppermute | solution.py:173
  83.0 10.1 %collective-permute-start.5 = (bf16[4,64,128]{2,1,0:T(8,128)(2,1)}, bf16[4,64,128]{2,1,0:T(8,128)(2,1)S(1)}, u32[]{:S(2)}, u32[]{:S(2)}) collective-permute-start(bf16[4,64,128]{2,1,0:T(8,128)(2,1)} %get-tuple-element.19), channel_id=1, source_target_pairs={{0,2},{1,3},{2,0},{3,1},{4,6},{5,7},{6,4},{7,5},{8,10},{9,11},{10,... | collective-permute-start | bytes 196616 | tf_op jit(solution)/shard_map/ppermute | solution.py:173
  84.9 9.1 %collective-permute-start.4 = (bf16[4,64,128]{2,1,0:T(8,128)(2,1)S(1)}, bf16[4,64,128]{2,1,0:T(8,128)(2,1)}, u32[]{:S(2)}, u32[]{:S(2)}) collective-permute-start(bf16[4,64,128]{2,1,0:T(8,128)(2,1)S(1)} %get-tuple-element.17), channel_id=1, source_target_pairs={{0,1},{1,2},{2,3},{3,0},{4,5},{5,6},{6,7},{7,4},{8,9},{9,10},{10,1... | collective-permute-start | bytes 196616 | tf_op jit(solution)/shard_map/ppermute | solution.py:173
  95.0 22.8 %collective-permute-start.9 = (bf16[64,128]{1,0:T(8,128)(2,1)S(1)}, bf16[64,128]{1,0:T(8,128)(2,1)S(1)}, u32[]{:S(2)}, u32[]{:S(2)}) collective-permute-start(bf16[64,128]{1,0:T(8,128)(2,1)S(1)} %get-tuple-element.21), channel_id=1, source_target_pairs={{0,12},{1,13},{2,14},{3,15},{4,0},{5,1},{6,2},{7,3},{8,4},{9,5},{1... | collective-permute-start | bytes 49160 | tf_op jit(solution)/shard_map/ppermute | solution.py:173
  106.7 13.2 %collective-permute-start.8 = (bf16[64,128]{1,0:T(8,128)(2,1)S(1)}, bf16[64,128]{1,0:T(8,128)(2,1)S(1)}, u32[]{:S(2)}, u32[]{:S(2)}) collective-permute-start(bf16[64,128]{1,0:T(8,128)(2,1)S(1)} %get-tuple-element.22), channel_id=1, source_target_pairs={{0,8},{1,9},{2,10},{3,11},{4,12},{5,13},{6,14},{7,15},{8,0},{9,1},... | collective-permute-start | bytes 49160 | tf_op jit(solution)/shard_map/ppermute | solution.py:173
  110.5 9.4 %collective-permute-start.7 = (bf16[64,128]{1,0:T(8,128)(2,1)S(1)}, bf16[64,128]{1,0:T(8,128)(2,1)S(1)}, u32[]{:S(2)}, u32[]{:S(2)}) collective-permute-start(bf16[64,128]{1,0:T(8,128)(2,1)S(1)} %get-tuple-element.20), channel_id=1, source_target_pairs={{0,4},{1,5},{2,6},{3,7},{4,8},{5,9},{6,10},{7,11},{8,12},{9,13},{1... | collective-permute-start | bytes 49160 | tf_op jit(solution)/shard_map/ppermute | solution.py:173
  134.1 20.3 %all-to-all-start.3 = ((bf16[64,8,128]{2,1,0:T(8,128)(2,1)}), bf16[64,8,128]{2,1,0:T(8,128)(2,1)S(1)}, u32[]{:S(2)}, u32[]{:S(2)}) async-start(bf16[64,8,128]{2,1,0:T(8,128)(2,1)} %broadcast_in_dim.32), calls=%async_computation.3 | async-start | bytes 262144 | tf_op jit(solution)/shard_map/all_to_all | solution.py:215
  144.1 1.6 copy-start.5
Sparse Core Ops, SparseCore 0:
  38.5 70.8 all-gather.1

commit v3 on v2

--- a/solution.py
+++ b/solution.py
@@ -90,22 +90,22 @@
             yield r * col_groups + c, r * GROUP_ROWS, c * share_cols
 
 
-def pack_kernel(keep, x_ref, g_ref, out_ref):
-    width, joint = x_ref.shape[1], x_ref.shape[1] + g_ref.shape[1]
-    row_groups = (x_ref.shape[0] - keep) // GROUP_ROWS
+def pack_kernel(keep, x_ref, g_ref, out_ref, block_ref, sems):
+    width, joint = x_ref.shape[1], block_ref.shape[1]
+    moved = block_ref.shape[0]
     share_cols = out_ref.shape[2]
-    for share, row, start in shares(row_groups, joint // share_cols, share_cols):
-        rows = pl.ds(keep + row, GROUP_ROWS)
-        split = min(max(width - start, 0), share_cols)
-        if split > 0:
-            out_ref[share, :, pl.ds(0, split)] = x_ref[rows, pl.ds(start, split)]
-        if split < share_cols:
-            out_ref[share, :, pl.ds(split, share_cols - split)] = g_ref[
-                rows, pl.ds(start + split - width, share_cols - split)
-            ]
-
-
-def term_kernel(keep, lengths_ref, x_ref, g_ref, seg_col_ref, seg_row_ref, term_ref, y_ref):
+    rows = pl.ds(keep, moved)
+    from_x = pltpu.make_async_copy(x_ref.at[rows], block_ref.at[:, pl.ds(0, width)], sems.at[0])
+    from_g = pltpu.make_async_copy(g_ref.at[rows], block_ref.at[:, pl.ds(width, joint - width)], sems.at[1])
+    from_x.start()
+    from_g.start()
+    from_x.wait()
+    from_g.wait()
+    for share, row, start in shares(moved // GROUP_ROWS, joint // share_cols, share_cols):
+        out_ref[share] = block_ref[pl.ds(row, GROUP_ROWS), pl.ds(start, share_cols)]
+
+
+def term_kernel(keep, core_ref, lengths_ref, x_ref, g_ref, seg_col_ref, seg_row_ref, mine_ref, other_ref, y_ref):
     width = g_ref.shape[1]
     rows_all = x_ref.shape[0]
 
@@ -121,12 +121,15 @@
         ends.append(total)
     rows_of(pl.ds(keep, moved), *masks(segments_of(ends, (moved, 1), 0), segments_of(ends, (1, moved), 1)))
     rows_of(pl.ds(0, keep), *masks(seg_col_ref[...], seg_row_ref[...]))
-    blocks, _, block_cols = term_ref.shape
+    blocks, _, block_cols = mine_ref.shape
     joined = max(1, 256 // block_cols)
-    for b in range(0, blocks, joined):
-        found = dot(g_ref[...], y_ref[:, pl.ds(b * block_cols, joined * block_cols)], ((0,), (0,)))
-        for i in range(joined):
-            term_ref[b + i] = found[:, i * block_cols : (i + 1) * block_cols].astype(BF16)
+    core = core_ref[0]
+    for half, term_ref in ((core, mine_ref), (1 - core, other_ref)):
+        for b in range(0, blocks, joined):
+            start = pl.multiple_of((half * blocks + b) * block_cols, 128)
+            found = dot(g_ref[...], y_ref[:, pl.ds(start, joined * block_cols)], ((0,), (0,)))
+            for i in range(joined):
+                term_ref[b + i] = found[:, i * block_cols : (i + 1) * block_cols].astype(BF16)
 
 
 def back_kernel(keep, lengths_ref, x_ref, g_ref, came_ref, w_ref, seg_col_ref, seg_row_ref, out_ref, block_ref):
@@ -160,8 +163,9 @@
 
 
 VMEM = pl.BlockSpec(memory_space=pltpu.VMEM)
+HBM = pl.BlockSpec(memory_space=pltpu.HBM)
 SMEM = pl.BlockSpec(memory_space=pltpu.SMEM)
-PARAMS = pltpu.CompilerParams(vmem_limit_bytes=40 * 2**20)
+PARAMS = pltpu.CompilerParams(vmem_limit_bytes=24 * 2**20)
 
 
 def cost(flops, nbytes):
@@ -188,6 +192,25 @@
         for step in range(1, size)
     ]
     return added(pick(value, me), *came).astype(BF16)
+
+
+def ring_of_four_sum(value, axis):
+    size, me = lax.axis_size(axis), lax.axis_index(axis)
+    if size != 4:
+        done = scatter_sum(value, axis)
+        return done, [done]
+    half = value.shape[1] // 2
+    halves = []
+    for rows, first, second in ((value[:, :half], 1, 3), (value[:, half:], 3, 1)):
+        sent = jnp.stack([pick(rows, me ^ first), pick(rows, me ^ 2)])
+        held = jnp.stack([pick(rows, me), pick(rows, me ^ second)])
+        halves.append((permuted(sent, axis, lambda i, first=first: i ^ first), held, second))
+    first_round = [added(held, came).astype(BF16) for came, held, _ in halves]
+    done = []
+    for held, (_, _, second) in zip(first_round, halves):
+        came = permuted(held[1], axis, lambda i, second=second: i ^ second)
+        done.append(added(held[0], came).astype(BF16))
+    return jnp.concatenate(done), first_round
 
 
 def ring_of_rings_sum(value, axis, inner):
@@ -234,32 +257,35 @@
     block = pl.pallas_call(
         functools.partial(pack_kernel, keep),
         out_shape=jax.ShapeDtypeStruct((groups, GROUP_ROWS, share_cols), BF16),
-        in_specs=[VMEM, VMEM],
+        in_specs=[HBM, HBM],
         out_specs=VMEM,
-        compiler_params=PARAMS,
+        scratch_shapes=[pltpu.VMEM((moved, 5 * width), BF16), pltpu.SemaphoreType.DMA((2,))],
+        compiler_params=pltpu.CompilerParams(vmem_limit_bytes=60 * 2**20),
         cost_estimate=cost(0, 8 * width),
         name="pack",
     )(uvqk, grad_out)
     uvqk, grad_out, block = lax.optimization_barrier((uvqk, grad_out, block))
     block = exchange(block)
 
-    blocks = n_core * n_x
-    block_cols = width // blocks
-    term = pl.pallas_call(
+    block_cols = width // (n_core * n_x)
+    core_half = jax.ShapeDtypeStruct((n_x, width, block_cols), BF16)
+    mine, other = pl.pallas_call(
         functools.partial(term_kernel, keep),
-        out_shape=jax.ShapeDtypeStruct((blocks, width, block_cols), BF16),
-        in_specs=[SMEM, VMEM, VMEM, VMEM, VMEM],
-        out_specs=VMEM,
+        out_shape=(core_half, core_half),
+        in_specs=[SMEM, SMEM, VMEM, VMEM, VMEM, VMEM],
+        out_specs=(VMEM, VMEM),
         scratch_shapes=[pltpu.VMEM((rows, width), BF16)],
         compiler_params=PARAMS,
         cost_estimate=cost(0, 8 * width),
         name="term",
-    )(own_lengths, uvqk, grad_out, seg_col, seg_row)
-    part = scatter_sum(term.reshape(n_core, n_x, width, block_cols), "core")
-    part = scatter_sum(part, "x")
+    )(lax.axis_index("core").reshape(1), own_lengths, uvqk, grad_out, seg_col, seg_row)
+    part = added(mine, permuted(other, "core", lambda i: i ^ 1)).astype(BF16)
+    part, first_round = ring_of_four_sum(part, "x")
     own_rows = width // n_z
+    block = lax.optimization_barrier((block, first_round))[0]
+    block = block[source_of]
     part, block = lax.optimization_barrier((part, block))
-    block = exchange(block[source_of])
+    block = exchange(block)
     part = ring_of_rings_sum(part.reshape(n_z, own_rows, block_cols), "z", min(4, n_z))
     part = lax.optimization_barrier((part, block))[0]
     part = exchange(part.reshape(n_y, own_rows // n_y, block_cols), "y")

time: 163 us -> 166 us (1.018)
  starting transfers between devices: 77.7 us -> 83.6 us
  local copies, waits for them, and re-layouts: 12.6 us -> 8.95 us
  waiting for transfers between devices: 30.5 us -> 27.9 us
  Pallas kernels: 8.33 us -> 10.7 us
    ppermute x10 -> x11, starting transfers between devices: 42 us -> 61.3 us  [permuted(): return lax.ppermute(value, axis, [(i, target(i)) for i in range(size)])]
    all_to_all x3, starting transfers between devices: 35.7 us -> 22.3 us  [exchange(): return lax.all_to_all(value, axes, split_axis=0, concat_axis=0, tiled=True)]
    ppermute x10 -> x11, waiting for transfers between devices: 26.8 us -> 21.2 us  [permuted(): return lax.ppermute(value, axis, [(i, target(i)) for i in range(size)])]
    unnamed x18 -> x12, local copies, waits for them, and re-layouts: 5.48 us -> 1.79 us
    all_to_all x3, waiting for transfers between devices: 3.65 us -> 5.99 us  [exchange(): return lax.all_to_all(value, axes, split_axis=0, concat_axis=0, tiled=True)]
  transfers between devices with their start and end apart: 14 -> 15, of which waited for: 7 -> 8; matrix products, arithmetic and copies ran while one was open for 7% -> 6% of each run, Pallas kernels for 4% -> 3%
where the time goes in v3:
time: 166 us; the launch traced here: 165 us
  starting transfers between devices  83.6 us (50%)
  waiting for transfers between devices  27.9 us (17%)
  between operations  15 us (9%)
  blocking collectives  13.6 us (8%)
  Pallas kernels  10.7 us (6%)
  local copies, waits for them, and re-layouts  8.95 us (5%)
  other arithmetic  4.97 us (3%)
    ppermute x11, starting transfers between devices, permuted(): return lax.ppermute(value, axis, [(i, target(i)) for i in range(size)])  61.3 us
    all_to_all x3, starting transfers between devices, exchange(): return lax.all_to_all(value, axes, split_axis=0, concat_axis=0, tiled=True)  22.3 us
    ppermute x11, waiting for transfers between devices, permuted(): return lax.ppermute(value, axis, [(i, target(i)) for i in range(size)])  21.2 us
    all_to_all x1, blocking collectives, exchange(): return lax.all_to_all(value, axes, split_axis=0, concat_axis=0, tiled=True)  13.6 us
    all_to_all x3, waiting for transfers between devices, exchange(): return lax.all_to_all(value, axes, split_axis=0, concat_axis=0, tiled=True)  5.99 us
    pallas_call x1, Pallas kernels, local(): pl.pallas_call(functools.partial(back_kernel, keep), out_shape=jax.ShapeD...  5.03 us
  transfers between devices with their start and end apart: 15, of which 8 were waited for; matrix products, arithmetic and copies ran while one was open for 6% of the time, Pallas kernels for 3%

profile of v3, /device:TPU:1, one launch (start us, length us, event | category | flops | bytes accessed | tf_op | source)
XLA Modules:
  0.0 164.8 jit_solution(1408594619686629938)
XLA Ops:
  7.2 1.3 fusion.7
  9.1 0.8 constant_dynamic-slice_fusion.8
  9.9 0.1 copy.27.lengths_ref
  10.0 2.6 %pack.1 = bf16[64,16,640]{2,1,0:T(8,128)(2,1)} custom-call(bf16[192,4096]{1,0:T(8,128)(2,1)} %x_ref.3, bf16[192,1024]{1,0:T(8,128)(2,1)} %g_ref.3), custom_call_target="tpu_custom_call" | custom-call | bytes 8192 | tf_op jit(solution)/shard_map/pack/pallas_call | solution.py:257
  12.6 0.1 copy.23.seg_col_ref
  12.7 3.1 %term.1 = (bf16[4,1024,128]{2,1,0:T(8,128)(2,1)S(1)}, bf16[4,1024,128]{2,1,0:T(8,128)(2,1)}) custom-call(s32[1]{0:T(128)} %bitcast.core_ref, s32[1,3]{1,0:T(1,128)S(1)} %copy.27.lengths_ref, bf16[192,4096]{1,0:T(8,128)(2,1)S(1)} %copy-done, bf16[192,1024]{1,0:T(8,128)(2,1)S(1)} %copy-done.1, s32[64,1]{1,0:T(8,128)S(1)} %copy.23.seg_col_ref, ...), custom_call_target="tpu_custom_call" | custom-call | bytes 8192 | tf_op jit(solution)/shard_map/term/pallas_call | solution.py:272
  15.8 16.2 %collective-permute-start = (bf16[4,1024,128]{2,1,0:T(8,128)(2,1)}, bf16[4,1024,128]{2,1,0:T(8,128)(2,1)}, u32[]{:S(2)}, u32[]{:S(2)}) collective-permute-start(bf16[4,1024,128]{2,1,0:T(8,128)(2,1)} %get-tuple-element.14), channel_id=1, source_target_pairs={{0,16},{16,0},{1,17},{17,1},{2,18},{18,2},{3,19},{19,3},{4,20},{20... | collective-permute-start | bytes 3145736 | tf_op jit(solution)/shard_map/ppermute | solution.py:177
  32.0 5.1 %all-to-all-start = ((bf16[64,16,640]{2,1,0:T(8,128)(2,1)}), bf16[64,16,640]{2,1,0:T(8,128)(2,1)}, u32[]{:S(2)}, u32[]{:S(2)}) async-start(bf16[64,16,640]{2,1,0:T(8,128)(2,1)} %pack.1), calls=%async_computation | async-start | bytes 2621440 | tf_op jit(solution)/shard_map/all_to_all | solution.py:238
  37.1 0.0 all-gather.2.cloned.1.call-start
  37.2 0.7 all-gather.2.cloned.1.call-update
  37.9 0.1 select_reduce_fusion
  38.0 0.0 collective-permute-done
  38.0 1.6 add_convert_fusion
  39.6 0.1 fusion.9
  39.7 0.1 constant_dynamic-slice_fusion.3
  39.8 3.2 %collective-permute-start.1 = (bf16[2,512,128]{2,1,0:T(8,128)(2,1)S(1)}, bf16[2,512,128]{2,1,0:T(8,128)(2,1)S(1)}, u32[]{:S(2)}, u32[]{:S(2)}) collective-permute-start(bf16[2,512,128]{2,1,0:T(8,128)(2,1)S(1)} %pad_maximum_fusion), channel_id=1, source_target_pairs={{0,256},{256,0},{512,768},{768,512},{1,257},{257,1},{513,769},{769... | collective-permute-start | bytes 786440 | tf_op jit(solution)/shard_map/ppermute | solution.py:177
  43.1 3.8 %collective-permute-start.3 = (bf16[2,512,128]{2,1,0:T(8,128)(2,1)S(1)}, bf16[2,512,128]{2,1,0:T(8,128)(2,1)S(1)}, u32[]{:S(2)}, u32[]{:S(2)}) collective-permute-start(bf16[2,512,128]{2,1,0:T(8,128)(2,1)S(1)} %pad_maximum_fusion.1), channel_id=1, source_target_pairs={{0,768},{256,512},{512,256},{768,0},{1,769},{257,513},{513,257},{7... | collective-permute-start | bytes 786440 | tf_op jit(solution)/shard_map/ppermute | solution.py:177
  46.9 5.7 %collective-permute-done.1 = bf16[2,512,128]{2,1,0:T(8,128)(2,1)S(1)} collective-permute-done((bf16[2,512,128]{2,1,0:T(8,128)(2,1)S(1)}, bf16[2,512,128]{2,1,0:T(8,128)(2,1)S(1)}, u32[]{:S(2)}, u32[]{:S(2)}) %collective-permute-start.1) | collective-permute-done | bytes 262176 | tf_op jit(solution)/shard_map/ppermute | solution.py:177
  52.6 0.1 add_convert_fusion.2
  52.7 5.9 %collective-permute-start.2 = (bf16[512,128]{1,0:T(8,128)(2,1)S(1)}, bf16[512,128]{1,0:T(8,128)(2,1)S(1)}, u32[]{:S(2)}, u32[]{:S(2)}) collective-permute-start(bf16[512,128]{1,0:T(8,128)(2,1)S(1)} %slice_bitcast_fusion.2), channel_id=1, source_target_pairs={{0,768},{256,512},{512,256},{768,0},{1,769},{257,513},{513,257},{7... | collective-permute-start | bytes 393224 | tf_op jit(solution)/shard_map/ppermute | solution.py:177
  58.6 0.1 add_convert_fusion.1
  58.7 1.9 %collective-permute-start.4 = (bf16[512,128]{1,0:T(8,128)(2,1)S(1)}, bf16[512,128]{1,0:T(8,128)(2,1)S(1)}, u32[]{:S(2)}, u32[]{:S(2)}) collective-permute-start(bf16[512,128]{1,0:T(8,128)(2,1)S(1)} %slice_bitcast_fusion), channel_id=1, source_target_pairs={{0,256},{256,0},{512,768},{768,512},{1,257},{257,1},{513,769},{769... | collective-permute-start | bytes 393224 | tf_op jit(solution)/shard_map/ppermute | solution.py:177
  60.6 3.6 %collective-permute-done.2 = bf16[512,128]{1,0:T(8,128)(2,1)S(1)} collective-permute-done((bf16[512,128]{1,0:T(8,128)(2,1)S(1)}, bf16[512,128]{1,0:T(8,128)(2,1)S(1)}, u32[]{:S(2)}, u32[]{:S(2)}) %collective-permute-start.2) | collective-permute-done | bytes 131104 | tf_op jit(solution)/shard_map/ppermute | solution.py:177
  64.3 3.7 %collective-permute-done.4 = bf16[512,128]{1,0:T(8,128)(2,1)S(1)} collective-permute-done((bf16[512,128]{1,0:T(8,128)(2,1)S(1)}, bf16[512,128]{1,0:T(8,128)(2,1)S(1)}, u32[]{:S(2)}, u32[]{:S(2)}) %collective-permute-start.4) | collective-permute-done | bytes 131104 | tf_op jit(solution)/shard_map/ppermute | solution.py:177
  68.0 0.7 pad_maximum_fusion.2
  68.7 2.3 %all-to-all-done = bf16[64,16,640]{2,1,0:T(8,128)(2,1)} async-done(((bf16[64,16,640]{2,1,0:T(8,128)(2,1)}), bf16[64,16,640]{2,1,0:T(8,128)(2,1)}, u32[]{:S(2)}, u32[]{:S(2)}) %all-to-all-start) | async-done | bytes 1310752 | tf_op jit(solution)/shard_map/all_to_all | solution.py:238
  71.1 3.1 %gather_fusion = bf16[64,16,640]{2,1,0:T(8,128)(2,1)} fusion(bf16[64,16,640]{2,1,0:T(8,128)(2,1)} %all-to-all-done, s32[1024]{0:T(1024)S(1)} %pad_clamp_fusion), kind=kCustom, calls=%fused_computation | custom fusion | bytes 2621696 | tf_op jit(solution)/shard_map/gather | solution.py:286
  74.2 7.8 %all-to-all-start.1 = ((bf16[64,16,640]{2,1,0:T(8,128)(2,1)}), bf16[64,16,640]{2,1,0:T(8,128)(2,1)S(1)}, u32[]{:S(2)}, u32[]{:S(2)}) async-start(bf16[64,16,640]{2,1,0:T(8,128)(2,1)} %gather_fusion), calls=%async_computation.1 | async-start | bytes 2621440 | tf_op jit(solution)/shard_map/all_to_all | solution.py:238
  82.0 1.6 dynamic-slice_bitcast_fusion.2
  83.6 1.9 %collective-permute-start.5 = (bf16[4,64,128]{2,1,0:T(8,128)(2,1)}, bf16[4,64,128]{2,1,0:T(8,128)(2,1)S(1)}, u32[]{:S(2)}, u32[]{:S(2)}) collective-permute-start(bf16[4,64,128]{2,1,0:T(8,128)(2,1)} %get-tuple-element.30), channel_id=1, source_target_pairs={{0,1},{1,2},{2,3},{3,0},{4,5},{5,6},{6,7},{7,4},{8,9},{9,10},{10,1... | collective-permute-start | bytes 196616 | tf_op jit(solution)/shard_map/ppermute | solution.py:177
  85.5 1.9 %collective-permute-start.6 = (bf16[4,64,128]{2,1,0:T(8,128)(2,1)}, bf16[4,64,128]{2,1,0:T(8,128)(2,1)S(1)}, u32[]{:S(2)}, u32[]{:S(2)}) collective-permute-start(bf16[4,64,128]{2,1,0:T(8,128)(2,1)} %get-tuple-element.32), channel_id=1, source_target_pairs={{0,2},{1,3},{2,0},{3,1},{4,6},{5,7},{6,4},{7,5},{8,10},{9,11},{10,... | collective-permute-start | bytes 196616 | tf_op jit(solution)/shard_map/ppermute | solution.py:177
  87.4 5.2 %collective-permute-start.7 = (bf16[4,64,128]{2,1,0:T(8,128)(2,1)S(1)}, bf16[4,64,128]{2,1,0:T(8,128)(2,1)}, u32[]{:S(2)}, u32[]{:S(2)}) collective-permute-start(bf16[4,64,128]{2,1,0:T(8,128)(2,1)S(1)} %get-tuple-element.31), channel_id=1, source_target_pairs={{0,3},{1,0},{2,1},{3,2},{4,7},{5,4},{6,5},{7,6},{8,11},{9,8},{10,9... | collective-permute-start | bytes 196616 | tf_op jit(solution)/shard_map/ppermute | solution.py:177
  92.6 0.0 collective-permute-done.5
  92.6 3.3 %collective-permute-done.6 = bf16[4,64,128]{2,1,0:T(8,128)(2,1)S(1)} collective-permute-done((bf16[4,64,128]{2,1,0:T(8,128)(2,1)}, bf16[4,64,128]{2,1,0:T(8,128)(2,1)S(1)}, u32[]{:S(2)}, u32[]{:S(2)}) %collective-permute-start.6) | collective-permute-done | bytes 65568 | tf_op jit(solution)/shard_map/ppermute | solution.py:177
  95.9 0.3 collective-permute-done.7
  96.2 0.9 fusion.4
  97.2 10.8 %collective-permute-start.10 = (bf16[64,128]{1,0:T(8,128)(2,1)S(1)}, bf16[64,128]{1,0:T(8,128)(2,1)S(1)}, u32[]{:S(2)}, u32[]{:S(2)}) collective-permute-start(bf16[64,128]{1,0:T(8,128)(2,1)S(1)} %get-tuple-element.34), channel_id=1, source_target_pairs={{0,12},{1,13},{2,14},{3,15},{4,0},{5,1},{6,2},{7,3},{8,4},{9,5},{1... | collective-permute-start | bytes 49160 | tf_op jit(solution)/shard_map/ppermute | solution.py:177
  108.0 1.9 %collective-permute-start.8 = (bf16[64,128]{1,0:T(8,128)(2,1)S(1)}, bf16[64,128]{1,0:T(8,128)(2,1)S(1)}, u32[]{:S(2)}, u32[]{:S(2)}) collective-permute-start(bf16[64,128]{1,0:T(8,128)(2,1)S(1)} %get-tuple-element.33), channel_id=1, source_target_pairs={{0,4},{1,5},{2,6},{3,7},{4,8},{5,9},{6,10},{7,11},{8,12},{9,13},{1... | collective-permute-start | bytes 49160 | tf_op jit(solution)/shard_map/ppermute | solution.py:177
  109.9 8.6 %collective-permute-start.9 = (bf16[64,128]{1,0:T(8,128)(2,1)S(1)}, bf16[64,128]{1,0:T(8,128)(2,1)S(1)}, u32[]{:S(2)}, u32[]{:S(2)}) collective-permute-start(bf16[64,128]{1,0:T(8,128)(2,1)S(1)} %get-tuple-element.35), channel_id=1, source_target_pairs={{0,8},{1,9},{2,10},{3,11},{4,12},{5,13},{6,14},{7,15},{8,0},{9,1},... | collective-permute-start | bytes 49160 | tf_op jit(solution)/shard_map/ppermute | solution.py:177
  118.6 4.6 %collective-permute-done.9 = bf16[64,128]{1,0:T(8,128)(2,1)S(1)} collective-permute-done((bf16[64,128]{1,0:T(8,128)(2,1)S(1)}, bf16[64,128]{1,0:T(8,128)(2,1)S(1)}, u32[]{:S(2)}, u32[]{:S(2)}) %collective-permute-start.9) | collective-permute-done | bytes 16416 | tf_op jit(solution)/shard_map/ppermute | solution.py:177
  123.1 13.6 %all_to_all.20 = f32[8,8,128]{2,1,0:T(8,128)S(1)} all-to-all(f32[8,8,128]{2,1,0:T(8,128)S(1)} %bitcast.50), channel_id=1, replica_groups=mesh['x'=4,'y'=8,'core'=2,'z'=16] {'y'}, dimensions={0} | all-to-all | bytes 65536 | tf_op jit(solution)/shard_map/all_to_all | solution.py:238
  136.8 0.7 broadcast_in_dim.32
  137.5 9.4 %all-to-all-start.3 = ((bf16[64,8,128]{2,1,0:T(8,128)(2,1)}), bf16[64,8,128]{2,1,0:T(8,128)(2,1)S(1)}, u32[]{:S(2)}, u32[]{:S(2)}) async-start(bf16[64,8,128]{2,1,0:T(8,128)(2,1)} %broadcast_in_dim.32), calls=%async_computation.3 | async-start | bytes 262144 | tf_op jit(solution)/shard_map/all_to_all | solution.py:238
  146.9 0.1 copy.26.lengths_ref
  147.0 1.6 copy-done.2
  148.6 5.0 %back.1 = bf16[192,4096]{1,0:T(8,128)(2,1)} custom-call(s32[1,3]{1,0:T(1,128)S(1)} %copy.26.lengths_ref, bf16[192,4096]{1,0:T(8,128)(2,1)S(1)} %copy-done, bf16[192,1024]{1,0:T(8,128)(2,1)S(1)} %copy-done.1, bf16[64,16,640]{2,1,0:T(8,128)(2,1)S(1)} %all-to-all-done.1.came_ref, bf16[1024,1024]{1,0:T(8,128)(2,1)S(1)} %copy-done.2, ...), custom_call_target="tpu_custom_call" | custom-call | flops 1610612736 | bytes 8388608 | tf_op jit(solution)/shard_map/back/pallas_call | solution.py:297
  153.6 3.6 %all-to-all-done.3 = bf16[64,8,128]{2,1,0:T(8,128)(2,1)S(1)} async-done(((bf16[64,8,128]{2,1,0:T(8,128)(2,1)}), bf16[64,8,128]{2,1,0:T(8,128)(2,1)S(1)}, u32[]{:S(2)}, u32[]{:S(2)}) %all-to-all-start.3) | async-done | bytes 131104 | tf_op jit(solution)/shard_map/all_to_all | solution.py:238
  157.3 0.7 copy.25
  (27 shorter events, 0.3 us)
Async XLA Ops:
  10.0 2.6 %copy-start.3 = (s32[1,64]{1,0:T(1,128)S(1)}, s32[1,64]{1,0:T(1,128)}, u32[]{:S(2)}) copy-start(s32[1,64]{1,0:T(1,128)} %seg_row_ref.3) | copy-start | bytes 772
  10.0 2.7 %copy-start = (bf16[192,4096]{1,0:T(8,128)(2,1)S(1)}, bf16[192,4096]{1,0:T(8,128)(2,1)}, u32[]{:S(2)}) copy-start(bf16[192,4096]{1,0:T(8,128)(2,1)} %x_ref.3) | copy-start | bytes 4718596
  10.0 2.7 %copy-start.1 = (bf16[192,1024]{1,0:T(8,128)(2,1)S(1)}, bf16[192,1024]{1,0:T(8,128)(2,1)}, u32[]{:S(2)}) copy-start(bf16[192,1024]{1,0:T(8,128)(2,1)} %g_ref.3) | copy-start | bytes 1179652
  15.8 22.0 %copy-start.4 = (s32[64]{0:T(128)S(1)}, s32[64]{0:T(128)}, u32[]{:S(2)}) copy-start(s32[64]{0:T(128)} %param.11) | copy-start | bytes 772
  15.8 22.2 %collective-permute-start = (bf16[4,1024,128]{2,1,0:T(8,128)(2,1)}, bf16[4,1024,128]{2,1,0:T(8,128)(2,1)}, u32[]{:S(2)}, u32[]{:S(2)}) collective-permute-start(bf16[4,1024,128]{2,1,0:T(8,128)(2,1)} %get-tuple-element.14), channel_id=1, source_target_pairs={{0,16},{16,0},{1,17},{17,1},{2,18},{18,2},{3,19},{19,3},{4,20},{20... | collective-permute-start | bytes 3145736 | tf_op jit(solution)/shard_map/ppermute | solution.py:177
  32.0 39.0 %all-to-all-start = ((bf16[64,16,640]{2,1,0:T(8,128)(2,1)}), bf16[64,16,640]{2,1,0:T(8,128)(2,1)}, u32[]{:S(2)}, u32[]{:S(2)}) async-start(bf16[64,16,640]{2,1,0:T(8,128)(2,1)} %pack.1), calls=%async_computation | async-start | bytes 2621440 | tf_op jit(solution)/shard_map/all_to_all | solution.py:238
  37.1 109.9 %all-gather.2.cloned.1.call-start = ((), (), s32[]{:S(2)}) async-start(), calls=%async_computation.4 | async-start | bytes 2228224 | tf_op jit(solution)/shard_map/all_gather | solution.py:255
  39.8 12.8 %collective-permute-start.1 = (bf16[2,512,128]{2,1,0:T(8,128)(2,1)S(1)}, bf16[2,512,128]{2,1,0:T(8,128)(2,1)S(1)}, u32[]{:S(2)}, u32[]{:S(2)}) collective-permute-start(bf16[2,512,128]{2,1,0:T(8,128)(2,1)S(1)} %pad_maximum_fusion), channel_id=1, source_target_pairs={{0,256},{256,0},{512,768},{768,512},{1,257},{257,1},{513,769},{769... | collective-permute-start | bytes 786440 | tf_op jit(solution)/shard_map/ppermute | solution.py:177
  43.1 15.5 %collective-permute-start.3 = (bf16[2,512,128]{2,1,0:T(8,128)(2,1)S(1)}, bf16[2,512,128]{2,1,0:T(8,128)(2,1)S(1)}, u32[]{:S(2)}, u32[]{:S(2)}) collective-permute-start(bf16[2,512,128]{2,1,0:T(8,128)(2,1)S(1)} %pad_maximum_fusion.1), channel_id=1, source_target_pairs={{0,768},{256,512},{512,256},{768,0},{1,769},{257,513},{513,257},{7... | collective-permute-start | bytes 786440 | tf_op jit(solution)/shard_map/ppermute | solution.py:177
  52.7 11.5 %collective-permute-start.2 = (bf16[512,128]{1,0:T(8,128)(2,1)S(1)}, bf16[512,128]{1,0:T(8,128)(2,1)S(1)}, u32[]{:S(2)}, u32[]{:S(2)}) collective-permute-start(bf16[512,128]{1,0:T(8,128)(2,1)S(1)} %slice_bitcast_fusion.2), channel_id=1, source_target_pairs={{0,768},{256,512},{512,256},{768,0},{1,769},{257,513},{513,257},{7... | collective-permute-start | bytes 393224 | tf_op jit(solution)/shard_map/ppermute | solution.py:177
  58.7 9.3 %collective-permute-start.4 = (bf16[512,128]{1,0:T(8,128)(2,1)S(1)}, bf16[512,128]{1,0:T(8,128)(2,1)S(1)}, u32[]{:S(2)}, u32[]{:S(2)}) collective-permute-start(bf16[512,128]{1,0:T(8,128)(2,1)S(1)} %slice_bitcast_fusion), channel_id=1, source_target_pairs={{0,256},{256,0},{512,768},{768,512},{1,257},{257,1},{513,769},{769... | collective-permute-start | bytes 393224 | tf_op jit(solution)/shard_map/ppermute | solution.py:177
  74.2 49.0 %all-to-all-start.1 = ((bf16[64,16,640]{2,1,0:T(8,128)(2,1)}), bf16[64,16,640]{2,1,0:T(8,128)(2,1)S(1)}, u32[]{:S(2)}, u32[]{:S(2)}) async-start(bf16[64,16,640]{2,1,0:T(8,128)(2,1)} %gather_fusion), calls=%async_computation.1 | async-start | bytes 2621440 | tf_op jit(solution)/shard_map/all_to_all | solution.py:238
  83.6 9.0 %collective-permute-start.5 = (bf16[4,64,128]{2,1,0:T(8,128)(2,1)}, bf16[4,64,128]{2,1,0:T(8,128)(2,1)S(1)}, u32[]{:S(2)}, u32[]{:S(2)}) collective-permute-start(bf16[4,64,128]{2,1,0:T(8,128)(2,1)} %get-tuple-element.30), channel_id=1, source_target_pairs={{0,1},{1,2},{2,3},{3,0},{4,5},{5,6},{6,7},{7,4},{8,9},{9,10},{10,1... | collective-permute-start | bytes 196616 | tf_op jit(solution)/shard_map/ppermute | solution.py:177
  85.5 10.4 %collective-permute-start.6 = (bf16[4,64,128]{2,1,0:T(8,128)(2,1)}, bf16[4,64,128]{2,1,0:T(8,128)(2,1)S(1)}, u32[]{:S(2)}, u32[]{:S(2)}) collective-permute-start(bf16[4,64,128]{2,1,0:T(8,128)(2,1)} %get-tuple-element.32), channel_id=1, source_target_pairs={{0,2},{1,3},{2,0},{3,1},{4,6},{5,7},{6,4},{7,5},{8,10},{9,11},{10,... | collective-permute-start | bytes 196616 | tf_op jit(solution)/shard_map/ppermute | solution.py:177
  87.4 8.8 %collective-permute-start.7 = (bf16[4,64,128]{2,1,0:T(8,128)(2,1)S(1)}, bf16[4,64,128]{2,1,0:T(8,128)(2,1)}, u32[]{:S(2)}, u32[]{:S(2)}) collective-permute-start(bf16[4,64,128]{2,1,0:T(8,128)(2,1)S(1)} %get-tuple-element.31), channel_id=1, source_target_pairs={{0,3},{1,0},{2,1},{3,2},{4,7},{5,4},{6,5},{7,6},{8,11},{9,8},{10,9... | collective-permute-start | bytes 196616 | tf_op jit(solution)/shard_map/ppermute | solution.py:177
  97.2 21.4 %collective-permute-start.10 = (bf16[64,128]{1,0:T(8,128)(2,1)S(1)}, bf16[64,128]{1,0:T(8,128)(2,1)S(1)}, u32[]{:S(2)}, u32[]{:S(2)}) collective-permute-start(bf16[64,128]{1,0:T(8,128)(2,1)S(1)} %get-tuple-element.34), channel_id=1, source_target_pairs={{0,12},{1,13},{2,14},{3,15},{4,0},{5,1},{6,2},{7,3},{8,4},{9,5},{1... | collective-permute-start | bytes 49160 | tf_op jit(solution)/shard_map/ppermute | solution.py:177
  108.0 10.6 %collective-permute-start.8 = (bf16[64,128]{1,0:T(8,128)(2,1)S(1)}, bf16[64,128]{1,0:T(8,128)(2,1)S(1)}, u32[]{:S(2)}, u32[]{:S(2)}) collective-permute-start(bf16[64,128]{1,0:T(8,128)(2,1)S(1)} %get-tuple-element.33), channel_id=1, source_target_pairs={{0,4},{1,5},{2,6},{3,7},{4,8},{5,9},{6,10},{7,11},{8,12},{9,13},{1... | collective-permute-start | bytes 49160 | tf_op jit(solution)/shard_map/ppermute | solution.py:177
  109.9 13.2 %collective-permute-start.9 = (bf16[64,128]{1,0:T(8,128)(2,1)S(1)}, bf16[64,128]{1,0:T(8,128)(2,1)S(1)}, u32[]{:S(2)}, u32[]{:S(2)}) collective-permute-start(bf16[64,128]{1,0:T(8,128)(2,1)S(1)} %get-tuple-element.35), channel_id=1, source_target_pairs={{0,8},{1,9},{2,10},{3,11},{4,12},{5,13},{6,14},{7,15},{8,0},{9,1},... | collective-permute-start | bytes 49160 | tf_op jit(solution)/shard_map/ppermute | solution.py:177
  137.5 19.8 %all-to-all-start.3 = ((bf16[64,8,128]{2,1,0:T(8,128)(2,1)}), bf16[64,8,128]{2,1,0:T(8,128)(2,1)S(1)}, u32[]{:S(2)}, u32[]{:S(2)}) async-start(bf16[64,8,128]{2,1,0:T(8,128)(2,1)} %broadcast_in_dim.32), calls=%async_computation.3 | async-start | bytes 262144 | tf_op jit(solution)/shard_map/all_to_all | solution.py:238
  147.0 1.6 copy-start.2
Sparse Core Ops, SparseCore 0:
  40.6 71.2 all-gather.1

commit v4 on v3

--- a/solution.py
+++ b/solution.py
@@ -105,7 +105,7 @@
         out_ref[share] = block_ref[pl.ds(row, GROUP_ROWS), pl.ds(start, share_cols)]
 
 
-def term_kernel(keep, core_ref, lengths_ref, x_ref, g_ref, seg_col_ref, seg_row_ref, mine_ref, other_ref, y_ref):
+def term_kernel(keep, lengths_ref, x_ref, g_ref, seg_col_ref, seg_row_ref, term_ref, y_ref):
     width = g_ref.shape[1]
     rows_all = x_ref.shape[0]
 
@@ -121,23 +121,28 @@
         ends.append(total)
     rows_of(pl.ds(keep, moved), *masks(segments_of(ends, (moved, 1), 0), segments_of(ends, (1, moved), 1)))
     rows_of(pl.ds(0, keep), *masks(seg_col_ref[...], seg_row_ref[...]))
-    blocks, _, block_cols = mine_ref.shape
-    joined = max(1, 256 // block_cols)
-    core = core_ref[0]
-    for half, term_ref in ((core, mine_ref), (1 - core, other_ref)):
-        for b in range(0, blocks, joined):
-            start = pl.multiple_of((half * blocks + b) * block_cols, 128)
-            found = dot(g_ref[...], y_ref[:, pl.ds(start, joined * block_cols)], ((0,), (0,)))
-            for i in range(joined):
-                term_ref[b + i] = found[:, i * block_cols : (i + 1) * block_cols].astype(BF16)
-
-
-def back_kernel(keep, lengths_ref, x_ref, g_ref, came_ref, w_ref, seg_col_ref, seg_row_ref, out_ref, block_ref):
+    for start in range(0, width, 256):
+        cols = pl.ds(start, 256)
+        term_ref[:, cols] = dot(g_ref[...], y_ref[:, cols], ((0,), (0,))).astype(BF16)
+
+
+def back_kernel(
+    keep, where_ref, lengths_ref, x_ref, g_ref, came_ref, w_mine_ref, w_other_ref, seg_col_ref, seg_row_ref,
+    out_ref, block_ref, grads_ref, grad_y_ref
+):
     width = g_ref.shape[1]
     moved, joint = block_ref.shape
     share_cols = came_ref.shape[2]
     for share, row, start in shares(moved // GROUP_ROWS, joint // share_cols, share_cols):
         block_ref[pl.ds(row, GROUP_ROWS), pl.ds(start, share_cols)] = came_ref[share]
+    grads_ref[pl.ds(0, keep), :] = g_ref[pl.ds(0, keep), :]
+    grads_ref[pl.ds(keep, moved), :] = block_ref[:, pl.ds(joint - width, width)]
+    core, x = where_ref[0], where_ref[1]
+    blocks, _, block_cols = w_mine_ref.shape
+    for half, w_ref in ((core, w_mine_ref), (1 - core, w_other_ref)):
+        for step in range(blocks):
+            start = pl.multiple_of((half * blocks + (x ^ step)) * block_cols, 128)
+            grad_y_ref[:, pl.ds(start, block_cols)] = dot(grads_ref[...], w_ref[step], ((1,), (0,)))
 
     def put_in(rows):
         def put(part, cols, found):
@@ -149,14 +154,12 @@
     for i in range(lengths_ref.shape[1]):
         total = total + lengths_ref[0, i]
         ends.append(total)
-    kept_grad_y = dot(g_ref[pl.ds(0, keep), :], w_ref[...], ((1,), (0,)))
     parts = [x_ref[pl.ds(0, keep), pl.ds(i * width, width)] for i in range(4)]
-    backward(*parts, kept_grad_y, *masks(seg_col_ref[...], seg_row_ref[...]), put_in(pl.ds(0, keep)))
-    *parts, grads = [block_ref[:, pl.ds(i * width, width)] for i in range(5)]
-    grad_y = dot(grads, w_ref[...], ((1,), (0,)))
+    backward(*parts, grad_y_ref[pl.ds(0, keep), :], *masks(seg_col_ref[...], seg_row_ref[...]), put_in(pl.ds(0, keep)))
+    parts = [block_ref[:, pl.ds(i * width, width)] for i in range(4)]
     backward(
         *parts,
-        grad_y,
+        grad_y_ref[pl.ds(keep, moved), :],
         *masks(segments_of(ends, (moved, 1), 0), segments_of(ends, (1, moved), 1)),
         put_in(pl.ds(keep, moved)),
     )
@@ -185,53 +188,14 @@
     return functools.reduce(jnp.add, [value.astype(F32) for value in values])
 
 
-def scatter_sum(value, axis):
-    size, me = lax.axis_size(axis), lax.axis_index(axis)
-    came = [
-        permuted(pick(value, (me + step) & (size - 1)), axis, lambda i, step=step: (i + step) % size)
-        for step in range(1, size)
-    ]
-    return added(pick(value, me), *came).astype(BF16)
-
-
-def ring_of_four_sum(value, axis):
-    size, me = lax.axis_size(axis), lax.axis_index(axis)
-    if size != 4:
-        done = scatter_sum(value, axis)
-        return done, [done]
-    half = value.shape[1] // 2
-    halves = []
-    for rows, first, second in ((value[:, :half], 1, 3), (value[:, half:], 3, 1)):
-        sent = jnp.stack([pick(rows, me ^ first), pick(rows, me ^ 2)])
-        held = jnp.stack([pick(rows, me), pick(rows, me ^ second)])
-        halves.append((permuted(sent, axis, lambda i, first=first: i ^ first), held, second))
-    first_round = [added(held, came).astype(BF16) for came, held, _ in halves]
-    done = []
-    for held, (_, _, second) in zip(first_round, halves):
-        came = permuted(held[1], axis, lambda i, second=second: i ^ second)
-        done.append(added(held[0], came).astype(BF16))
-    return jnp.concatenate(done), first_round
-
-
-def ring_of_rings_sum(value, axis, inner):
-    size, me = lax.axis_size(axis), lax.axis_index(axis)
-    outer = size // inner
-    value = value.reshape((outer, inner) + value.shape[1:])
-    low, high = me & (inner - 1), me >> (inner.bit_length() - 1)
-    came = [
-        permuted(
-            pick(value, (low + step) & (inner - 1), 1),
-            axis,
-            lambda i, step=step: i // inner * inner + (i + step) % inner,
-        )
-        for step in range(1, inner)
-    ]
-    value = added(pick(value, low, 1), *came).astype(BF16)
-    came = [
-        permuted(pick(value, (high + step) & (outer - 1)), axis, lambda i, step=step: (i + step * inner) % size)
-        for step in range(1, outer)
-    ]
-    return added(pick(value, high), *came)
+def doubling_gather(value, axis):
+    me = lax.axis_index(axis)
+    value = value[None]
+    for step in range(lax.axis_size(axis).bit_length() - 1):
+        came = permuted(value, axis, lambda i, step=step: i ^ (1 << step))
+        low = ((me >> step) & 1) == 0
+        value = jnp.concatenate([jnp.where(low, value, came), jnp.where(low, came, value)])
+    return value
 
 
 def exchange(value, axes=DP):
@@ -246,13 +210,8 @@
     groups = n_x * n_y * n_core
     dp_index, z_index = lax.axis_index(DP), lax.axis_index("z")
     indices = jnp.arange(groups, dtype=jnp.int32)
-    source_of = jnp.sum(jnp.where(dest_device[None, :] == indices[:, None], indices[None, :], 0), axis=1)
-    own_source = jnp.sum(jnp.where(dest_device == dp_index, indices, 0))
-    own_lengths = lax.dynamic_slice_in_dim(moved_lengths, dp_index * n_z + z_index, 1, 0)
-    recv_lengths = lax.dynamic_slice_in_dim(moved_lengths, own_source * n_z + z_index, 1, 0)
     seg_col, seg_row = kept_segments.reshape(keep, 1), kept_segments
 
-    w_all = lax.all_gather(w_out, "z", axis=0, tiled=True)
     share_cols = 5 * width * (moved // GROUP_ROWS) // groups
     block = pl.pallas_call(
         functools.partial(pack_kernel, keep),
@@ -264,46 +223,60 @@
         cost_estimate=cost(0, 8 * width),
         name="pack",
     )(uvqk, grad_out)
-    uvqk, grad_out, block = lax.optimization_barrier((uvqk, grad_out, block))
+    uvqk, grad_out, dest_device, block = lax.optimization_barrier((uvqk, grad_out, dest_device, block))
     block = exchange(block)
 
-    block_cols = width // (n_core * n_x)
-    core_half = jax.ShapeDtypeStruct((n_x, width, block_cols), BF16)
-    mine, other = pl.pallas_call(
+    source_of = jnp.sum(jnp.where(dest_device[None, :] == indices[:, None], indices[None, :], 0), axis=1)
+    own_source = jnp.sum(jnp.where(dest_device == dp_index, indices, 0))
+    own_lengths = lax.dynamic_slice_in_dim(moved_lengths, dp_index * n_z + z_index, 1, 0)
+    recv_lengths = lax.dynamic_slice_in_dim(moved_lengths, own_source * n_z + z_index, 1, 0)
+    term = pl.pallas_call(
         functools.partial(term_kernel, keep),
-        out_shape=(core_half, core_half),
-        in_specs=[SMEM, SMEM, VMEM, VMEM, VMEM, VMEM],
-        out_specs=(VMEM, VMEM),
+        out_shape=jax.ShapeDtypeStruct((width, width), BF16),
+        in_specs=[SMEM, VMEM, VMEM, VMEM, VMEM],
+        out_specs=VMEM,
         scratch_shapes=[pltpu.VMEM((rows, width), BF16)],
         compiler_params=PARAMS,
         cost_estimate=cost(0, 8 * width),
         name="term",
-    )(lax.axis_index("core").reshape(1), own_lengths, uvqk, grad_out, seg_col, seg_row)
-    part = added(mine, permuted(other, "core", lambda i: i ^ 1)).astype(BF16)
-    part, first_round = ring_of_four_sum(part, "x")
-    own_rows = width // n_z
-    block = lax.optimization_barrier((block, first_round))[0]
-    block = block[source_of]
-    part, block = lax.optimization_barrier((part, block))
+    )(own_lengths, uvqk, grad_out, seg_col, seg_row)
+    x, core = lax.axis_index("x"), lax.axis_index("core")
+    block_cols = width // (n_core * n_x)
+    w_mine = lax.dynamic_slice_in_dim(w_out, (core * n_x + x) * block_cols, block_cols, 1)
+    w_mine, term = lax.optimization_barrier((w_mine, term))
+    w_mine = doubling_gather(w_mine, "z").reshape(width, block_cols)
+    part = lax.psum_scatter(term, "z", scatter_dimension=0, tiled=True)
+
+    block, w_mine = lax.optimization_barrier((block[source_of], w_mine))
     block = exchange(block)
-    part = ring_of_rings_sum(part.reshape(n_z, own_rows, block_cols), "z", min(4, n_z))
+    others = [permuted(w_mine, "x", lambda i, step=step: i ^ step) for step in range(1, n_x)]
+    w_mine = jnp.stack([w_mine, *others])
+    w_other = permuted(w_mine, "core", lambda i: i ^ 1)
+
+    tile_rows = width // n_z // 8
+    slot_cols = width * 8 // groups
     part = lax.optimization_barrier((part, block))[0]
-    part = exchange(part.reshape(n_y, own_rows // n_y, block_cols), "y")
-    part = (jnp.sum(part, axis=0) * (1.0 / (groups * n_z))).astype(BF16)
-    spread = exchange(jnp.broadcast_to(part[None], (groups,) + part.shape))
-    spread = spread.astype(F32).reshape(n_x, n_y, n_core, own_rows // n_y, block_cols)
-    grad_weight = spread.transpose(1, 3, 2, 0, 4).reshape(own_rows, width)
+    part = part.reshape(8, tile_rows, width // slot_cols, slot_cols).transpose(0, 2, 1, 3)
+    part = exchange(part.reshape(groups, tile_rows, slot_cols))
+    part = (jnp.sum(part.astype(F32), axis=0) * (1.0 / (groups * n_z))).astype(BF16)
+    spread = exchange(jnp.broadcast_to(part[None], (groups,) + part.shape)).astype(F32)
+    spread = spread.reshape(8, groups // 8, tile_rows, slot_cols).transpose(0, 2, 1, 3)
+    grad_weight = spread.reshape(width // n_z, width)
 
     grad_rows = pl.pallas_call(
         functools.partial(back_kernel, keep),
         out_shape=jax.ShapeDtypeStruct(uvqk.shape, BF16),
-        in_specs=[SMEM] + [VMEM] * 6,
+        in_specs=[SMEM, SMEM] + [VMEM] * 7,
         out_specs=VMEM,
-        scratch_shapes=[pltpu.VMEM((moved, 5 * width), BF16)],
+        scratch_shapes=[
+            pltpu.VMEM((moved, 5 * width), BF16),
+            pltpu.VMEM((rows, width), BF16),
+            pltpu.VMEM((rows, width), F32),
+        ],
         compiler_params=PARAMS,
         cost_estimate=cost(8 * rows * width * width, 8 * width * width),
         name="back",
-    )(recv_lengths, uvqk, grad_out, block, w_all, seg_col, seg_row)
+    )(jnp.stack([core, x]), recv_lengths, uvqk, grad_out, block, w_mine, w_other, seg_col, seg_row)
     return grad_rows, grad_weight
 
 

time: 166 us -> 179 us (1.078)
  the two profiles are of different devices: /device:TPU:1 before, /device:TPU:65 now
where the time goes in v4:
time: 179 us; the launch traced here: 178 us
  starting transfers between devices  93.3 us (52%)
  waiting for transfers between devices  45.5 us (25%)
  between operations  15 us (8%)
  Pallas kernels  11 us (6%)
  other arithmetic  7.86 us (4%)
  local copies, waits for them, and re-layouts  5.48 us (3%)
    all_to_all x4, starting transfers between devices, exchange(): return lax.all_to_all(value, axes, split_axis=0, concat_axis=0, tiled=True)  50.5 us
    ppermute x8, starting transfers between devices, permuted(): return lax.ppermute(value, axis, [(i, target(i)) for i in range(size)])  42.8 us
    ppermute x8, waiting for transfers between devices, permuted(): return lax.ppermute(value, axis, [(i, target(i)) for i in range(size)])  30.6 us
    all_to_all x4, waiting for transfers between devices, exchange(): return lax.all_to_all(value, axes, split_axis=0, concat_axis=0, tiled=True)  14.9 us
    pallas_call x1, Pallas kernels, local(): pl.pallas_call(functools.partial(back_kernel, keep), out_shape=jax.ShapeD...  6.33 us
  transfers between devices with their start and end apart: 13, of which 9 were waited for; matrix products, arithmetic and copies ran while one was open for 5% of the time, Pallas kernels for 5%

profile of v4, /device:TPU:65, one launch (start us, length us, event | category | flops | bytes accessed | tf_op | source)
XLA Modules:
  0.0 178.1 jit_solution(12551104031145349899)
XLA Ops:
  7.2 0.0 copy-start
  7.2 2.5 %pack.1 = bf16[64,16,640]{2,1,0:T(8,128)(2,1)} custom-call(bf16[192,4096]{1,0:T(8,128)(2,1)} %x_ref.3, bf16[192,1024]{1,0:T(8,128)(2,1)} %g_ref.3), custom_call_target="tpu_custom_call" | custom-call | bytes 8192 | tf_op jit(solution)/shard_map/pack/pallas_call | solution.py:216
  9.7 0.0 copy-start.6
  9.7 0.0 copy-start.4
  9.7 0.0 copy-start.1
  9.7 10.9 %all-to-all-start = ((bf16[64,16,640]{2,1,0:T(8,128)(2,1)}), bf16[64,16,640]{2,1,0:T(8,128)(2,1)S(1)}, u32[]{:S(2)}, u32[]{:S(2)}) async-start(bf16[64,16,640]{2,1,0:T(8,128)(2,1)} %pack.1), calls=%async_computation | async-start | bytes 2621440 | tf_op jit(solution)/shard_map/all_to_all | solution.py:202
  20.7 0.0 reduce-scatter.2.cloned.1.call-start
  20.7 0.6 fusion
  22.0 0.1 copy.14.seg_col_ref
  22.1 0.8 constant_dynamic-slice_fusion
  22.9 0.1 copy.17.lengths_ref
  23.0 2.1 %term.1 = bf16[1024,1024]{1,0:T(8,128)(2,1)S(1)} custom-call(s32[1,3]{1,0:T(1,128)S(1)} %copy.17.lengths_ref, bf16[192,4096]{1,0:T(8,128)(2,1)S(1)} %copy-done.1, bf16[192,1024]{1,0:T(8,128)(2,1)S(1)} %copy-done.3, s32[64,1]{1,0:T(8,128)S(1)} %copy.14.seg_col_ref, s32[1,64]{1,0:T(1,128)S(1)} %copy-done.4), custom_call_target="tpu_custom_call" | custom-call | bytes 8192 | tf_op jit(solution)/shard_map/term/pallas_call | solution.py:233
  25.2 1.3 copy-done.2
  26.5 7.9 %collective-permute-start = (bf16[1,64,128]{2,1,0:T(8,128)(2,1)S(1)}, bf16[1,64,128]{2,1,0:T(8,128)(2,1)S(1)}, u32[]{:S(2)}, u32[]{:S(2)}) collective-permute-start(bf16[1,64,128]{2,1,0:T(8,128)(2,1)S(1)} %bitcast.35), channel_id=1, source_target_pairs={{0,1},{1,0},{2,3},{3,2},{4,5},{5,4},{6,7},{7,6},{8,9},{9,8},{10,11... | collective-permute-start | bytes 49160 | tf_op jit(solution)/shard_map/ppermute | solution.py:180
  34.4 0.0 reduce-scatter.2.cloned.1.call-update
  34.5 1.4 collective-permute-done
  35.9 1.9 %collective-permute-start.1 = (bf16[2,64,128]{2,1,0:T(8,128)(2,1)S(1)}, bf16[2,64,128]{2,1,0:T(8,128)(2,1)S(1)}, u32[]{:S(2)}, u32[]{:S(2)}) collective-permute-start(bf16[2,64,128]{2,1,0:T(8,128)(2,1)S(1)} %pad_maximum_fusion.4), channel_id=1, source_target_pairs={{0,2},{1,3},{2,0},{3,1},{4,6},{5,7},{6,4},{7,5},{8,10},{9,11},{10,... | collective-permute-start | bytes 98312 | tf_op jit(solution)/shard_map/ppermute | solution.py:180
  37.8 3.9 %collective-permute-done.1 = bf16[2,64,128]{2,1,0:T(8,128)(2,1)S(1)} collective-permute-done((bf16[2,64,128]{2,1,0:T(8,128)(2,1)S(1)}, bf16[2,64,128]{2,1,0:T(8,128)(2,1)S(1)}, u32[]{:S(2)}, u32[]{:S(2)}) %collective-permute-start.1) | collective-permute-done | bytes 32800 | tf_op jit(solution)/shard_map/ppermute | solution.py:180
  41.7 7.6 %collective-permute-start.2 = (bf16[4,64,128]{2,1,0:T(8,128)(2,1)S(1)}, bf16[4,64,128]{2,1,0:T(8,128)(2,1)S(1)}, u32[]{:S(2)}, u32[]{:S(2)}) collective-permute-start(bf16[4,64,128]{2,1,0:T(8,128)(2,1)S(1)} %pad_maximum_fusion.3), channel_id=1, source_target_pairs={{0,4},{1,5},{2,6},{3,7},{4,0},{5,1},{6,2},{7,3},{8,12},{9,13},{10,... | collective-permute-start | bytes 196616 | tf_op jit(solution)/shard_map/ppermute | solution.py:180
  49.4 0.1 select_reduce_fusion
  49.5 1.6 collective-permute-done.2
  51.1 0.6 copy-done.5
  51.8 0.7 pad_maximum_fusion.2
  52.4 13.4 %collective-permute-start.3 = (bf16[8,64,128]{2,1,0:T(8,128)(2,1)}, bf16[8,64,128]{2,1,0:T(8,128)(2,1)}, u32[]{:S(2)}, u32[]{:S(2)}) collective-permute-start(bf16[8,64,128]{2,1,0:T(8,128)(2,1)} %pad_maximum_fusion.2), channel_id=1, source_target_pairs={{0,8},{1,9},{2,10},{3,11},{4,12},{5,13},{6,14},{7,15},{8,0},{9,1},... | collective-permute-start | bytes 393224 | tf_op jit(solution)/shard_map/ppermute | solution.py:180
  65.9 4.2 %collective-permute-done.3 = bf16[8,64,128]{2,1,0:T(8,128)(2,1)} collective-permute-done((bf16[8,64,128]{2,1,0:T(8,128)(2,1)}, bf16[8,64,128]{2,1,0:T(8,128)(2,1)}, u32[]{:S(2)}, u32[]{:S(2)}) %collective-permute-start.3) | collective-permute-done | bytes 131104 | tf_op jit(solution)/shard_map/ppermute | solution.py:180
  70.1 0.9 broadcast_select_fusion.1
  71.1 0.7 pad_maximum_fusion.1
  71.8 1.8 gather_fusion
  73.5 23.5 %all-to-all-start.1 = ((bf16[64,16,640]{2,1,0:T(8,128)(2,1)}), bf16[64,16,640]{2,1,0:T(8,128)(2,1)S(1)}, u32[]{:S(2)}, u32[]{:S(2)}) async-start(bf16[64,16,640]{2,1,0:T(8,128)(2,1)} %gather_fusion), calls=%async_computation.1 | async-start | bytes 2621440 | tf_op jit(solution)/shard_map/all_to_all | solution.py:202
  97.1 4.7 %collective-permute-start.6 = (bf16[1024,128]{1,0:T(8,128)(2,1)}, bf16[1024,128]{1,0:T(8,128)(2,1)S(1)}, u32[]{:S(2)}, u32[]{:S(2)}) collective-permute-start(bf16[1024,128]{1,0:T(8,128)(2,1)} %bitcast.27), channel_id=1, source_target_pairs={{0,768},{256,512},{512,256},{768,0},{1,769},{257,513},{513,257},{7... | collective-permute-start | bytes 786440 | tf_op jit(solution)/shard_map/ppermute | solution.py:180
  101.8 2.3 %collective-permute-start.5 = (bf16[1024,128]{1,0:T(8,128)(2,1)}, bf16[1024,128]{1,0:T(8,128)(2,1)S(1)}, u32[]{:S(2)}, u32[]{:S(2)}) collective-permute-start(bf16[1024,128]{1,0:T(8,128)(2,1)} %bitcast.28), channel_id=1, source_target_pairs={{0,512},{256,768},{512,0},{768,256},{1,513},{257,769},{513,1},{769... | collective-permute-start | bytes 786440 | tf_op jit(solution)/shard_map/ppermute | solution.py:180
  104.1 2.1 %collective-permute-start.4 = (bf16[1024,128]{1,0:T(8,128)(2,1)}, bf16[1024,128]{1,0:T(8,128)(2,1)S(1)}, u32[]{:S(2)}, u32[]{:S(2)}) collective-permute-start(bf16[1024,128]{1,0:T(8,128)(2,1)} %bitcast.29), channel_id=1, source_target_pairs={{0,256},{256,0},{512,768},{768,512},{1,257},{257,1},{513,769},{769... | collective-permute-start | bytes 786440 | tf_op jit(solution)/shard_map/ppermute | solution.py:180
  106.2 15.6 %collective-permute-done.6 = bf16[1024,128]{1,0:T(8,128)(2,1)S(1)} collective-permute-done((bf16[1024,128]{1,0:T(8,128)(2,1)}, bf16[1024,128]{1,0:T(8,128)(2,1)S(1)}, u32[]{:S(2)}, u32[]{:S(2)}) %collective-permute-start.6) | collective-permute-done | bytes 262176 | tf_op jit(solution)/shard_map/ppermute | solution.py:180
  121.8 3.8 %collective-permute-done.4 = bf16[1024,128]{1,0:T(8,128)(2,1)S(1)} collective-permute-done((bf16[1024,128]{1,0:T(8,128)(2,1)}, bf16[1024,128]{1,0:T(8,128)(2,1)S(1)}, u32[]{:S(2)}, u32[]{:S(2)}) %collective-permute-start.4) | collective-permute-done | bytes 262176 | tf_op jit(solution)/shard_map/ppermute | solution.py:180
  125.7 2.0 %pad_maximum_fusion.w_mine_ref = bf16[4,1024,128]{2,1,0:T(8,128)(2,1)} fusion(bf16[1,1024,128]{2,1,0:T(8,128)(2,1)S(1)} %bitcast.31, bf16[1,1024,128]{2,1,0:T(8,128)(2,1)S(1)} %bitcast.32, bf16[1,1024,128]{2,1,0:T(8,128)(2,1)S(1)} %bitcast.33, bf16[1,1024,128]{2,1,0:T(8,128)(2,1)} %bitcast.30), kind=kLoop, calls=%fused_computation.1 | loop fusion | flops 1572864 | bytes 2097152 | tf_op jit(solution)/shard_map/stack | solution.py:253
  127.7 2.8 %collective-permute-start.7 = (bf16[4,1024,128]{2,1,0:T(8,128)(2,1)}, bf16[4,1024,128]{2,1,0:T(8,128)(2,1)}, u32[]{:S(2)}, u32[]{:S(2)}) collective-permute-start(bf16[4,1024,128]{2,1,0:T(8,128)(2,1)} %pad_maximum_fusion.w_mine_ref), channel_id=1, source_target_pairs={{0,16},{16,0},{1,17},{17,1},{2,18},{18,2},{3,19},{19,3},{4,20},{20... | collective-permute-start | bytes 3145736 | tf_op jit(solution)/shard_map/ppermute | solution.py:180
  130.5 0.0 reduce-scatter.2.cloned.1.call-done
  130.6 0.7 all-to-all-done.1.came_ref
  131.3 10.8 %all-to-all-start.2 = ((bf16[64,8,128]{2,1,0:T(8,128)(2,1)}), bf16[64,8,128]{2,1,0:T(8,128)(2,1)}, u32[]{:S(2)}, u32[]{:S(2)}) async-start(bf16[64,8,128]{2,1,0:T(8,128)(2,1)} %bitcast.34), calls=%async_computation.3 | async-start | bytes 262144 | tf_op jit(solution)/shard_map/all_to_all | solution.py:202
  142.0 0.1 copy.16.lengths_ref
  142.1 10.2 %all-to-all-done.2 = bf16[64,8,128]{2,1,0:T(8,128)(2,1)} async-done(((bf16[64,8,128]{2,1,0:T(8,128)(2,1)}), bf16[64,8,128]{2,1,0:T(8,128)(2,1)}, u32[]{:S(2)}, u32[]{:S(2)}) %all-to-all-start.2) | async-done | bytes 131104 | tf_op jit(solution)/shard_map/all_to_all | solution.py:202
  152.3 1.0 convert_reduce_fusion
  153.3 0.7 broadcast_in_dim.36
  154.0 5.2 %all-to-all-start.3 = ((bf16[64,8,128]{2,1,0:T(8,128)(2,1)}), bf16[64,8,128]{2,1,0:T(8,128)(2,1)}, u32[]{:S(2)}, u32[]{:S(2)}) async-start(bf16[64,8,128]{2,1,0:T(8,128)(2,1)} %broadcast_in_dim.36), calls=%async_computation.4 | async-start | bytes 262144 | tf_op jit(solution)/shard_map/all_to_all | solution.py:202
  159.2 0.1 pad_add_fusion.where_ref
  159.3 6.3 %back.1 = bf16[192,4096]{1,0:T(8,128)(2,1)} custom-call(s32[2]{0:T(128)S(1)} %pad_add_fusion.where_ref, s32[1,3]{1,0:T(1,128)S(1)} %copy.16.lengths_ref, bf16[192,4096]{1,0:T(8,128)(2,1)S(1)} %copy-done.1, bf16[192,1024]{1,0:T(8,128)(2,1)S(1)} %copy-done.3, bf16[64,16,640]{2,1,0:T(8,128)(2,1)S(1)} %all-to-all-done.1.came_ref, ...), custom_call_target="tpu_custom_call" | custom-call | flops 1610612736 | bytes 8388608 | tf_op jit(solution)/shard_map/back/pallas_call | solution.py:266
  165.6 4.0 %all-to-all-done.3 = bf16[64,8,128]{2,1,0:T(8,128)(2,1)} async-done(((bf16[64,8,128]{2,1,0:T(8,128)(2,1)}), bf16[64,8,128]{2,1,0:T(8,128)(2,1)}, u32[]{:S(2)}, u32[]{:S(2)}) %all-to-all-start.3) | async-done | bytes 131104 | tf_op jit(solution)/shard_map/all_to_all | solution.py:202
  169.6 1.6 convert_bitcast_fusion
  (20 shorter events, 0.1 us)
Async XLA Ops:
  7.2 19.3 %copy-start = (bf16[64,1024]{1,0:T(8,128)(2,1)S(1)}, bf16[64,1024]{1,0:T(8,128)(2,1)}, u32[]{:S(2)}) copy-start(bf16[64,1024]{1,0:T(8,128)(2,1)} %param.8) | copy-start | bytes 393220
  9.7 11.1 %copy-start.6 = (s32[64]{0:T(128)S(1)}, s32[64]{0:T(128)}, u32[]{:S(2)}) copy-start(s32[64]{0:T(128)} %param.11) | copy-start | bytes 772
  9.7 12.3 %copy-start.4 = (s32[1,64]{1,0:T(1,128)S(1)}, s32[1,64]{1,0:T(1,128)}, u32[]{:S(2)}) copy-start(s32[1,64]{1,0:T(1,128)} %seg_row_ref.3) | copy-start | bytes 772
  9.7 13.3 %copy-start.1 = (bf16[192,4096]{1,0:T(8,128)(2,1)S(1)}, bf16[192,4096]{1,0:T(8,128)(2,1)}, u32[]{:S(2)}) copy-start(bf16[192,4096]{1,0:T(8,128)(2,1)} %x_ref.3) | copy-start | bytes 4718596
  9.7 13.3 %copy-start.3 = (bf16[192,1024]{1,0:T(8,128)(2,1)S(1)}, bf16[192,1024]{1,0:T(8,128)(2,1)}, u32[]{:S(2)}) copy-start(bf16[192,1024]{1,0:T(8,128)(2,1)} %g_ref.3) | copy-start | bytes 1179652
  9.7 62.1 %all-to-all-start = ((bf16[64,16,640]{2,1,0:T(8,128)(2,1)}), bf16[64,16,640]{2,1,0:T(8,128)(2,1)S(1)}, u32[]{:S(2)}, u32[]{:S(2)}) async-start(bf16[64,16,640]{2,1,0:T(8,128)(2,1)} %pack.1), calls=%async_computation | async-start | bytes 2621440 | tf_op jit(solution)/shard_map/all_to_all | solution.py:202
  20.7 109.9 %reduce-scatter.2.cloned.1.call-start = ((), (), s32[]{:S(2)}) async-start(), calls=%async_computation.5 | async-start | bytes 2228224 | tf_op jit(solution)/shard_map/reduce_scatter | solution.py:248
  25.1 1.3 copy-start.2
  26.5 9.3 %collective-permute-start = (bf16[1,64,128]{2,1,0:T(8,128)(2,1)S(1)}, bf16[1,64,128]{2,1,0:T(8,128)(2,1)S(1)}, u32[]{:S(2)}, u32[]{:S(2)}) collective-permute-start(bf16[1,64,128]{2,1,0:T(8,128)(2,1)S(1)} %bitcast.35), channel_id=1, source_target_pairs={{0,1},{1,0},{2,3},{3,2},{4,5},{5,4},{6,7},{7,6},{8,9},{9,8},{10,11... | collective-permute-start | bytes 49160 | tf_op jit(solution)/shard_map/ppermute | solution.py:180
  35.9 5.9 %collective-permute-start.1 = (bf16[2,64,128]{2,1,0:T(8,128)(2,1)S(1)}, bf16[2,64,128]{2,1,0:T(8,128)(2,1)S(1)}, u32[]{:S(2)}, u32[]{:S(2)}) collective-permute-start(bf16[2,64,128]{2,1,0:T(8,128)(2,1)S(1)} %pad_maximum_fusion.4), channel_id=1, source_target_pairs={{0,2},{1,3},{2,0},{3,1},{4,6},{5,7},{6,4},{7,5},{8,10},{9,11},{10,... | collective-permute-start | bytes 98312 | tf_op jit(solution)/shard_map/ppermute | solution.py:180
  41.7 9.4 %collective-permute-start.2 = (bf16[4,64,128]{2,1,0:T(8,128)(2,1)S(1)}, bf16[4,64,128]{2,1,0:T(8,128)(2,1)S(1)}, u32[]{:S(2)}, u32[]{:S(2)}) collective-permute-start(bf16[4,64,128]{2,1,0:T(8,128)(2,1)S(1)} %pad_maximum_fusion.3), channel_id=1, source_target_pairs={{0,4},{1,5},{2,6},{3,7},{4,0},{5,1},{6,2},{7,3},{8,12},{9,13},{10,... | collective-permute-start | bytes 196616 | tf_op jit(solution)/shard_map/ppermute | solution.py:180
  51.1 0.6 copy-start.5
  52.4 17.7 %collective-permute-start.3 = (bf16[8,64,128]{2,1,0:T(8,128)(2,1)}, bf16[8,64,128]{2,1,0:T(8,128)(2,1)}, u32[]{:S(2)}, u32[]{:S(2)}) collective-permute-start(bf16[8,64,128]{2,1,0:T(8,128)(2,1)} %pad_maximum_fusion.2), channel_id=1, source_target_pairs={{0,8},{1,9},{2,10},{3,11},{4,12},{5,13},{6,14},{7,15},{8,0},{9,1},... | collective-permute-start | bytes 393224 | tf_op jit(solution)/shard_map/ppermute | solution.py:180
  73.5 57.7 %all-to-all-start.1 = ((bf16[64,16,640]{2,1,0:T(8,128)(2,1)}), bf16[64,16,640]{2,1,0:T(8,128)(2,1)S(1)}, u32[]{:S(2)}, u32[]{:S(2)}) async-start(bf16[64,16,640]{2,1,0:T(8,128)(2,1)} %gather_fusion), calls=%async_computation.1 | async-start | bytes 2621440 | tf_op jit(solution)/shard_map/all_to_all | solution.py:202
  97.1 24.7 %collective-permute-start.6 = (bf16[1024,128]{1,0:T(8,128)(2,1)}, bf16[1024,128]{1,0:T(8,128)(2,1)S(1)}, u32[]{:S(2)}, u32[]{:S(2)}) collective-permute-start(bf16[1024,128]{1,0:T(8,128)(2,1)} %bitcast.27), channel_id=1, source_target_pairs={{0,768},{256,512},{512,256},{768,0},{1,769},{257,513},{513,257},{7... | collective-permute-start | bytes 786440 | tf_op jit(solution)/shard_map/ppermute | solution.py:180
  101.8 20.0 %collective-permute-start.5 = (bf16[1024,128]{1,0:T(8,128)(2,1)}, bf16[1024,128]{1,0:T(8,128)(2,1)S(1)}, u32[]{:S(2)}, u32[]{:S(2)}) collective-permute-start(bf16[1024,128]{1,0:T(8,128)(2,1)} %bitcast.28), channel_id=1, source_target_pairs={{0,512},{256,768},{512,0},{768,256},{1,513},{257,769},{513,1},{769... | collective-permute-start | bytes 786440 | tf_op jit(solution)/shard_map/ppermute | solution.py:180
  104.1 21.6 %collective-permute-start.4 = (bf16[1024,128]{1,0:T(8,128)(2,1)}, bf16[1024,128]{1,0:T(8,128)(2,1)S(1)}, u32[]{:S(2)}, u32[]{:S(2)}) collective-permute-start(bf16[1024,128]{1,0:T(8,128)(2,1)} %bitcast.29), channel_id=1, source_target_pairs={{0,256},{256,0},{512,768},{768,512},{1,257},{257,1},{513,769},{769... | collective-permute-start | bytes 786440 | tf_op jit(solution)/shard_map/ppermute | solution.py:180
  127.7 31.6 %collective-permute-start.7 = (bf16[4,1024,128]{2,1,0:T(8,128)(2,1)}, bf16[4,1024,128]{2,1,0:T(8,128)(2,1)}, u32[]{:S(2)}, u32[]{:S(2)}) collective-permute-start(bf16[4,1024,128]{2,1,0:T(8,128)(2,1)} %pad_maximum_fusion.w_mine_ref), channel_id=1, source_target_pairs={{0,16},{16,0},{1,17},{17,1},{2,18},{18,2},{3,19},{19,3},{4,20},{20... | collective-permute-start | bytes 3145736 | tf_op jit(solution)/shard_map/ppermute | solution.py:180
  131.3 21.0 %all-to-all-start.2 = ((bf16[64,8,128]{2,1,0:T(8,128)(2,1)}), bf16[64,8,128]{2,1,0:T(8,128)(2,1)}, u32[]{:S(2)}, u32[]{:S(2)}) async-start(bf16[64,8,128]{2,1,0:T(8,128)(2,1)} %bitcast.34), calls=%async_computation.3 | async-start | bytes 262144 | tf_op jit(solution)/shard_map/all_to_all | solution.py:202
  154.0 15.6 %all-to-all-start.3 = ((bf16[64,8,128]{2,1,0:T(8,128)(2,1)}), bf16[64,8,128]{2,1,0:T(8,128)(2,1)}, u32[]{:S(2)}, u32[]{:S(2)}) async-start(bf16[64,8,128]{2,1,0:T(8,128)(2,1)} %broadcast_in_dim.36), calls=%async_computation.4 | async-start | bytes 262144 | tf_op jit(solution)/shard_map/all_to_all | solution.py:202
Sparse Core Ops, SparseCore 0:
  34.6 80.9 reduce-scatter.1

commit v5 on v3

--- a/solution.py
+++ b/solution.py
@@ -121,15 +121,13 @@
         ends.append(total)
     rows_of(pl.ds(keep, moved), *masks(segments_of(ends, (moved, 1), 0), segments_of(ends, (1, moved), 1)))
     rows_of(pl.ds(0, keep), *masks(seg_col_ref[...], seg_row_ref[...]))
-    blocks, _, block_cols = mine_ref.shape
-    joined = max(1, 256 // block_cols)
+    half_cols = mine_ref.shape[1]
     core = core_ref[0]
     for half, term_ref in ((core, mine_ref), (1 - core, other_ref)):
-        for b in range(0, blocks, joined):
-            start = pl.multiple_of((half * blocks + b) * block_cols, 128)
-            found = dot(g_ref[...], y_ref[:, pl.ds(start, joined * block_cols)], ((0,), (0,)))
-            for i in range(joined):
-                term_ref[b + i] = found[:, i * block_cols : (i + 1) * block_cols].astype(BF16)
+        for b in range(0, half_cols, 256):
+            start = pl.multiple_of(half * half_cols + b, 256)
+            found = dot(g_ref[...], y_ref[:, pl.ds(start, 256)], ((0,), (0,)))
+            term_ref[:, pl.ds(b, 256)] = found.astype(BF16)
 
 
 def back_kernel(keep, lengths_ref, x_ref, g_ref, came_ref, w_ref, seg_col_ref, seg_row_ref, out_ref, block_ref):
@@ -185,50 +183,18 @@
     return functools.reduce(jnp.add, [value.astype(F32) for value in values])
 
 
-def scatter_sum(value, axis):
-    size, me = lax.axis_size(axis), lax.axis_index(axis)
+def halving_round(value, axis, bit):
+    pairs = value.reshape((value.shape[0] // 2, 2) + value.shape[1:])
+    mine = (lax.axis_index(axis) >> bit) & 1
+    came = permuted(pick(pairs, 1 - mine, 1), axis, lambda i: i ^ (1 << bit))
+    return added(pick(pairs, mine, 1), came).astype(BF16)
+
+
+def direct_round(value, axis, stride):
+    size, outer = lax.axis_size(axis), value.shape[0]
+    high = lax.axis_index(axis) // stride
     came = [
-        permuted(pick(value, (me + step) & (size - 1)), axis, lambda i, step=step: (i + step) % size)
-        for step in range(1, size)
-    ]
-    return added(pick(value, me), *came).astype(BF16)
-
-
-def ring_of_four_sum(value, axis):
-    size, me = lax.axis_size(axis), lax.axis_index(axis)
-    if size != 4:
-        done = scatter_sum(value, axis)
-        return done, [done]
-    half = value.shape[1] // 2
-    halves = []
-    for rows, first, second in ((value[:, :half], 1, 3), (value[:, half:], 3, 1)):
-        sent = jnp.stack([pick(rows, me ^ first), pick(rows, me ^ 2)])
-        held = jnp.stack([pick(rows, me), pick(rows, me ^ second)])
-        halves.append((permuted(sent, axis, lambda i, first=first: i ^ first), held, second))
-    first_round = [added(held, came).astype(BF16) for came, held, _ in halves]
-    done = []
-    for held, (_, _, second) in zip(first_round, halves):
-        came = permuted(held[1], axis, lambda i, second=second: i ^ second)
-        done.append(added(held[0], came).astype(BF16))
-    return jnp.concatenate(done), first_round
-
-
-def ring_of_rings_sum(value, axis, inner):
-    size, me = lax.axis_size(axis), lax.axis_index(axis)
-    outer = size // inner
-    value = value.reshape((outer, inner) + value.shape[1:])
-    low, high = me & (inner - 1), me >> (inner.bit_length() - 1)
-    came = [
-        permuted(
-            pick(value, (low + step) & (inner - 1), 1),
-            axis,
-            lambda i, step=step: i // inner * inner + (i + step) % inner,
-        )
-        for step in range(1, inner)
-    ]
-    value = added(pick(value, low, 1), *came).astype(BF16)
-    came = [
-        permuted(pick(value, (high + step) & (outer - 1)), axis, lambda i, step=step: (i + step * inner) % size)
+        permuted(pick(value, (high + step) & (outer - 1)), axis, lambda i, step=step: (i + step * stride) % size)
         for step in range(1, outer)
     ]
     return added(pick(value, high), *came)
@@ -246,10 +212,6 @@
     groups = n_x * n_y * n_core
     dp_index, z_index = lax.axis_index(DP), lax.axis_index("z")
     indices = jnp.arange(groups, dtype=jnp.int32)
-    source_of = jnp.sum(jnp.where(dest_device[None, :] == indices[:, None], indices[None, :], 0), axis=1)
-    own_source = jnp.sum(jnp.where(dest_device == dp_index, indices, 0))
-    own_lengths = lax.dynamic_slice_in_dim(moved_lengths, dp_index * n_z + z_index, 1, 0)
-    recv_lengths = lax.dynamic_slice_in_dim(moved_lengths, own_source * n_z + z_index, 1, 0)
     seg_col, seg_row = kept_segments.reshape(keep, 1), kept_segments
 
     w_all = lax.all_gather(w_out, "z", axis=0, tiled=True)
@@ -264,11 +226,15 @@
         cost_estimate=cost(0, 8 * width),
         name="pack",
     )(uvqk, grad_out)
-    uvqk, grad_out, block = lax.optimization_barrier((uvqk, grad_out, block))
+    uvqk, grad_out, dest_device, block = lax.optimization_barrier((uvqk, grad_out, dest_device, block))
     block = exchange(block)
 
-    block_cols = width // (n_core * n_x)
-    core_half = jax.ShapeDtypeStruct((n_x, width, block_cols), BF16)
+    source_of = jnp.sum(jnp.where(dest_device[None, :] == indices[:, None], indices[None, :], 0), axis=1)
+    own_source = jnp.sum(jnp.where(dest_device == dp_index, indices, 0))
+    own_lengths = lax.dynamic_slice_in_dim(moved_lengths, dp_index * n_z + z_index, 1, 0)
+    recv_lengths = lax.dynamic_slice_in_dim(moved_lengths, own_source * n_z + z_index, 1, 0)
+    half_cols = width // n_core
+    core_half = jax.ShapeDtypeStruct((width, half_cols), BF16)
     mine, other = pl.pallas_call(
         functools.partial(term_kernel, keep),
         out_shape=(core_half, core_half),
@@ -280,19 +246,25 @@
         name="term",
     )(lax.axis_index("core").reshape(1), own_lengths, uvqk, grad_out, seg_col, seg_row)
     part = added(mine, permuted(other, "core", lambda i: i ^ 1)).astype(BF16)
-    part, first_round = ring_of_four_sum(part, "x")
     own_rows = width // n_z
-    block = lax.optimization_barrier((block, first_round))[0]
-    block = block[source_of]
-    part, block = lax.optimization_barrier((part, block))
-    block = exchange(block)
-    part = ring_of_rings_sum(part.reshape(n_z, own_rows, block_cols), "z", min(4, n_z))
+    part = halving_round(part.reshape(n_z, own_rows, half_cols), "z", 0)
+    block = lax.optimization_barrier((block, part))[0]
+    block = exchange(block[source_of])
+    stride = 2
+    if part.shape[0] > 4:
+        part, stride = halving_round(part, "z", 1), 4
+    part = direct_round(part, "z", stride)
+
     part = lax.optimization_barrier((part, block))[0]
-    part = exchange(part.reshape(n_y, own_rows // n_y, block_cols), "y")
-    part = (jnp.sum(part, axis=0) * (1.0 / (groups * n_z))).astype(BF16)
-    spread = exchange(jnp.broadcast_to(part[None], (groups,) + part.shape))
-    spread = spread.astype(F32).reshape(n_x, n_y, n_core, own_rows // n_y, block_cols)
-    grad_weight = spread.transpose(1, 3, 2, 0, 4).reshape(own_rows, width)
+    col_blocks = half_cols // 128
+    row_blocks = n_x * n_y // col_blocks
+    tile_rows = own_rows // row_blocks
+    part = part.astype(BF16).reshape(row_blocks, tile_rows, col_blocks, 128).transpose(0, 2, 1, 3)
+    part = exchange(part.reshape(n_x * n_y, tile_rows, 128), ("x", "y"))
+    part = (jnp.sum(part.astype(F32), axis=0) * (1.0 / (groups * n_z))).astype(BF16)
+    spread = exchange(jnp.broadcast_to(part[None], (groups,) + part.shape)).astype(F32)
+    spread = spread.reshape(row_blocks, col_blocks, n_core, tile_rows, 128)
+    grad_weight = spread.transpose(0, 3, 2, 1, 4).reshape(own_rows, width)
 
     grad_rows = pl.pallas_call(
         functools.partial(back_kernel, keep),

time: 166 us -> 177 us (1.066)
  waiting for transfers between devices: 27.9 us -> 52 us
  starting transfers between devices: 83.6 us -> 61.5 us
  blocking collectives: 13.6 us -> 19.8 us
  local copies, waits for them, and re-layouts: 8.95 us -> 11.2 us
    ppermute x11 -> x6, starting transfers between devices: 61.3 us -> 29.1 us  [permuted(): return lax.ppermute(value, axis, [(i, target(i)) for i in range(size)])]
    ppermute x11 -> x6, waiting for transfers between devices: 21.2 us -> 44.5 us  [permuted(): return lax.ppermute(value, axis, [(i, target(i)) for i in range(size)])]
    all_to_all x3, starting transfers between devices: 22.3 us -> 32.4 us  [exchange(): return lax.all_to_all(value, axes, split_axis=0, concat_axis=0, tiled=True)]
    all_to_all x1, blocking collectives: 13.6 us -> 19.8 us  [exchange(): return lax.all_to_all(value, axes, split_axis=0, concat_axis=0, tiled=True)]
    convert_element_type x6 -> x3, other arithmetic: 1.15 us -> 3.13 us  [the longest x2 3.13 us: halving_round(): return added(pick(pairs, mine, 1), came).astype(BF16)]
  transfers between devices with their start and end apart: 15 -> 10, of which waited for: 8 -> 7; matrix products, arithmetic and copies ran while one was open for 6% -> 8% of each run, Pallas kernels for 3% -> 5%
where the time goes in v5:
time: 177 us
  starting transfers between devices  61.5 us (35%)
  waiting for transfers between devices  52 us (29%)
  blocking collectives  19.8 us (11%)
  between operations  14.9 us (8%)
  local copies, waits for them, and re-layouts  11.2 us (6%)
  Pallas kernels  10.6 us (6%)
  other arithmetic  6.45 us (4%)
    ppermute x6, waiting for transfers between devices, permuted(): return lax.ppermute(value, axis, [(i, target(i)) for i in range(size)])  44.5 us
    all_to_all x3, starting transfers between devices, exchange(): return lax.all_to_all(value, axes, split_axis=0, concat_axis=0, tiled=True)  32.4 us
    ppermute x6, starting transfers between devices, permuted(): return lax.ppermute(value, axis, [(i, target(i)) for i in range(size)])  29.1 us
    all_to_all x1, blocking collectives, exchange(): return lax.all_to_all(value, axes, split_axis=0, concat_axis=0, tiled=True)  19.8 us
    all_to_all x3, waiting for transfers between devices, exchange(): return lax.all_to_all(value, axes, split_axis=0, concat_axis=0, tiled=True)  7.51 us
    pallas_call x1, Pallas kernels, local(): pl.pallas_call(functools.partial(back_kernel, keep), out_shape=jax.ShapeD...  5.03 us
  transfers between devices with their start and end apart: 10, of which 7 were waited for; matrix products, arithmetic and copies ran while one was open for 8% of the time, Pallas kernels for 5%

profile of v5, /device:TPU:1, one launch (start us, length us, event | category | flops | bytes accessed | tf_op | source)
XLA Modules:
  0.0 176.5 jit_solution(3137775367575770423)
XLA Ops:
  7.2 2.4 %pack.1 = bf16[64,16,640]{2,1,0:T(8,128)(2,1)} custom-call(bf16[192,4096]{1,0:T(8,128)(2,1)} %x_ref.3, bf16[192,1024]{1,0:T(8,128)(2,1)} %g_ref.3), custom_call_target="tpu_custom_call" | custom-call | bytes 8192 | tf_op jit(solution)/shard_map/pack/pallas_call | solution.py:219
  9.6 0.0 copy-start.6
  9.6 0.0 copy-start.3
  9.6 0.0 copy-start
  9.7 0.0 copy-start.1
  9.7 19.2 %all-to-all-start = ((bf16[64,16,640]{2,1,0:T(8,128)(2,1)}), bf16[64,16,640]{2,1,0:T(8,128)(2,1)}, u32[]{:S(2)}, u32[]{:S(2)}) async-start(bf16[64,16,640]{2,1,0:T(8,128)(2,1)} %pack.1), calls=%async_computation | async-start | bytes 2621440 | tf_op jit(solution)/shard_map/all_to_all | solution.py:204
  28.8 0.0 all-gather.2.cloned.1.call-start
  28.9 0.7 fusion.4
  30.2 0.8 constant_dynamic-slice_fusion
  31.0 0.1 copy.27.lengths_ref
  31.1 0.0 copy-done.3
  31.1 0.1 copy.23.seg_col_ref
  31.2 3.1 %term.1 = (bf16[1024,512]{1,0:T(8,128)(2,1)S(1)}, bf16[1024,512]{1,0:T(8,128)(2,1)}) custom-call(s32[1]{0:T(128)} %bitcast.core_ref, s32[1,3]{1,0:T(1,128)S(1)} %copy.27.lengths_ref, bf16[192,4096]{1,0:T(8,128)(2,1)S(1)} %copy-done, bf16[192,1024]{1,0:T(8,128)(2,1)S(1)} %copy-done.1, s32[64,1]{1,0:T(8,128)S(1)} %copy.23.seg_col_ref, s32[1,64]{1,0:T(1,128)S(1)} %copy-done.3), custom_call_target="tpu_custom_call" | custom-call | bytes 8192 | tf_op jit(solution)/shard_map/term/pallas_call | solution.py:238
  34.3 2.5 %collective-permute-start = (bf16[1024,512]{1,0:T(8,128)(2,1)}, bf16[1024,512]{1,0:T(8,128)(2,1)}, u32[]{:S(2)}, u32[]{:S(2)}) collective-permute-start(bf16[1024,512]{1,0:T(8,128)(2,1)} %get-tuple-element.15), channel_id=1, source_target_pairs={{0,16},{16,0},{1,17},{17,1},{2,18},{18,2},{3,19},{19,3},{4,20},{20... | collective-permute-start | bytes 3145736 | tf_op jit(solution)/shard_map/ppermute | solution.py:175
  36.9 0.0 all-gather.2.cloned.1.call-update
  36.9 2.6 %collective-permute-done = bf16[1024,512]{1,0:T(8,128)(2,1)} collective-permute-done((bf16[1024,512]{1,0:T(8,128)(2,1)}, bf16[1024,512]{1,0:T(8,128)(2,1)}, u32[]{:S(2)}, u32[]{:S(2)}) %collective-permute-start) | collective-permute-done | bytes 1048608 | tf_op jit(solution)/shard_map/ppermute | solution.py:175
  39.5 1.6 add_convert_fusion
  41.1 1.0 copy-done.4
  42.1 1.9 %collective-permute-start.1 = (bf16[8,64,512]{2,1,0:T(8,128)(2,1)S(1)}, bf16[8,64,512]{2,1,0:T(8,128)(2,1)S(1)}, u32[]{:S(2)}, u32[]{:S(2)}) collective-permute-start(bf16[8,64,512]{2,1,0:T(8,128)(2,1)S(1)} %dynamic-slice_bitcast_fusion), channel_id=1, source_target_pairs={{0,1},{1,0},{2,3},{3,2},{4,5},{5,4},{6,7},{7,6},{8,9},{9,8},{10,11... | collective-permute-start | bytes 1572872 | tf_op jit(solution)/shard_map/ppermute | solution.py:175
  44.0 0.1 select_reduce_fusion
  44.1 13.1 %collective-permute-done.1 = bf16[8,64,512]{2,1,0:T(8,128)(2,1)S(1)} collective-permute-done((bf16[8,64,512]{2,1,0:T(8,128)(2,1)S(1)}, bf16[8,64,512]{2,1,0:T(8,128)(2,1)S(1)}, u32[]{:S(2)}, u32[]{:S(2)}) %collective-permute-start.1) | collective-permute-done | bytes 524320 | tf_op jit(solution)/shard_map/ppermute | solution.py:175
  57.2 2.0 %fusion = bf16[8,64,512]{2,1,0:T(8,128)(2,1)} fusion(bf16[8,64,512]{2,1,0:T(8,128)(2,1)S(1)} %collective-permute-done.1, bf16[8,2,64,512]{3,2,1,0:T(8,128)(2,1)} %bitcast.39, s32[]{:T(128)S(6)} %select_n.59), kind=kLoop, calls=%fused_computation.3 | loop fusion | flops 1048576 | bytes 1572868 | tf_op jit(solution)/shard_map/convert_element_type | solution.py:190
  59.2 3.7 %all-to-all-done = bf16[64,16,640]{2,1,0:T(8,128)(2,1)} async-done(((bf16[64,16,640]{2,1,0:T(8,128)(2,1)}), bf16[64,16,640]{2,1,0:T(8,128)(2,1)}, u32[]{:S(2)}, u32[]{:S(2)}) %all-to-all-start) | async-done | bytes 1310752 | tf_op jit(solution)/shard_map/all_to_all | solution.py:204
  63.0 3.1 %gather_fusion = bf16[64,16,640]{2,1,0:T(8,128)(2,1)} fusion(bf16[64,16,640]{2,1,0:T(8,128)(2,1)} %all-to-all-done, s32[1024]{0:T(1024)S(1)} %pad_clamp_fusion), kind=kCustom, calls=%fused_computation | custom fusion | bytes 2621696 | tf_op jit(solution)/shard_map/gather | solution.py:252
  66.1 7.2 %all-to-all-start.1 = ((bf16[64,16,640]{2,1,0:T(8,128)(2,1)}), bf16[64,16,640]{2,1,0:T(8,128)(2,1)S(1)}, u32[]{:S(2)}, u32[]{:S(2)}) async-start(bf16[64,16,640]{2,1,0:T(8,128)(2,1)} %gather_fusion), calls=%async_computation.1 | async-start | bytes 2621440 | tf_op jit(solution)/shard_map/all_to_all | solution.py:204
  73.3 1.7 dynamic-slice_bitcast_fusion.1
  75.0 1.9 %collective-permute-start.2 = (bf16[4,64,512]{2,1,0:T(8,128)(2,1)}, bf16[4,64,512]{2,1,0:T(8,128)(2,1)}, u32[]{:S(2)}, u32[]{:S(2)}) collective-permute-start(bf16[4,64,512]{2,1,0:T(8,128)(2,1)} %dynamic-slice_bitcast_fusion.1), channel_id=1, source_target_pairs={{0,2},{1,3},{2,0},{3,1},{4,6},{5,7},{6,4},{7,5},{8,10},{9,11},{10,... | collective-permute-start | bytes 786440 | tf_op jit(solution)/shard_map/ppermute | solution.py:175
  76.9 19.1 %collective-permute-done.2 = bf16[4,64,512]{2,1,0:T(8,128)(2,1)} collective-permute-done((bf16[4,64,512]{2,1,0:T(8,128)(2,1)}, bf16[4,64,512]{2,1,0:T(8,128)(2,1)}, u32[]{:S(2)}, u32[]{:S(2)}) %collective-permute-start.2) | collective-permute-done | bytes 262176 | tf_op jit(solution)/shard_map/ppermute | solution.py:175
  96.0 1.1 fusion.1
  97.1 0.0 copy-start.5
  97.2 0.7 copy-done.5
  97.8 0.7 dynamic-slice_bitcast_fusion.4
  98.5 6.3 %collective-permute-start.3 = (bf16[64,512]{1,0:T(8,128)(2,1)}, bf16[64,512]{1,0:T(8,128)(2,1)S(1)}, u32[]{:S(2)}, u32[]{:S(2)}) collective-permute-start(bf16[64,512]{1,0:T(8,128)(2,1)} %get-tuple-element.18), channel_id=1, source_target_pairs={{0,4},{1,5},{2,6},{3,7},{4,8},{5,9},{6,10},{7,11},{8,12},{9,13},{1... | collective-permute-start | bytes 196616 | tf_op jit(solution)/shard_map/ppermute | solution.py:175
  104.8 13.9 %collective-permute-start.4 = (bf16[64,512]{1,0:T(8,128)(2,1)}, bf16[64,512]{1,0:T(8,128)(2,1)S(1)}, u32[]{:S(2)}, u32[]{:S(2)}) collective-permute-start(bf16[64,512]{1,0:T(8,128)(2,1)} %get-tuple-element.20), channel_id=1, source_target_pairs={{0,8},{1,9},{2,10},{3,11},{4,12},{5,13},{6,14},{7,15},{8,0},{9,1},... | collective-permute-start | bytes 196616 | tf_op jit(solution)/shard_map/ppermute | solution.py:175
  118.7 2.5 %collective-permute-start.5 = (bf16[64,512]{1,0:T(8,128)(2,1)S(1)}, bf16[64,512]{1,0:T(8,128)(2,1)}, u32[]{:S(2)}, u32[]{:S(2)}) collective-permute-start(bf16[64,512]{1,0:T(8,128)(2,1)S(1)} %get-tuple-element.19), channel_id=1, source_target_pairs={{0,12},{1,13},{2,14},{3,15},{4,0},{5,1},{6,2},{7,3},{8,4},{9,5},{1... | collective-permute-start | bytes 196616 | tf_op jit(solution)/shard_map/ppermute | solution.py:175
  121.3 0.0 collective-permute-done.3
  121.3 5.9 %collective-permute-done.4 = bf16[64,512]{1,0:T(8,128)(2,1)S(1)} collective-permute-done((bf16[64,512]{1,0:T(8,128)(2,1)}, bf16[64,512]{1,0:T(8,128)(2,1)S(1)}, u32[]{:S(2)}, u32[]{:S(2)}) %collective-permute-start.4) | collective-permute-done | bytes 65568 | tf_op jit(solution)/shard_map/ppermute | solution.py:175
  127.2 3.8 %collective-permute-done.5 = bf16[64,512]{1,0:T(8,128)(2,1)} collective-permute-done((bf16[64,512]{1,0:T(8,128)(2,1)S(1)}, bf16[64,512]{1,0:T(8,128)(2,1)}, u32[]{:S(2)}, u32[]{:S(2)}) %collective-permute-start.5) | collective-permute-done | bytes 65568 | tf_op jit(solution)/shard_map/ppermute | solution.py:175
  131.0 0.9 fusion.3
  131.9 0.0 all-to-all-done.1.came_ref
  131.9 19.8 %all_to_all.20 = bf16[32,8,128]{2,1,0:T(8,128)(2,1)S(1)} all-to-all(bf16[32,8,128]{2,1,0:T(8,128)(2,1)S(1)} %bitcast.43), channel_id=1, replica_groups=mesh['x'=4,'y'=8,'core'=2,'z'=16] {'x','y'}, dimensions={0} | all-to-all | bytes 131072 | tf_op jit(solution)/shard_map/all_to_all | solution.py:204
  151.8 0.7 broadcast_in_dim.32
  152.4 6.0 %all-to-all-start.3 = ((bf16[64,8,128]{2,1,0:T(8,128)(2,1)}), bf16[64,8,128]{2,1,0:T(8,128)(2,1)S(1)}, u32[]{:S(2)}, u32[]{:S(2)}) async-start(bf16[64,8,128]{2,1,0:T(8,128)(2,1)} %broadcast_in_dim.32), calls=%async_computation.3 | async-start | bytes 262144 | tf_op jit(solution)/shard_map/all_to_all | solution.py:204
  158.4 0.1 copy.26.lengths_ref
  158.5 1.6 copy-done.2
  160.1 5.0 %back.1 = bf16[192,4096]{1,0:T(8,128)(2,1)} custom-call(s32[1,3]{1,0:T(1,128)S(1)} %copy.26.lengths_ref, bf16[192,4096]{1,0:T(8,128)(2,1)S(1)} %copy-done, bf16[192,1024]{1,0:T(8,128)(2,1)S(1)} %copy-done.1, bf16[64,16,640]{2,1,0:T(8,128)(2,1)S(1)} %all-to-all-done.1.came_ref, bf16[1024,1024]{1,0:T(8,128)(2,1)S(1)} %copy-done.2, ...), custom_call_target="tpu_custom_call" | custom-call | flops 1610612736 | bytes 8388608 | tf_op jit(solution)/shard_map/back/pallas_call | solution.py:269
  165.1 3.8 %all-to-all-done.3 = bf16[64,8,128]{2,1,0:T(8,128)(2,1)S(1)} async-done(((bf16[64,8,128]{2,1,0:T(8,128)(2,1)}), bf16[64,8,128]{2,1,0:T(8,128)(2,1)S(1)}, u32[]{:S(2)}, u32[]{:S(2)}) %all-to-all-start.3) | async-done | bytes 131104 | tf_op jit(solution)/shard_map/all_to_all | solution.py:204
  168.9 0.7 copy.25
  (12 shorter events, 0.1 us)
Async XLA Ops:
  9.6 19.3 %copy-start.6 = (s32[64]{0:T(128)S(1)}, s32[64]{0:T(128)}, u32[]{:S(2)}) copy-start(s32[64]{0:T(128)} %param.11) | copy-start | bytes 772
  9.6 21.5 %copy-start.3 = (s32[1,64]{1,0:T(1,128)S(1)}, s32[1,64]{1,0:T(1,128)}, u32[]{:S(2)}) copy-start(s32[1,64]{1,0:T(1,128)} %seg_row_ref.3) | copy-start | bytes 772
  9.6 21.5 %copy-start = (bf16[192,4096]{1,0:T(8,128)(2,1)S(1)}, bf16[192,4096]{1,0:T(8,128)(2,1)}, u32[]{:S(2)}) copy-start(bf16[192,4096]{1,0:T(8,128)(2,1)} %x_ref.3) | copy-start | bytes 4718596
  9.7 21.5 %copy-start.1 = (bf16[192,1024]{1,0:T(8,128)(2,1)S(1)}, bf16[192,1024]{1,0:T(8,128)(2,1)}, u32[]{:S(2)}) copy-start(bf16[192,1024]{1,0:T(8,128)(2,1)} %g_ref.3) | copy-start | bytes 1179652
  9.7 53.3 %all-to-all-start = ((bf16[64,16,640]{2,1,0:T(8,128)(2,1)}), bf16[64,16,640]{2,1,0:T(8,128)(2,1)}, u32[]{:S(2)}, u32[]{:S(2)}) async-start(bf16[64,16,640]{2,1,0:T(8,128)(2,1)} %pack.1), calls=%async_computation | async-start | bytes 2621440 | tf_op jit(solution)/shard_map/all_to_all | solution.py:204
  28.8 129.7 %all-gather.2.cloned.1.call-start = ((), (), s32[]{:S(2)}) async-start(), calls=%async_computation.4 | async-start | bytes 2228224 | tf_op jit(solution)/shard_map/all_gather | solution.py:217
  34.3 5.1 %collective-permute-start = (bf16[1024,512]{1,0:T(8,128)(2,1)}, bf16[1024,512]{1,0:T(8,128)(2,1)}, u32[]{:S(2)}, u32[]{:S(2)}) collective-permute-start(bf16[1024,512]{1,0:T(8,128)(2,1)} %get-tuple-element.15), channel_id=1, source_target_pairs={{0,16},{16,0},{1,17},{17,1},{2,18},{18,2},{3,19},{19,3},{4,20},{20... | collective-permute-start | bytes 3145736 | tf_op jit(solution)/shard_map/ppermute | solution.py:175
  41.0 1.0 copy-start.4
  42.1 15.1 %collective-permute-start.1 = (bf16[8,64,512]{2,1,0:T(8,128)(2,1)S(1)}, bf16[8,64,512]{2,1,0:T(8,128)(2,1)S(1)}, u32[]{:S(2)}, u32[]{:S(2)}) collective-permute-start(bf16[8,64,512]{2,1,0:T(8,128)(2,1)S(1)} %dynamic-slice_bitcast_fusion), channel_id=1, source_target_pairs={{0,1},{1,0},{2,3},{3,2},{4,5},{5,4},{6,7},{7,6},{8,9},{9,8},{10,11... | collective-permute-start | bytes 1572872 | tf_op jit(solution)/shard_map/ppermute | solution.py:175
  66.1 65.9 %all-to-all-start.1 = ((bf16[64,16,640]{2,1,0:T(8,128)(2,1)}), bf16[64,16,640]{2,1,0:T(8,128)(2,1)S(1)}, u32[]{:S(2)}, u32[]{:S(2)}) async-start(bf16[64,16,640]{2,1,0:T(8,128)(2,1)} %gather_fusion), calls=%async_computation.1 | async-start | bytes 2621440 | tf_op jit(solution)/shard_map/all_to_all | solution.py:204
  75.0 21.1 %collective-permute-start.2 = (bf16[4,64,512]{2,1,0:T(8,128)(2,1)}, bf16[4,64,512]{2,1,0:T(8,128)(2,1)}, u32[]{:S(2)}, u32[]{:S(2)}) collective-permute-start(bf16[4,64,512]{2,1,0:T(8,128)(2,1)} %dynamic-slice_bitcast_fusion.1), channel_id=1, source_target_pairs={{0,2},{1,3},{2,0},{3,1},{4,6},{5,7},{6,4},{7,5},{8,10},{9,11},{10,... | collective-permute-start | bytes 786440 | tf_op jit(solution)/shard_map/ppermute | solution.py:175
  97.1 0.7 copy-start.5
  98.5 22.8 %collective-permute-start.3 = (bf16[64,512]{1,0:T(8,128)(2,1)}, bf16[64,512]{1,0:T(8,128)(2,1)S(1)}, u32[]{:S(2)}, u32[]{:S(2)}) collective-permute-start(bf16[64,512]{1,0:T(8,128)(2,1)} %get-tuple-element.18), channel_id=1, source_target_pairs={{0,4},{1,5},{2,6},{3,7},{4,8},{5,9},{6,10},{7,11},{8,12},{9,13},{1... | collective-permute-start | bytes 196616 | tf_op jit(solution)/shard_map/ppermute | solution.py:175
  104.8 22.3 %collective-permute-start.4 = (bf16[64,512]{1,0:T(8,128)(2,1)}, bf16[64,512]{1,0:T(8,128)(2,1)S(1)}, u32[]{:S(2)}, u32[]{:S(2)}) collective-permute-start(bf16[64,512]{1,0:T(8,128)(2,1)} %get-tuple-element.20), channel_id=1, source_target_pairs={{0,8},{1,9},{2,10},{3,11},{4,12},{5,13},{6,14},{7,15},{8,0},{9,1},... | collective-permute-start | bytes 196616 | tf_op jit(solution)/shard_map/ppermute | solution.py:175
  118.7 12.3 %collective-permute-start.5 = (bf16[64,512]{1,0:T(8,128)(2,1)S(1)}, bf16[64,512]{1,0:T(8,128)(2,1)}, u32[]{:S(2)}, u32[]{:S(2)}) collective-permute-start(bf16[64,512]{1,0:T(8,128)(2,1)S(1)} %get-tuple-element.19), channel_id=1, source_target_pairs={{0,12},{1,13},{2,14},{3,15},{4,0},{5,1},{6,2},{7,3},{8,4},{9,5},{1... | collective-permute-start | bytes 196616 | tf_op jit(solution)/shard_map/ppermute | solution.py:175
  152.4 16.5 %all-to-all-start.3 = ((bf16[64,8,128]{2,1,0:T(8,128)(2,1)}), bf16[64,8,128]{2,1,0:T(8,128)(2,1)S(1)}, u32[]{:S(2)}, u32[]{:S(2)}) async-start(bf16[64,8,128]{2,1,0:T(8,128)(2,1)} %broadcast_in_dim.32), calls=%async_computation.3 | async-start | bytes 262144 | tf_op jit(solution)/shard_map/all_to_all | solution.py:204
  158.5 1.6 copy-start.2
Sparse Core Ops, SparseCore 0:
  37.0 75.8 all-gather.1

commit v6 on v3

--- a/solution.py
+++ b/solution.py
@@ -194,25 +194,6 @@
     return added(pick(value, me), *came).astype(BF16)
 
 
-def ring_of_four_sum(value, axis):
-    size, me = lax.axis_size(axis), lax.axis_index(axis)
-    if size != 4:
-        done = scatter_sum(value, axis)
-        return done, [done]
-    half = value.shape[1] // 2
-    halves = []
-    for rows, first, second in ((value[:, :half], 1, 3), (value[:, half:], 3, 1)):
-        sent = jnp.stack([pick(rows, me ^ first), pick(rows, me ^ 2)])
-        held = jnp.stack([pick(rows, me), pick(rows, me ^ second)])
-        halves.append((permuted(sent, axis, lambda i, first=first: i ^ first), held, second))
-    first_round = [added(held, came).astype(BF16) for came, held, _ in halves]
-    done = []
-    for held, (_, _, second) in zip(first_round, halves):
-        came = permuted(held[1], axis, lambda i, second=second: i ^ second)
-        done.append(added(held[0], came).astype(BF16))
-    return jnp.concatenate(done), first_round
-
-
 def ring_of_rings_sum(value, axis, inner):
     size, me = lax.axis_size(axis), lax.axis_index(axis)
     outer = size // inner
@@ -246,10 +227,6 @@
     groups = n_x * n_y * n_core
     dp_index, z_index = lax.axis_index(DP), lax.axis_index("z")
     indices = jnp.arange(groups, dtype=jnp.int32)
-    source_of = jnp.sum(jnp.where(dest_device[None, :] == indices[:, None], indices[None, :], 0), axis=1)
-    own_source = jnp.sum(jnp.where(dest_device == dp_index, indices, 0))
-    own_lengths = lax.dynamic_slice_in_dim(moved_lengths, dp_index * n_z + z_index, 1, 0)
-    recv_lengths = lax.dynamic_slice_in_dim(moved_lengths, own_source * n_z + z_index, 1, 0)
     seg_col, seg_row = kept_segments.reshape(keep, 1), kept_segments
 
     w_all = lax.all_gather(w_out, "z", axis=0, tiled=True)
@@ -264,9 +241,13 @@
         cost_estimate=cost(0, 8 * width),
         name="pack",
     )(uvqk, grad_out)
-    uvqk, grad_out, block = lax.optimization_barrier((uvqk, grad_out, block))
+    uvqk, grad_out, dest_device, block = lax.optimization_barrier((uvqk, grad_out, dest_device, block))
     block = exchange(block)
 
+    source_of = jnp.sum(jnp.where(dest_device[None, :] == indices[:, None], indices[None, :], 0), axis=1)
+    own_source = jnp.sum(jnp.where(dest_device == dp_index, indices, 0))
+    own_lengths = lax.dynamic_slice_in_dim(moved_lengths, dp_index * n_z + z_index, 1, 0)
+    recv_lengths = lax.dynamic_slice_in_dim(moved_lengths, own_source * n_z + z_index, 1, 0)
     block_cols = width // (n_core * n_x)
     core_half = jax.ShapeDtypeStruct((n_x, width, block_cols), BF16)
     mine, other = pl.pallas_call(
@@ -280,19 +261,18 @@
         name="term",
     )(lax.axis_index("core").reshape(1), own_lengths, uvqk, grad_out, seg_col, seg_row)
     part = added(mine, permuted(other, "core", lambda i: i ^ 1)).astype(BF16)
-    part, first_round = ring_of_four_sum(part, "x")
+    part = scatter_sum(part, "x")
     own_rows = width // n_z
-    block = lax.optimization_barrier((block, first_round))[0]
-    block = block[source_of]
     part, block = lax.optimization_barrier((part, block))
-    block = exchange(block)
-    part = ring_of_rings_sum(part.reshape(n_z, own_rows, block_cols), "z", min(4, n_z))
+    block = exchange(block[source_of])
+    own_rows = width // n_z
+    part = ring_of_rings_sum(part.reshape(n_z, own_rows, block_cols), "z", min(4, n_z)).astype(BF16)
     part = lax.optimization_barrier((part, block))[0]
-    part = exchange(part.reshape(n_y, own_rows // n_y, block_cols), "y")
-    part = (jnp.sum(part, axis=0) * (1.0 / (groups * n_z))).astype(BF16)
-    spread = exchange(jnp.broadcast_to(part[None], (groups,) + part.shape))
-    spread = spread.astype(F32).reshape(n_x, n_y, n_core, own_rows // n_y, block_cols)
-    grad_weight = spread.transpose(1, 3, 2, 0, 4).reshape(own_rows, width)
+    part = exchange(jnp.broadcast_to(part[None], (n_y,) + part.shape), "y")
+    part = (jnp.sum(part.astype(F32), axis=0) * (1.0 / (groups * n_z))).astype(BF16)
+    spread = exchange(jnp.broadcast_to(part[None], (n_x * n_core,) + part.shape), ("x", "core"))
+    spread = spread.reshape(n_x, n_core, own_rows, block_cols).transpose(2, 1, 0, 3)
+    grad_weight = spread.reshape(own_rows, width).astype(F32)
 
     grad_rows = pl.pallas_call(
         functools.partial(back_kernel, keep),

time: 166 us -> 162 us (0.976)
  blocking collectives: 13.6 us -> 0 us
  starting transfers between devices: 83.6 us -> 89.1 us
  waiting for transfers between devices: 27.9 us -> 32.5 us
    all_to_all x3 -> x4, starting transfers between devices: 22.3 us -> 44.8 us  [exchange(): return lax.all_to_all(value, axes, split_axis=0, concat_axis=0, tiled=True)]
    ppermute x11 -> x10, starting transfers between devices: 61.3 us -> 44.2 us  [permuted(): return lax.ppermute(value, axis, [(i, target(i)) for i in range(size)])]
    all_to_all x1 -> x0, blocking collectives: 13.6 us -> none  [exchange(): return lax.all_to_all(value, axes, split_axis=0, concat_axis=0, tiled=True)]
    ppermute x11 -> x10, waiting for transfers between devices: 21.2 us -> 24.7 us  [permuted(): return lax.ppermute(value, axis, [(i, target(i)) for i in range(size)])]
    all_to_all x3 -> x4, waiting for transfers between devices: 5.99 us -> 7.87 us  [exchange(): return lax.all_to_all(value, axes, split_axis=0, concat_axis=0, tiled=True)]
  transfers between devices with their start and end apart: 15 -> 15, of which waited for: 8 -> 8; matrix products, arithmetic and copies ran while one was open for 6% -> 7% of each run, Pallas kernels for 3% -> 5%
where the time goes in v6:
time: 162 us; the launch traced here: 161 us
  starting transfers between devices  89.1 us (55%)
  waiting for transfers between devices  32.5 us (20%)
  between operations  15 us (9%)
  Pallas kernels  10.6 us (7%)
  local copies, waits for them, and re-layouts  9.8 us (6%)
  other arithmetic  4.19 us (3%)
    all_to_all x4, starting transfers between devices, exchange(): return lax.all_to_all(value, axes, split_axis=0, concat_axis=0, tiled=True)  44.8 us
    ppermute x10, starting transfers between devices, permuted(): return lax.ppermute(value, axis, [(i, target(i)) for i in range(size)])  44.2 us
    ppermute x10, waiting for transfers between devices, permuted(): return lax.ppermute(value, axis, [(i, target(i)) for i in range(size)])  24.7 us
    all_to_all x4, waiting for transfers between devices, exchange(): return lax.all_to_all(value, axes, split_axis=0, concat_axis=0, tiled=True)  7.87 us
    pallas_call x1, Pallas kernels, local(): pl.pallas_call(functools.partial(back_kernel, keep), out_shape=jax.ShapeD...  5.03 us
  transfers between devices with their start and end apart: 15, of which 8 were waited for; matrix products, arithmetic and copies ran while one was open for 7% of the time, Pallas kernels for 5%

profile of v6, /device:TPU:1, one launch (start us, length us, event | category | flops | bytes accessed | tf_op | source)
XLA Modules:
  0.0 161.2 jit_solution(5744695205901202400)
XLA Ops:
  7.2 2.4 %pack.1 = bf16[64,16,640]{2,1,0:T(8,128)(2,1)} custom-call(bf16[192,4096]{1,0:T(8,128)(2,1)} %x_ref.3, bf16[192,1024]{1,0:T(8,128)(2,1)} %g_ref.3), custom_call_target="tpu_custom_call" | custom-call | bytes 8192 | tf_op jit(solution)/shard_map/pack/pallas_call | solution.py:234
  9.6 0.0 copy-start.4
  9.6 0.0 copy-start.3
  9.6 0.0 copy-start
  9.7 0.0 copy-start.1
  9.7 19.2 %all-to-all-start = ((bf16[64,16,640]{2,1,0:T(8,128)(2,1)}), bf16[64,16,640]{2,1,0:T(8,128)(2,1)}, u32[]{:S(2)}, u32[]{:S(2)}) async-start(bf16[64,16,640]{2,1,0:T(8,128)(2,1)} %pack.1), calls=%async_computation | async-start | bytes 2621440 | tf_op jit(solution)/shard_map/all_to_all | solution.py:219
  28.8 0.0 all-gather.2.cloned.1.call-start
  28.9 0.7 fusion.9
  30.2 0.8 constant_dynamic-slice_fusion
  31.1 0.1 copy.27.lengths_ref
  31.2 0.1 copy.23.seg_col_ref
  31.3 3.1 %term.1 = (bf16[4,1024,128]{2,1,0:T(8,128)(2,1)S(1)}, bf16[4,1024,128]{2,1,0:T(8,128)(2,1)}) custom-call(s32[1]{0:T(128)} %bitcast.core_ref, s32[1,3]{1,0:T(1,128)S(1)} %copy.27.lengths_ref, bf16[192,4096]{1,0:T(8,128)(2,1)S(1)} %copy-done, bf16[192,1024]{1,0:T(8,128)(2,1)S(1)} %copy-done.1, s32[64,1]{1,0:T(8,128)S(1)} %copy.23.seg_col_ref, ...), custom_call_target="tpu_custom_call" | custom-call | bytes 8192 | tf_op jit(solution)/shard_map/term/pallas_call | solution.py:253
  34.4 2.5 %collective-permute-start = (bf16[4,1024,128]{2,1,0:T(8,128)(2,1)}, bf16[4,1024,128]{2,1,0:T(8,128)(2,1)}, u32[]{:S(2)}, u32[]{:S(2)}) collective-permute-start(bf16[4,1024,128]{2,1,0:T(8,128)(2,1)} %get-tuple-element.15), channel_id=1, source_target_pairs={{0,16},{16,0},{1,17},{17,1},{2,18},{18,2},{3,19},{19,3},{4,20},{20... | collective-permute-start | bytes 3145736 | tf_op jit(solution)/shard_map/ppermute | solution.py:177
  36.9 0.0 all-gather.2.cloned.1.call-update
  36.9 0.1 select_reduce_fusion
  37.0 2.5 %collective-permute-done = bf16[4,1024,128]{2,1,0:T(8,128)(2,1)} collective-permute-done((bf16[4,1024,128]{2,1,0:T(8,128)(2,1)}, bf16[4,1024,128]{2,1,0:T(8,128)(2,1)}, u32[]{:S(2)}, u32[]{:S(2)}) %collective-permute-start) | collective-permute-done | bytes 1048608 | tf_op jit(solution)/shard_map/ppermute | solution.py:177
  39.5 1.6 add_convert_fusion
  41.1 0.1 dynamic-slice_bitcast_fusion.2
  41.1 3.1 %collective-permute-start.1 = (bf16[1024,128]{1,0:T(8,128)(2,1)S(1)}, bf16[1024,128]{1,0:T(8,128)(2,1)S(1)}, u32[]{:S(2)}, u32[]{:S(2)}) collective-permute-start(bf16[1024,128]{1,0:T(8,128)(2,1)S(1)} %get-tuple-element.20), channel_id=1, source_target_pairs={{0,256},{256,512},{512,768},{768,0},{1,257},{257,513},{513,769},{7... | collective-permute-start | bytes 786440 | tf_op jit(solution)/shard_map/ppermute | solution.py:177
  44.3 4.5 %collective-permute-start.2 = (bf16[1024,128]{1,0:T(8,128)(2,1)S(1)}, bf16[1024,128]{1,0:T(8,128)(2,1)S(1)}, u32[]{:S(2)}, u32[]{:S(2)}) collective-permute-start(bf16[1024,128]{1,0:T(8,128)(2,1)S(1)} %get-tuple-element.22), channel_id=1, source_target_pairs={{0,512},{256,768},{512,0},{768,256},{1,513},{257,769},{513,1},{769... | collective-permute-start | bytes 786440 | tf_op jit(solution)/shard_map/ppermute | solution.py:177
  48.8 3.0 %collective-permute-start.3 = (bf16[1024,128]{1,0:T(8,128)(2,1)S(1)}, bf16[1024,128]{1,0:T(8,128)(2,1)S(1)}, u32[]{:S(2)}, u32[]{:S(2)}) collective-permute-start(bf16[1024,128]{1,0:T(8,128)(2,1)S(1)} %get-tuple-element.21), channel_id=1, source_target_pairs={{0,768},{256,0},{512,256},{768,512},{1,769},{257,1},{513,257},{769... | collective-permute-start | bytes 786440 | tf_op jit(solution)/shard_map/ppermute | solution.py:177
  51.9 7.1 %collective-permute-done.1 = bf16[1024,128]{1,0:T(8,128)(2,1)S(1)} collective-permute-done((bf16[1024,128]{1,0:T(8,128)(2,1)S(1)}, bf16[1024,128]{1,0:T(8,128)(2,1)S(1)}, u32[]{:S(2)}, u32[]{:S(2)}) %collective-permute-start.1) | collective-permute-done | bytes 262176 | tf_op jit(solution)/shard_map/ppermute | solution.py:177
  59.0 6.6 %collective-permute-done.2 = bf16[1024,128]{1,0:T(8,128)(2,1)S(1)} collective-permute-done((bf16[1024,128]{1,0:T(8,128)(2,1)S(1)}, bf16[1024,128]{1,0:T(8,128)(2,1)S(1)}, u32[]{:S(2)}, u32[]{:S(2)}) %collective-permute-start.2) | collective-permute-done | bytes 262176 | tf_op jit(solution)/shard_map/ppermute | solution.py:177
  65.5 0.1 collective-permute-done.3
  65.7 0.8 fusion.2
  66.5 3.1 %gather_fusion = bf16[64,16,640]{2,1,0:T(8,128)(2,1)} fusion(bf16[64,16,640]{2,1,0:T(8,128)(2,1)} %all-to-all-done, s32[1024]{0:T(1024)S(1)} %pad_clamp_fusion), kind=kCustom, calls=%fused_computation | custom fusion | bytes 2621696 | tf_op jit(solution)/shard_map/gather | solution.py:267
  69.6 10.2 %all-to-all-start.1 = ((bf16[64,16,640]{2,1,0:T(8,128)(2,1)}), bf16[64,16,640]{2,1,0:T(8,128)(2,1)S(1)}, u32[]{:S(2)}, u32[]{:S(2)}) async-start(bf16[64,16,640]{2,1,0:T(8,128)(2,1)} %gather_fusion), calls=%async_computation.1 | async-start | bytes 2621440 | tf_op jit(solution)/shard_map/all_to_all | solution.py:219
  79.8 1.6 dynamic-slice_bitcast_fusion.5
  81.4 1.9 %collective-permute-start.4 = (bf16[4,64,128]{2,1,0:T(8,128)(2,1)}, bf16[4,64,128]{2,1,0:T(8,128)(2,1)S(1)}, u32[]{:S(2)}, u32[]{:S(2)}) collective-permute-start(bf16[4,64,128]{2,1,0:T(8,128)(2,1)} %get-tuple-element.23), channel_id=1, source_target_pairs={{0,1},{1,2},{2,3},{3,0},{4,5},{5,6},{6,7},{7,4},{8,9},{9,10},{10,1... | collective-permute-start | bytes 196616 | tf_op jit(solution)/shard_map/ppermute | solution.py:177
  83.3 1.9 %collective-permute-start.5 = (bf16[4,64,128]{2,1,0:T(8,128)(2,1)}, bf16[4,64,128]{2,1,0:T(8,128)(2,1)S(1)}, u32[]{:S(2)}, u32[]{:S(2)}) collective-permute-start(bf16[4,64,128]{2,1,0:T(8,128)(2,1)} %get-tuple-element.25), channel_id=1, source_target_pairs={{0,2},{1,3},{2,0},{3,1},{4,6},{5,7},{6,4},{7,5},{8,10},{9,11},{10,... | collective-permute-start | bytes 196616 | tf_op jit(solution)/shard_map/ppermute | solution.py:177
  85.2 5.2 %collective-permute-start.6 = (bf16[4,64,128]{2,1,0:T(8,128)(2,1)S(1)}, bf16[4,64,128]{2,1,0:T(8,128)(2,1)}, u32[]{:S(2)}, u32[]{:S(2)}) collective-permute-start(bf16[4,64,128]{2,1,0:T(8,128)(2,1)S(1)} %get-tuple-element.24), channel_id=1, source_target_pairs={{0,3},{1,0},{2,1},{3,2},{4,7},{5,4},{6,5},{7,6},{8,11},{9,8},{10,9... | collective-permute-start | bytes 196616 | tf_op jit(solution)/shard_map/ppermute | solution.py:177
  90.4 3.3 %collective-permute-done.5 = bf16[4,64,128]{2,1,0:T(8,128)(2,1)S(1)} collective-permute-done((bf16[4,64,128]{2,1,0:T(8,128)(2,1)}, bf16[4,64,128]{2,1,0:T(8,128)(2,1)S(1)}, u32[]{:S(2)}, u32[]{:S(2)}) %collective-permute-start.5) | collective-permute-done | bytes 65568 | tf_op jit(solution)/shard_map/ppermute | solution.py:177
  93.7 0.7 collective-permute-done.6
  94.4 0.9 fusion.5
  95.4 6.4 %collective-permute-start.7 = (bf16[64,128]{1,0:T(8,128)(2,1)S(1)}, bf16[64,128]{1,0:T(8,128)(2,1)S(1)}, u32[]{:S(2)}, u32[]{:S(2)}) collective-permute-start(bf16[64,128]{1,0:T(8,128)(2,1)S(1)} %get-tuple-element.26), channel_id=1, source_target_pairs={{0,4},{1,5},{2,6},{3,7},{4,8},{5,9},{6,10},{7,11},{8,12},{9,13},{1... | collective-permute-start | bytes 49160 | tf_op jit(solution)/shard_map/ppermute | solution.py:177
  101.7 11.7 %collective-permute-start.8 = (bf16[64,128]{1,0:T(8,128)(2,1)S(1)}, bf16[64,128]{1,0:T(8,128)(2,1)S(1)}, u32[]{:S(2)}, u32[]{:S(2)}) collective-permute-start(bf16[64,128]{1,0:T(8,128)(2,1)S(1)} %get-tuple-element.28), channel_id=1, source_target_pairs={{0,8},{1,9},{2,10},{3,11},{4,12},{5,13},{6,14},{7,15},{8,0},{9,1},... | collective-permute-start | bytes 49160 | tf_op jit(solution)/shard_map/ppermute | solution.py:177
  113.4 4.0 %collective-permute-start.9 = (bf16[64,128]{1,0:T(8,128)(2,1)S(1)}, bf16[64,128]{1,0:T(8,128)(2,1)S(1)}, u32[]{:S(2)}, u32[]{:S(2)}) collective-permute-start(bf16[64,128]{1,0:T(8,128)(2,1)S(1)} %get-tuple-element.27), channel_id=1, source_target_pairs={{0,12},{1,13},{2,14},{3,15},{4,0},{5,1},{6,2},{7,3},{8,4},{9,5},{1... | collective-permute-start | bytes 49160 | tf_op jit(solution)/shard_map/ppermute | solution.py:177
  117.5 4.4 %collective-permute-done.9 = bf16[64,128]{1,0:T(8,128)(2,1)S(1)} collective-permute-done((bf16[64,128]{1,0:T(8,128)(2,1)S(1)}, bf16[64,128]{1,0:T(8,128)(2,1)S(1)}, u32[]{:S(2)}, u32[]{:S(2)}) %collective-permute-start.9) | collective-permute-done | bytes 16416 | tf_op jit(solution)/shard_map/ppermute | solution.py:177
  121.9 0.7 broadcast_in_dim.38
  122.5 7.1 %all-to-all-start.2 = ((bf16[8,64,128]{2,1,0:T(8,128)(2,1)}), bf16[8,64,128]{2,1,0:T(8,128)(2,1)S(1)}, u32[]{:S(2)}, u32[]{:S(2)}) async-start(bf16[8,64,128]{2,1,0:T(8,128)(2,1)} %broadcast_in_dim.38), calls=%async_computation.2 | async-start | bytes 262144 | tf_op jit(solution)/shard_map/all_to_all | solution.py:219
  129.7 0.1 copy.26.lengths_ref
  129.8 7.9 %all-to-all-done.2 = bf16[8,64,128]{2,1,0:T(8,128)(2,1)S(1)} async-done(((bf16[8,64,128]{2,1,0:T(8,128)(2,1)}), bf16[8,64,128]{2,1,0:T(8,128)(2,1)S(1)}, u32[]{:S(2)}, u32[]{:S(2)}) %all-to-all-start.2) | async-done | bytes 131104 | tf_op jit(solution)/shard_map/all_to_all | solution.py:219
  137.7 0.7 broadcast_in_dim.39
  138.3 8.4 %all-to-all-start.3 = ((bf16[8,64,128]{2,1,0:T(8,128)(2,1)}), bf16[8,64,128]{2,1,0:T(8,128)(2,1)S(1)}, u32[]{:S(2)}, u32[]{:S(2)}) async-start(bf16[8,64,128]{2,1,0:T(8,128)(2,1)} %broadcast_in_dim.39), calls=%async_computation.3 | async-start | bytes 262144 | tf_op jit(solution)/shard_map/all_to_all | solution.py:219
  146.7 1.6 copy-done.2
  148.3 5.0 %back.1 = bf16[192,4096]{1,0:T(8,128)(2,1)} custom-call(s32[1,3]{1,0:T(1,128)S(1)} %copy.26.lengths_ref, bf16[192,4096]{1,0:T(8,128)(2,1)S(1)} %copy-done, bf16[192,1024]{1,0:T(8,128)(2,1)S(1)} %copy-done.1, bf16[64,16,640]{2,1,0:T(8,128)(2,1)S(1)} %all-to-all-done.1.came_ref, bf16[1024,1024]{1,0:T(8,128)(2,1)S(1)} %copy-done.2, ...), custom_call_target="tpu_custom_call" | custom-call | flops 1610612736 | bytes 8388608 | tf_op jit(solution)/shard_map/back/pallas_call | solution.py:277
  153.4 0.2 copy.25
  153.5 0.8 reshape.46
  (19 shorter events, 0.1 us)
Async XLA Ops:
  9.6 19.3 %copy-start.4 = (s32[64]{0:T(128)S(1)}, s32[64]{0:T(128)}, u32[]{:S(2)}) copy-start(s32[64]{0:T(128)} %param.11) | copy-start | bytes 772
  9.6 21.5 %copy-start.3 = (s32[1,64]{1,0:T(1,128)S(1)}, s32[1,64]{1,0:T(1,128)}, u32[]{:S(2)}) copy-start(s32[1,64]{1,0:T(1,128)} %seg_row_ref.3) | copy-start | bytes 772
  9.6 21.6 %copy-start = (bf16[192,4096]{1,0:T(8,128)(2,1)S(1)}, bf16[192,4096]{1,0:T(8,128)(2,1)}, u32[]{:S(2)}) copy-start(bf16[192,4096]{1,0:T(8,128)(2,1)} %x_ref.3) | copy-start | bytes 4718596
  9.7 21.6 %copy-start.1 = (bf16[192,1024]{1,0:T(8,128)(2,1)S(1)}, bf16[192,1024]{1,0:T(8,128)(2,1)}, u32[]{:S(2)}) copy-start(bf16[192,1024]{1,0:T(8,128)(2,1)} %g_ref.3) | copy-start | bytes 1179652
  9.7 56.9 %all-to-all-start = ((bf16[64,16,640]{2,1,0:T(8,128)(2,1)}), bf16[64,16,640]{2,1,0:T(8,128)(2,1)}, u32[]{:S(2)}, u32[]{:S(2)}) async-start(bf16[64,16,640]{2,1,0:T(8,128)(2,1)} %pack.1), calls=%async_computation | async-start | bytes 2621440 | tf_op jit(solution)/shard_map/all_to_all | solution.py:219
  28.8 117.9 %all-gather.2.cloned.1.call-start = ((), (), s32[]{:S(2)}) async-start(), calls=%async_computation.4 | async-start | bytes 2228224 | tf_op jit(solution)/shard_map/all_gather | solution.py:232
  34.4 5.1 %collective-permute-start = (bf16[4,1024,128]{2,1,0:T(8,128)(2,1)}, bf16[4,1024,128]{2,1,0:T(8,128)(2,1)}, u32[]{:S(2)}, u32[]{:S(2)}) collective-permute-start(bf16[4,1024,128]{2,1,0:T(8,128)(2,1)} %get-tuple-element.15), channel_id=1, source_target_pairs={{0,16},{16,0},{1,17},{17,1},{2,18},{18,2},{3,19},{19,3},{4,20},{20... | collective-permute-start | bytes 3145736 | tf_op jit(solution)/shard_map/ppermute | solution.py:177
  41.1 17.8 %collective-permute-start.1 = (bf16[1024,128]{1,0:T(8,128)(2,1)S(1)}, bf16[1024,128]{1,0:T(8,128)(2,1)S(1)}, u32[]{:S(2)}, u32[]{:S(2)}) collective-permute-start(bf16[1024,128]{1,0:T(8,128)(2,1)S(1)} %get-tuple-element.20), channel_id=1, source_target_pairs={{0,256},{256,512},{512,768},{768,0},{1,257},{257,513},{513,769},{7... | collective-permute-start | bytes 786440 | tf_op jit(solution)/shard_map/ppermute | solution.py:177
  44.3 21.3 %collective-permute-start.2 = (bf16[1024,128]{1,0:T(8,128)(2,1)S(1)}, bf16[1024,128]{1,0:T(8,128)(2,1)S(1)}, u32[]{:S(2)}, u32[]{:S(2)}) collective-permute-start(bf16[1024,128]{1,0:T(8,128)(2,1)S(1)} %get-tuple-element.22), channel_id=1, source_target_pairs={{0,512},{256,768},{512,0},{768,256},{1,513},{257,769},{513,1},{769... | collective-permute-start | bytes 786440 | tf_op jit(solution)/shard_map/ppermute | solution.py:177
  48.8 16.9 %collective-permute-start.3 = (bf16[1024,128]{1,0:T(8,128)(2,1)S(1)}, bf16[1024,128]{1,0:T(8,128)(2,1)S(1)}, u32[]{:S(2)}, u32[]{:S(2)}) collective-permute-start(bf16[1024,128]{1,0:T(8,128)(2,1)S(1)} %get-tuple-element.21), channel_id=1, source_target_pairs={{0,768},{256,0},{512,256},{768,512},{1,769},{257,1},{513,257},{769... | collective-permute-start | bytes 786440 | tf_op jit(solution)/shard_map/ppermute | solution.py:177
  69.6 52.2 %all-to-all-start.1 = ((bf16[64,16,640]{2,1,0:T(8,128)(2,1)}), bf16[64,16,640]{2,1,0:T(8,128)(2,1)S(1)}, u32[]{:S(2)}, u32[]{:S(2)}) async-start(bf16[64,16,640]{2,1,0:T(8,128)(2,1)} %gather_fusion), calls=%async_computation.1 | async-start | bytes 2621440 | tf_op jit(solution)/shard_map/all_to_all | solution.py:219
  81.4 9.0 %collective-permute-start.4 = (bf16[4,64,128]{2,1,0:T(8,128)(2,1)}, bf16[4,64,128]{2,1,0:T(8,128)(2,1)S(1)}, u32[]{:S(2)}, u32[]{:S(2)}) collective-permute-start(bf16[4,64,128]{2,1,0:T(8,128)(2,1)} %get-tuple-element.23), channel_id=1, source_target_pairs={{0,1},{1,2},{2,3},{3,0},{4,5},{5,6},{6,7},{7,4},{8,9},{9,10},{10,1... | collective-permute-start | bytes 196616 | tf_op jit(solution)/shard_map/ppermute | solution.py:177
  83.3 10.4 %collective-permute-start.5 = (bf16[4,64,128]{2,1,0:T(8,128)(2,1)}, bf16[4,64,128]{2,1,0:T(8,128)(2,1)S(1)}, u32[]{:S(2)}, u32[]{:S(2)}) collective-permute-start(bf16[4,64,128]{2,1,0:T(8,128)(2,1)} %get-tuple-element.25), channel_id=1, source_target_pairs={{0,2},{1,3},{2,0},{3,1},{4,6},{5,7},{6,4},{7,5},{8,10},{9,11},{10,... | collective-permute-start | bytes 196616 | tf_op jit(solution)/shard_map/ppermute | solution.py:177
  85.2 9.2 %collective-permute-start.6 = (bf16[4,64,128]{2,1,0:T(8,128)(2,1)S(1)}, bf16[4,64,128]{2,1,0:T(8,128)(2,1)}, u32[]{:S(2)}, u32[]{:S(2)}) collective-permute-start(bf16[4,64,128]{2,1,0:T(8,128)(2,1)S(1)} %get-tuple-element.24), channel_id=1, source_target_pairs={{0,3},{1,0},{2,1},{3,2},{4,7},{5,4},{6,5},{7,6},{8,11},{9,8},{10,9... | collective-permute-start | bytes 196616 | tf_op jit(solution)/shard_map/ppermute | solution.py:177
  95.4 22.1 %collective-permute-start.7 = (bf16[64,128]{1,0:T(8,128)(2,1)S(1)}, bf16[64,128]{1,0:T(8,128)(2,1)S(1)}, u32[]{:S(2)}, u32[]{:S(2)}) collective-permute-start(bf16[64,128]{1,0:T(8,128)(2,1)S(1)} %get-tuple-element.26), channel_id=1, source_target_pairs={{0,4},{1,5},{2,6},{3,7},{4,8},{5,9},{6,10},{7,11},{8,12},{9,13},{1... | collective-permute-start | bytes 49160 | tf_op jit(solution)/shard_map/ppermute | solution.py:177
  101.7 15.7 %collective-permute-start.8 = (bf16[64,128]{1,0:T(8,128)(2,1)S(1)}, bf16[64,128]{1,0:T(8,128)(2,1)S(1)}, u32[]{:S(2)}, u32[]{:S(2)}) collective-permute-start(bf16[64,128]{1,0:T(8,128)(2,1)S(1)} %get-tuple-element.28), channel_id=1, source_target_pairs={{0,8},{1,9},{2,10},{3,11},{4,12},{5,13},{6,14},{7,15},{8,0},{9,1},... | collective-permute-start | bytes 49160 | tf_op jit(solution)/shard_map/ppermute | solution.py:177
  113.4 8.4 %collective-permute-start.9 = (bf16[64,128]{1,0:T(8,128)(2,1)S(1)}, bf16[64,128]{1,0:T(8,128)(2,1)S(1)}, u32[]{:S(2)}, u32[]{:S(2)}) collective-permute-start(bf16[64,128]{1,0:T(8,128)(2,1)S(1)} %get-tuple-element.27), channel_id=1, source_target_pairs={{0,12},{1,13},{2,14},{3,15},{4,0},{5,1},{6,2},{7,3},{8,4},{9,5},{1... | collective-permute-start | bytes 49160 | tf_op jit(solution)/shard_map/ppermute | solution.py:177
  122.5 15.1 %all-to-all-start.2 = ((bf16[8,64,128]{2,1,0:T(8,128)(2,1)}), bf16[8,64,128]{2,1,0:T(8,128)(2,1)S(1)}, u32[]{:S(2)}, u32[]{:S(2)}) async-start(bf16[8,64,128]{2,1,0:T(8,128)(2,1)} %broadcast_in_dim.38), calls=%async_computation.2 | async-start | bytes 262144 | tf_op jit(solution)/shard_map/all_to_all | solution.py:219
  138.3 15.0 %all-to-all-start.3 = ((bf16[8,64,128]{2,1,0:T(8,128)(2,1)}), bf16[8,64,128]{2,1,0:T(8,128)(2,1)S(1)}, u32[]{:S(2)}, u32[]{:S(2)}) async-start(bf16[8,64,128]{2,1,0:T(8,128)(2,1)} %broadcast_in_dim.39), calls=%async_computation.3 | async-start | bytes 262144 | tf_op jit(solution)/shard_map/all_to_all | solution.py:219
  146.7 1.6 copy-start.2
Sparse Core Ops, SparseCore 0:
  37.0 70.5 all-gather.1

commit v7 on v6

--- a/solution.py
+++ b/solution.py
@@ -263,17 +263,11 @@
     part = added(mine, permuted(other, "core", lambda i: i ^ 1)).astype(BF16)
     part = scatter_sum(part, "x")
     own_rows = width // n_z
-    part, block = lax.optimization_barrier((part, block))
-    block = exchange(block[source_of])
-    own_rows = width // n_z
+    part, block = lax.optimization_barrier((part, block[source_of]))
+    block = exchange(block)
     part = ring_of_rings_sum(part.reshape(n_z, own_rows, block_cols), "z", min(4, n_z)).astype(BF16)
     part = lax.optimization_barrier((part, block))[0]
     part = exchange(jnp.broadcast_to(part[None], (n_y,) + part.shape), "y")
-    part = (jnp.sum(part.astype(F32), axis=0) * (1.0 / (groups * n_z))).astype(BF16)
-    spread = exchange(jnp.broadcast_to(part[None], (n_x * n_core,) + part.shape), ("x", "core"))
-    spread = spread.reshape(n_x, n_core, own_rows, block_cols).transpose(2, 1, 0, 3)
-    grad_weight = spread.reshape(own_rows, width).astype(F32)
-
     grad_rows = pl.pallas_call(
         functools.partial(back_kernel, keep),
         out_shape=jax.ShapeDtypeStruct(uvqk.shape, BF16),
@@ -284,6 +278,11 @@
         cost_estimate=cost(8 * rows * width * width, 8 * width * width),
         name="back",
     )(recv_lengths, uvqk, grad_out, block, w_all, seg_col, seg_row)
+    part, grad_rows = lax.optimization_barrier((part, grad_rows))
+    part = (jnp.sum(part.astype(F32), axis=0) * (1.0 / (groups * n_z))).astype(BF16)
+    spread = exchange(jnp.broadcast_to(part[None], (n_x * n_core,) + part.shape), ("x", "core"))
+    spread = spread.reshape(n_x, n_core, own_rows, block_cols).transpose(2, 1, 0, 3)
+    grad_weight = spread.reshape(own_rows, width).astype(F32)
     return grad_rows, grad_weight
 
 

time: 162 us -> 157 us (0.969)
  starting transfers between devices: 89.1 us -> 74.9 us
  blocking collectives: 0 us -> 13.7 us
  waiting for transfers between devices: 32.5 us -> 28.9 us
    all_to_all x0 -> x1, blocking collectives: none -> 13.7 us  [exchange(): return lax.all_to_all(value, axes, split_axis=0, concat_axis=0, tiled=True)]
    all_to_all x4 -> x3, starting transfers between devices: 44.8 us -> 32.8 us  [exchange(): return lax.all_to_all(value, axes, split_axis=0, concat_axis=0, tiled=True)]
    all_to_all x4 -> x3, waiting for transfers between devices: 7.87 us -> 1.33 us  [exchange(): return lax.all_to_all(value, axes, split_axis=0, concat_axis=0, tiled=True)]
    ppermute x10, waiting for transfers between devices: 24.7 us -> 27.6 us  [permuted(): return lax.ppermute(value, axis, [(i, target(i)) for i in range(size)])]
    ppermute x10, starting transfers between devices: 44.2 us -> 42.1 us  [permuted(): return lax.ppermute(value, axis, [(i, target(i)) for i in range(size)])]
  transfers between devices with their start and end apart: 15 -> 14, of which waited for: 8 -> 8; matrix products, arithmetic and copies ran while one was open for 7% -> 7% of each run, Pallas kernels for 5% -> 5%
where the time goes in v7:
time: 157 us; the launch traced here: 156 us
  starting transfers between devices  74.9 us (48%)
  waiting for transfers between devices  28.9 us (18%)
  between operations  14.9 us (9%)
  blocking collectives  13.7 us (9%)
  Pallas kernels  10.6 us (7%)
  local copies, waits for them, and re-layouts  9.1 us (6%)
  other arithmetic  4.16 us (3%)
    ppermute x10, starting transfers between devices, permuted(): return lax.ppermute(value, axis, [(i, target(i)) for i in range(size)])  42.1 us
    all_to_all x3, starting transfers between devices, exchange(): return lax.all_to_all(value, axes, split_axis=0, concat_axis=0, tiled=True)  32.8 us
    ppermute x10, waiting for transfers between devices, permuted(): return lax.ppermute(value, axis, [(i, target(i)) for i in range(size)])  27.6 us
    all_to_all x1, blocking collectives, exchange(): return lax.all_to_all(value, axes, split_axis=0, concat_axis=0, tiled=True)  13.7 us
    pallas_call x1, Pallas kernels, local(): pl.pallas_call(functools.partial(back_kernel, keep), out_shape=jax.ShapeD...  5.02 us
  transfers between devices with their start and end apart: 14, of which 8 were waited for; matrix products, arithmetic and copies ran while one was open for 7% of the time, Pallas kernels for 5%

profile of v7, /device:TPU:1, one launch (start us, length us, event | category | flops | bytes accessed | tf_op | source)
XLA Modules:
  0.0 156.2 jit_solution(9674292385489023428)
XLA Ops:
  7.2 2.4 %pack.1 = bf16[64,16,640]{2,1,0:T(8,128)(2,1)} custom-call(bf16[192,4096]{1,0:T(8,128)(2,1)} %x_ref.3, bf16[192,1024]{1,0:T(8,128)(2,1)} %g_ref.3), custom_call_target="tpu_custom_call" | custom-call | bytes 8192 | tf_op jit(solution)/shard_map/pack/pallas_call | solution.py:234
  9.6 0.0 copy-start.4
  9.6 0.0 copy-start.3
  9.6 0.0 copy-start
  9.7 0.0 copy-start.1
  9.7 19.2 %all-to-all-start = ((bf16[64,16,640]{2,1,0:T(8,128)(2,1)}), bf16[64,16,640]{2,1,0:T(8,128)(2,1)}, u32[]{:S(2)}, u32[]{:S(2)}) async-start(bf16[64,16,640]{2,1,0:T(8,128)(2,1)} %pack.1), calls=%async_computation | async-start | bytes 2621440 | tf_op jit(solution)/shard_map/all_to_all | solution.py:219
  28.8 0.0 all-gather.2.cloned.1.call-start
  28.9 0.6 fusion.9
  30.1 0.8 constant_dynamic-slice_fusion
  30.9 0.1 copy.26.lengths_ref
  31.0 0.1 copy.22.seg_col_ref
  31.1 3.1 %term.1 = (bf16[4,1024,128]{2,1,0:T(8,128)(2,1)S(1)}, bf16[4,1024,128]{2,1,0:T(8,128)(2,1)}) custom-call(s32[1]{0:T(128)} %bitcast.core_ref, s32[1,3]{1,0:T(1,128)S(1)} %copy.26.lengths_ref, bf16[192,4096]{1,0:T(8,128)(2,1)S(1)} %copy-done, bf16[192,1024]{1,0:T(8,128)(2,1)S(1)} %copy-done.1, s32[64,1]{1,0:T(8,128)S(1)} %copy.22.seg_col_ref, ...), custom_call_target="tpu_custom_call" | custom-call | bytes 8192 | tf_op jit(solution)/shard_map/term/pallas_call | solution.py:253
  34.2 2.5 %collective-permute-start = (bf16[4,1024,128]{2,1,0:T(8,128)(2,1)}, bf16[4,1024,128]{2,1,0:T(8,128)(2,1)}, u32[]{:S(2)}, u32[]{:S(2)}) collective-permute-start(bf16[4,1024,128]{2,1,0:T(8,128)(2,1)} %get-tuple-element.16), channel_id=1, source_target_pairs={{0,16},{16,0},{1,17},{17,1},{2,18},{18,2},{3,19},{19,3},{4,20},{20... | collective-permute-start | bytes 3145736 | tf_op jit(solution)/shard_map/ppermute | solution.py:177
  36.8 0.0 all-gather.2.cloned.1.call-update
  36.8 0.1 select_reduce_fusion
  36.9 2.5 %collective-permute-done = bf16[4,1024,128]{2,1,0:T(8,128)(2,1)} collective-permute-done((bf16[4,1024,128]{2,1,0:T(8,128)(2,1)}, bf16[4,1024,128]{2,1,0:T(8,128)(2,1)}, u32[]{:S(2)}, u32[]{:S(2)}) %collective-permute-start) | collective-permute-done | bytes 1048608 | tf_op jit(solution)/shard_map/ppermute | solution.py:177
  39.4 1.6 %add_convert_fusion = bf16[4,1024,128]{2,1,0:T(8,128)(2,1)S(1)} fusion(bf16[4,1024,128]{2,1,0:T(8,128)(2,1)} %collective-permute-done, bf16[4,1024,128]{2,1,0:T(8,128)(2,1)S(1)} %get-tuple-element.15), kind=kLoop, calls=%fused_computation.1 | loop fusion | flops 2097152 | bytes 3145728 | tf_op jit(solution)/shard_map/convert_element_type | solution.py:263
  40.9 0.1 dynamic-slice_bitcast_fusion.2
  41.0 4.6 %collective-permute-start.3 = (bf16[1024,128]{1,0:T(8,128)(2,1)S(1)}, bf16[1024,128]{1,0:T(8,128)(2,1)S(1)}, u32[]{:S(2)}, u32[]{:S(2)}) collective-permute-start(bf16[1024,128]{1,0:T(8,128)(2,1)S(1)} %get-tuple-element.25), channel_id=1, source_target_pairs={{0,768},{256,0},{512,256},{768,512},{1,769},{257,1},{513,257},{769... | collective-permute-start | bytes 786440 | tf_op jit(solution)/shard_map/ppermute | solution.py:177
  45.6 2.3 %collective-permute-start.2 = (bf16[1024,128]{1,0:T(8,128)(2,1)S(1)}, bf16[1024,128]{1,0:T(8,128)(2,1)S(1)}, u32[]{:S(2)}, u32[]{:S(2)}) collective-permute-start(bf16[1024,128]{1,0:T(8,128)(2,1)S(1)} %get-tuple-element.26), channel_id=1, source_target_pairs={{0,512},{256,768},{512,0},{768,256},{1,513},{257,769},{513,1},{769... | collective-permute-start | bytes 786440 | tf_op jit(solution)/shard_map/ppermute | solution.py:177
  47.9 2.6 %collective-permute-start.1 = (bf16[1024,128]{1,0:T(8,128)(2,1)S(1)}, bf16[1024,128]{1,0:T(8,128)(2,1)S(1)}, u32[]{:S(2)}, u32[]{:S(2)}) collective-permute-start(bf16[1024,128]{1,0:T(8,128)(2,1)S(1)} %get-tuple-element.24), channel_id=1, source_target_pairs={{0,256},{256,512},{512,768},{768,0},{1,257},{257,513},{513,769},{7... | collective-permute-start | bytes 786440 | tf_op jit(solution)/shard_map/ppermute | solution.py:177
  50.5 6.1 %collective-permute-done.3 = bf16[1024,128]{1,0:T(8,128)(2,1)S(1)} collective-permute-done((bf16[1024,128]{1,0:T(8,128)(2,1)S(1)}, bf16[1024,128]{1,0:T(8,128)(2,1)S(1)}, u32[]{:S(2)}, u32[]{:S(2)}) %collective-permute-start.3) | collective-permute-done | bytes 262176 | tf_op jit(solution)/shard_map/ppermute | solution.py:177
  56.6 3.5 %collective-permute-done.2 = bf16[1024,128]{1,0:T(8,128)(2,1)S(1)} collective-permute-done((bf16[1024,128]{1,0:T(8,128)(2,1)S(1)}, bf16[1024,128]{1,0:T(8,128)(2,1)S(1)}, u32[]{:S(2)}, u32[]{:S(2)}) %collective-permute-start.2) | collective-permute-done | bytes 262176 | tf_op jit(solution)/shard_map/ppermute | solution.py:177
  60.1 7.4 %collective-permute-done.1 = bf16[1024,128]{1,0:T(8,128)(2,1)S(1)} collective-permute-done((bf16[1024,128]{1,0:T(8,128)(2,1)S(1)}, bf16[1024,128]{1,0:T(8,128)(2,1)S(1)}, u32[]{:S(2)}, u32[]{:S(2)}) %collective-permute-start.1) | collective-permute-done | bytes 262176 | tf_op jit(solution)/shard_map/ppermute | solution.py:177
  67.5 0.8 fusion.2
  68.3 0.0 all-to-all-done
  68.3 3.1 %gather_fusion = bf16[64,16,640]{2,1,0:T(8,128)(2,1)} fusion(bf16[64,16,640]{2,1,0:T(8,128)(2,1)} %all-to-all-done, s32[1024]{0:T(1024)S(1)} %pad_clamp_fusion), kind=kCustom, calls=%fused_computation | custom fusion | bytes 2621696 | tf_op jit(solution)/shard_map/gather | solution.py:266
  71.4 6.7 %all-to-all-start.1 = ((bf16[64,16,640]{2,1,0:T(8,128)(2,1)}), bf16[64,16,640]{2,1,0:T(8,128)(2,1)S(1)}, u32[]{:S(2)}, u32[]{:S(2)}) async-start(bf16[64,16,640]{2,1,0:T(8,128)(2,1)} %gather_fusion), calls=%async_computation.1 | async-start | bytes 2621440 | tf_op jit(solution)/shard_map/all_to_all | solution.py:219
  78.2 1.6 %dynamic-slice_bitcast_fusion.5 = (bf16[4,64,128]{2,1,0:T(8,128)(2,1)S(1)}, bf16[4,64,128]{2,1,0:T(8,128)(2,1)}, bf16[4,64,128]{2,1,0:T(8,128)(2,1)}) fusion(bf16[4,4,64,128]{3,2,1,0:T(8,128)(2,1)} %bitcast.39, s32[]{:T(128)S(6)} %select_n.71, s32[]{:T(128)S(6)} %select_n.73, s32[]{:T(128)S(6)} %select_n.72), kind=kLoop, calls=%fused_computation.17 | loop fusion | bytes 393228 | tf_op jit(solution)/shard_map/jit(dynamic_index_in_dim)/squeeze | solution.py:181
  79.7 1.9 %collective-permute-start.6 = (bf16[4,64,128]{2,1,0:T(8,128)(2,1)}, bf16[4,64,128]{2,1,0:T(8,128)(2,1)S(1)}, u32[]{:S(2)}, u32[]{:S(2)}) collective-permute-start(bf16[4,64,128]{2,1,0:T(8,128)(2,1)} %get-tuple-element.28), channel_id=1, source_target_pairs={{0,3},{1,0},{2,1},{3,2},{4,7},{5,4},{6,5},{7,6},{8,11},{9,8},{10,9... | collective-permute-start | bytes 196616 | tf_op jit(solution)/shard_map/ppermute | solution.py:177
  81.6 1.9 %collective-permute-start.5 = (bf16[4,64,128]{2,1,0:T(8,128)(2,1)}, bf16[4,64,128]{2,1,0:T(8,128)(2,1)S(1)}, u32[]{:S(2)}, u32[]{:S(2)}) collective-permute-start(bf16[4,64,128]{2,1,0:T(8,128)(2,1)} %get-tuple-element.29), channel_id=1, source_target_pairs={{0,2},{1,3},{2,0},{3,1},{4,6},{5,7},{6,4},{7,5},{8,10},{9,11},{10,... | collective-permute-start | bytes 196616 | tf_op jit(solution)/shard_map/ppermute | solution.py:177
  83.6 3.4 %collective-permute-start.4 = (bf16[4,64,128]{2,1,0:T(8,128)(2,1)S(1)}, bf16[4,64,128]{2,1,0:T(8,128)(2,1)}, u32[]{:S(2)}, u32[]{:S(2)}) collective-permute-start(bf16[4,64,128]{2,1,0:T(8,128)(2,1)S(1)} %get-tuple-element.27), channel_id=1, source_target_pairs={{0,1},{1,2},{2,3},{3,0},{4,5},{5,6},{6,7},{7,4},{8,9},{9,10},{10,1... | collective-permute-start | bytes 196616 | tf_op jit(solution)/shard_map/ppermute | solution.py:177
  87.0 4.2 %collective-permute-done.5 = bf16[4,64,128]{2,1,0:T(8,128)(2,1)S(1)} collective-permute-done((bf16[4,64,128]{2,1,0:T(8,128)(2,1)}, bf16[4,64,128]{2,1,0:T(8,128)(2,1)S(1)}, u32[]{:S(2)}, u32[]{:S(2)}) %collective-permute-start.5) | collective-permute-done | bytes 65568 | tf_op jit(solution)/shard_map/ppermute | solution.py:177
  91.1 1.3 collective-permute-done.4
  92.4 0.9 fusion.5
  93.3 12.3 %collective-permute-start.9 = (bf16[64,128]{1,0:T(8,128)(2,1)S(1)}, bf16[64,128]{1,0:T(8,128)(2,1)S(1)}, u32[]{:S(2)}, u32[]{:S(2)}) collective-permute-start(bf16[64,128]{1,0:T(8,128)(2,1)S(1)} %get-tuple-element.31), channel_id=1, source_target_pairs={{0,12},{1,13},{2,14},{3,15},{4,0},{5,1},{6,2},{7,3},{8,4},{9,5},{1... | collective-permute-start | bytes 49160 | tf_op jit(solution)/shard_map/ppermute | solution.py:177
  105.6 3.4 %collective-permute-start.8 = (bf16[64,128]{1,0:T(8,128)(2,1)S(1)}, bf16[64,128]{1,0:T(8,128)(2,1)S(1)}, u32[]{:S(2)}, u32[]{:S(2)}) collective-permute-start(bf16[64,128]{1,0:T(8,128)(2,1)S(1)} %get-tuple-element.32), channel_id=1, source_target_pairs={{0,8},{1,9},{2,10},{3,11},{4,12},{5,13},{6,14},{7,15},{8,0},{9,1},... | collective-permute-start | bytes 49160 | tf_op jit(solution)/shard_map/ppermute | solution.py:177
  109.0 7.3 %collective-permute-start.7 = (bf16[64,128]{1,0:T(8,128)(2,1)S(1)}, bf16[64,128]{1,0:T(8,128)(2,1)S(1)}, u32[]{:S(2)}, u32[]{:S(2)}) collective-permute-start(bf16[64,128]{1,0:T(8,128)(2,1)S(1)} %get-tuple-element.30), channel_id=1, source_target_pairs={{0,4},{1,5},{2,6},{3,7},{4,8},{5,9},{6,10},{7,11},{8,12},{9,13},{1... | collective-permute-start | bytes 49160 | tf_op jit(solution)/shard_map/ppermute | solution.py:177
  116.3 2.6 %collective-permute-done.8 = bf16[64,128]{1,0:T(8,128)(2,1)S(1)} collective-permute-done((bf16[64,128]{1,0:T(8,128)(2,1)S(1)}, bf16[64,128]{1,0:T(8,128)(2,1)S(1)}, u32[]{:S(2)}, u32[]{:S(2)}) %collective-permute-start.8) | collective-permute-done | bytes 16416 | tf_op jit(solution)/shard_map/ppermute | solution.py:177
  119.0 0.7 broadcast_in_dim.20
  119.6 6.9 %all-to-all-start.2 = ((bf16[8,64,128]{2,1,0:T(8,128)(2,1)}), bf16[8,64,128]{2,1,0:T(8,128)(2,1)S(1)}, u32[]{:S(2)}, u32[]{:S(2)}) async-start(bf16[8,64,128]{2,1,0:T(8,128)(2,1)} %broadcast_in_dim.20), calls=%async_computation.2 | async-start | bytes 262144 | tf_op jit(solution)/shard_map/all_to_all | solution.py:219
  126.6 0.1 copy.27.lengths_ref
  126.7 1.6 %copy-done.2 = bf16[1024,1024]{1,0:T(8,128)(2,1)S(1)} copy-done((bf16[1024,1024]{1,0:T(8,128)(2,1)S(1)}, bf16[1024,1024]{1,0:T(8,128)(2,1)}, u32[]{:S(2)}) %copy-start.2) | copy-done | bytes 2097176
  128.2 5.0 %back.1 = bf16[192,4096]{1,0:T(8,128)(2,1)} custom-call(s32[1,3]{1,0:T(1,128)S(1)} %copy.27.lengths_ref, bf16[192,4096]{1,0:T(8,128)(2,1)S(1)} %copy-done, bf16[192,1024]{1,0:T(8,128)(2,1)S(1)} %copy-done.1, bf16[64,16,640]{2,1,0:T(8,128)(2,1)S(1)} %all-to-all-done.1.came_ref, bf16[1024,1024]{1,0:T(8,128)(2,1)S(1)} %copy-done.2, ...), custom_call_target="tpu_custom_call" | custom-call | flops 1610612736 | bytes 8388608 | tf_op jit(solution)/shard_map/back/pallas_call | solution.py:271
  133.3 1.3 all-to-all-done.2
  134.7 13.7 %all_to_all.20 = bf16[8,64,128]{2,1,0:T(8,128)(2,1)S(1)} all-to-all(bf16[8,64,128]{2,1,0:T(8,128)(2,1)S(1)} %broadcast_in_dim.21), channel_id=1, replica_groups=mesh['x'=4,'y'=8,'core'=2,'z'=16] {'x','core'}, dimensions={0} | all-to-all | bytes 262144 | tf_op jit(solution)/shard_map/all_to_all | solution.py:219
  148.4 0.2 copy.25
  148.6 0.8 reshape.46
  (18 shorter events, 0.1 us)
Async XLA Ops:
  9.6 19.3 %copy-start.4 = (s32[64]{0:T(128)S(1)}, s32[64]{0:T(128)}, u32[]{:S(2)}) copy-start(s32[64]{0:T(128)} %param.11) | copy-start | bytes 772
  9.6 21.4 %copy-start.3 = (s32[1,64]{1,0:T(1,128)S(1)}, s32[1,64]{1,0:T(1,128)}, u32[]{:S(2)}) copy-start(s32[1,64]{1,0:T(1,128)} %seg_row_ref.3) | copy-start | bytes 772
  9.6 21.4 %copy-start = (bf16[192,4096]{1,0:T(8,128)(2,1)S(1)}, bf16[192,4096]{1,0:T(8,128)(2,1)}, u32[]{:S(2)}) copy-start(bf16[192,4096]{1,0:T(8,128)(2,1)} %x_ref.3) | copy-start | bytes 4718596
  9.7 21.4 %copy-start.1 = (bf16[192,1024]{1,0:T(8,128)(2,1)S(1)}, bf16[192,1024]{1,0:T(8,128)(2,1)}, u32[]{:S(2)}) copy-start(bf16[192,1024]{1,0:T(8,128)(2,1)} %g_ref.3) | copy-start | bytes 1179652
  9.7 58.7 %all-to-all-start = ((bf16[64,16,640]{2,1,0:T(8,128)(2,1)}), bf16[64,16,640]{2,1,0:T(8,128)(2,1)}, u32[]{:S(2)}, u32[]{:S(2)}) async-start(bf16[64,16,640]{2,1,0:T(8,128)(2,1)} %pack.1), calls=%async_computation | async-start | bytes 2621440 | tf_op jit(solution)/shard_map/all_to_all | solution.py:219
  28.8 97.8 %all-gather.2.cloned.1.call-start = ((), (), s32[]{:S(2)}) async-start(), calls=%async_computation.4 | async-start | bytes 2228224 | tf_op jit(solution)/shard_map/all_gather | solution.py:232
  34.2 5.1 %collective-permute-start = (bf16[4,1024,128]{2,1,0:T(8,128)(2,1)}, bf16[4,1024,128]{2,1,0:T(8,128)(2,1)}, u32[]{:S(2)}, u32[]{:S(2)}) collective-permute-start(bf16[4,1024,128]{2,1,0:T(8,128)(2,1)} %get-tuple-element.16), channel_id=1, source_target_pairs={{0,16},{16,0},{1,17},{17,1},{2,18},{18,2},{3,19},{19,3},{4,20},{20... | collective-permute-start | bytes 3145736 | tf_op jit(solution)/shard_map/ppermute | solution.py:177
  41.0 15.6 %collective-permute-start.3 = (bf16[1024,128]{1,0:T(8,128)(2,1)S(1)}, bf16[1024,128]{1,0:T(8,128)(2,1)S(1)}, u32[]{:S(2)}, u32[]{:S(2)}) collective-permute-start(bf16[1024,128]{1,0:T(8,128)(2,1)S(1)} %get-tuple-element.25), channel_id=1, source_target_pairs={{0,768},{256,0},{512,256},{768,512},{1,769},{257,1},{513,257},{769... | collective-permute-start | bytes 786440 | tf_op jit(solution)/shard_map/ppermute | solution.py:177
  45.6 14.5 %collective-permute-start.2 = (bf16[1024,128]{1,0:T(8,128)(2,1)S(1)}, bf16[1024,128]{1,0:T(8,128)(2,1)S(1)}, u32[]{:S(2)}, u32[]{:S(2)}) collective-permute-start(bf16[1024,128]{1,0:T(8,128)(2,1)S(1)} %get-tuple-element.26), channel_id=1, source_target_pairs={{0,512},{256,768},{512,0},{768,256},{1,513},{257,769},{513,1},{769... | collective-permute-start | bytes 786440 | tf_op jit(solution)/shard_map/ppermute | solution.py:177
  47.9 19.6 %collective-permute-start.1 = (bf16[1024,128]{1,0:T(8,128)(2,1)S(1)}, bf16[1024,128]{1,0:T(8,128)(2,1)S(1)}, u32[]{:S(2)}, u32[]{:S(2)}) collective-permute-start(bf16[1024,128]{1,0:T(8,128)(2,1)S(1)} %get-tuple-element.24), channel_id=1, source_target_pairs={{0,256},{256,512},{512,768},{768,0},{1,257},{257,513},{513,769},{7... | collective-permute-start | bytes 786440 | tf_op jit(solution)/shard_map/ppermute | solution.py:177
  71.4 47.5 %all-to-all-start.1 = ((bf16[64,16,640]{2,1,0:T(8,128)(2,1)}), bf16[64,16,640]{2,1,0:T(8,128)(2,1)S(1)}, u32[]{:S(2)}, u32[]{:S(2)}) async-start(bf16[64,16,640]{2,1,0:T(8,128)(2,1)} %gather_fusion), calls=%async_computation.1 | async-start | bytes 2621440 | tf_op jit(solution)/shard_map/all_to_all | solution.py:219
  79.7 7.2 %collective-permute-start.6 = (bf16[4,64,128]{2,1,0:T(8,128)(2,1)}, bf16[4,64,128]{2,1,0:T(8,128)(2,1)S(1)}, u32[]{:S(2)}, u32[]{:S(2)}) collective-permute-start(bf16[4,64,128]{2,1,0:T(8,128)(2,1)} %get-tuple-element.28), channel_id=1, source_target_pairs={{0,3},{1,0},{2,1},{3,2},{4,7},{5,4},{6,5},{7,6},{8,11},{9,8},{10,9... | collective-permute-start | bytes 196616 | tf_op jit(solution)/shard_map/ppermute | solution.py:177
  81.6 9.5 %collective-permute-start.5 = (bf16[4,64,128]{2,1,0:T(8,128)(2,1)}, bf16[4,64,128]{2,1,0:T(8,128)(2,1)S(1)}, u32[]{:S(2)}, u32[]{:S(2)}) collective-permute-start(bf16[4,64,128]{2,1,0:T(8,128)(2,1)} %get-tuple-element.29), channel_id=1, source_target_pairs={{0,2},{1,3},{2,0},{3,1},{4,6},{5,7},{6,4},{7,5},{8,10},{9,11},{10,... | collective-permute-start | bytes 196616 | tf_op jit(solution)/shard_map/ppermute | solution.py:177
  83.6 8.8 %collective-permute-start.4 = (bf16[4,64,128]{2,1,0:T(8,128)(2,1)S(1)}, bf16[4,64,128]{2,1,0:T(8,128)(2,1)}, u32[]{:S(2)}, u32[]{:S(2)}) collective-permute-start(bf16[4,64,128]{2,1,0:T(8,128)(2,1)S(1)} %get-tuple-element.27), channel_id=1, source_target_pairs={{0,1},{1,2},{2,3},{3,0},{4,5},{5,6},{6,7},{7,4},{8,9},{9,10},{10,1... | collective-permute-start | bytes 196616 | tf_op jit(solution)/shard_map/ppermute | solution.py:177
  93.3 22.9 %collective-permute-start.9 = (bf16[64,128]{1,0:T(8,128)(2,1)S(1)}, bf16[64,128]{1,0:T(8,128)(2,1)S(1)}, u32[]{:S(2)}, u32[]{:S(2)}) collective-permute-start(bf16[64,128]{1,0:T(8,128)(2,1)S(1)} %get-tuple-element.31), channel_id=1, source_target_pairs={{0,12},{1,13},{2,14},{3,15},{4,0},{5,1},{6,2},{7,3},{8,4},{9,5},{1... | collective-permute-start | bytes 49160 | tf_op jit(solution)/shard_map/ppermute | solution.py:177
  105.6 13.3 %collective-permute-start.8 = (bf16[64,128]{1,0:T(8,128)(2,1)S(1)}, bf16[64,128]{1,0:T(8,128)(2,1)S(1)}, u32[]{:S(2)}, u32[]{:S(2)}) collective-permute-start(bf16[64,128]{1,0:T(8,128)(2,1)S(1)} %get-tuple-element.32), channel_id=1, source_target_pairs={{0,8},{1,9},{2,10},{3,11},{4,12},{5,13},{6,14},{7,15},{8,0},{9,1},... | collective-permute-start | bytes 49160 | tf_op jit(solution)/shard_map/ppermute | solution.py:177
  109.0 9.9 %collective-permute-start.7 = (bf16[64,128]{1,0:T(8,128)(2,1)S(1)}, bf16[64,128]{1,0:T(8,128)(2,1)S(1)}, u32[]{:S(2)}, u32[]{:S(2)}) collective-permute-start(bf16[64,128]{1,0:T(8,128)(2,1)S(1)} %get-tuple-element.30), channel_id=1, source_target_pairs={{0,4},{1,5},{2,6},{3,7},{4,8},{5,9},{6,10},{7,11},{8,12},{9,13},{1... | collective-permute-start | bytes 49160 | tf_op jit(solution)/shard_map/ppermute | solution.py:177
  119.6 14.9 %all-to-all-start.2 = ((bf16[8,64,128]{2,1,0:T(8,128)(2,1)}), bf16[8,64,128]{2,1,0:T(8,128)(2,1)S(1)}, u32[]{:S(2)}, u32[]{:S(2)}) async-start(bf16[8,64,128]{2,1,0:T(8,128)(2,1)} %broadcast_in_dim.20), calls=%async_computation.2 | async-start | bytes 262144 | tf_op jit(solution)/shard_map/all_to_all | solution.py:219
  126.7 1.6 %copy-start.2 = (bf16[1024,1024]{1,0:T(8,128)(2,1)S(1)}, bf16[1024,1024]{1,0:T(8,128)(2,1)}, u32[]{:S(2)}) copy-start(bf16[1024,1024]{1,0:T(8,128)(2,1)} %all-gather.2.cloned.1.call-done.w_ref) | copy-start | bytes 6291460
Sparse Core Ops, SparseCore 0:
  36.9 70.8 all-gather.1

commit v8 on v7

--- a/solution.py
+++ b/solution.py
@@ -185,13 +185,14 @@
     return functools.reduce(jnp.add, [value.astype(F32) for value in values])
 
 
-def scatter_sum(value, axis):
+def scatter_sum(value, axis, beside):
     size, me = lax.axis_size(axis), lax.axis_index(axis)
     came = [
         permuted(pick(value, (me + step) & (size - 1)), axis, lambda i, step=step: (i + step) % size)
         for step in range(1, size)
     ]
-    return added(pick(value, me), *came).astype(BF16)
+    came, beside = lax.optimization_barrier((came, beside))
+    return added(pick(value, me), *came).astype(BF16), beside
 
 
 def ring_of_rings_sum(value, axis, inner):
@@ -261,9 +262,9 @@
         name="term",
     )(lax.axis_index("core").reshape(1), own_lengths, uvqk, grad_out, seg_col, seg_row)
     part = added(mine, permuted(other, "core", lambda i: i ^ 1)).astype(BF16)
-    part = scatter_sum(part, "x")
+    part, block = scatter_sum(part, "x", block[source_of])
     own_rows = width // n_z
-    part, block = lax.optimization_barrier((part, block[source_of]))
+    part, block = lax.optimization_barrier((part, block))
     block = exchange(block)
     part = ring_of_rings_sum(part.reshape(n_z, own_rows, block_cols), "z", min(4, n_z)).astype(BF16)
     part = lax.optimization_barrier((part, block))[0]

time: 157 us -> 157 us (level)
  waiting for transfers between devices: 28.9 us -> 22.2 us
  starting transfers between devices: 74.9 us -> 78.8 us
    ppermute x10, waiting for transfers between devices: 27.6 us -> 10.8 us  [permuted(): return lax.ppermute(value, axis, [(i, target(i)) for i in range(size)])]
    all_to_all x3, waiting for transfers between devices: 1.33 us -> 11.4 us  [exchange(): return lax.all_to_all(value, axes, split_axis=0, concat_axis=0, tiled=True)]
    all_to_all x3, starting transfers between devices: 32.8 us -> 35.3 us  [exchange(): return lax.all_to_all(value, axes, split_axis=0, concat_axis=0, tiled=True)]
  transfers between devices with their start and end apart: 14 -> 14, of which waited for: 8 -> 7; matrix products, arithmetic and copies ran while one was open for 7% -> 7% of each run, Pallas kernels for 5% -> 5%
where the time goes in v8:
time: 157 us; the launch traced here: 156 us
  starting transfers between devices  78.8 us (50%)
  waiting for transfers between devices  22.2 us (14%)
  between operations  15 us (10%)
  blocking collectives  14.3 us (9%)
  Pallas kernels  10.6 us (7%)
  local copies, waits for them, and re-layouts  10.1 us (6%)
  other arithmetic  5.25 us (3%)
    ppermute x10, starting transfers between devices, permuted(): return lax.ppermute(value, axis, [(i, target(i)) for i in range(size)])  43.5 us
    all_to_all x3, starting transfers between devices, exchange(): return lax.all_to_all(value, axes, split_axis=0, concat_axis=0, tiled=True)  35.3 us
    all_to_all x1, blocking collectives, exchange(): return lax.all_to_all(value, axes, split_axis=0, concat_axis=0, tiled=True)  14.3 us
    all_to_all x3, waiting for transfers between devices, exchange(): return lax.all_to_all(value, axes, split_axis=0, concat_axis=0, tiled=True)  11.4 us
    ppermute x10, waiting for transfers between devices, permuted(): return lax.ppermute(value, axis, [(i, target(i)) for i in range(size)])  10.8 us
    pallas_call x1, Pallas kernels, local(): pl.pallas_call(functools.partial(back_kernel, keep), out_shape=jax.ShapeD...  5.02 us
  transfers between devices with their start and end apart: 14, of which 7 were waited for; matrix products, arithmetic and copies ran while one was open for 7% of the time, Pallas kernels for 5%

profile of v8, /device:TPU:1, one launch (start us, length us, event | category | flops | bytes accessed | tf_op | source)
XLA Modules:
  0.0 156.2 jit_solution(7195561737564704558)
XLA Ops:
  7.2 2.4 %pack.1 = bf16[64,16,640]{2,1,0:T(8,128)(2,1)} custom-call(bf16[192,4096]{1,0:T(8,128)(2,1)} %x_ref.3, bf16[192,1024]{1,0:T(8,128)(2,1)} %g_ref.3), custom_call_target="tpu_custom_call" | custom-call | bytes 8192 | tf_op jit(solution)/shard_map/pack/pallas_call | solution.py:235
  9.6 0.0 copy-start.5
  9.6 0.0 copy-start.3
  9.6 0.0 copy-start
  9.7 0.0 copy-start.1
  9.7 19.2 %all-to-all-start = ((bf16[64,16,640]{2,1,0:T(8,128)(2,1)}), bf16[64,16,640]{2,1,0:T(8,128)(2,1)}, u32[]{:S(2)}, u32[]{:S(2)}) async-start(bf16[64,16,640]{2,1,0:T(8,128)(2,1)} %pack.1), calls=%async_computation | async-start | bytes 2621440 | tf_op jit(solution)/shard_map/all_to_all | solution.py:220
  28.8 0.0 all-gather.2.cloned.1.call-start
  28.9 0.6 fusion.9
  30.2 0.8 constant_dynamic-slice_fusion
  31.0 0.1 copy.26.lengths_ref
  31.1 0.1 copy.22.seg_col_ref
  31.2 3.1 %term.1 = (bf16[4,1024,128]{2,1,0:T(8,128)(2,1)S(1)}, bf16[4,1024,128]{2,1,0:T(8,128)(2,1)}) custom-call(s32[1]{0:T(128)} %bitcast.core_ref, s32[1,3]{1,0:T(1,128)S(1)} %copy.26.lengths_ref, bf16[192,4096]{1,0:T(8,128)(2,1)S(1)} %copy-done, bf16[192,1024]{1,0:T(8,128)(2,1)S(1)} %copy-done.1, s32[64,1]{1,0:T(8,128)S(1)} %copy.22.seg_col_ref, ...), custom_call_target="tpu_custom_call" | custom-call | bytes 8192 | tf_op jit(solution)/shard_map/term/pallas_call | solution.py:254
  34.3 2.5 %collective-permute-start = (bf16[4,1024,128]{2,1,0:T(8,128)(2,1)}, bf16[4,1024,128]{2,1,0:T(8,128)(2,1)}, u32[]{:S(2)}, u32[]{:S(2)}) collective-permute-start(bf16[4,1024,128]{2,1,0:T(8,128)(2,1)} %get-tuple-element.20), channel_id=1, source_target_pairs={{0,16},{16,0},{1,17},{17,1},{2,18},{18,2},{3,19},{19,3},{4,20},{20... | collective-permute-start | bytes 3145736 | tf_op jit(solution)/shard_map/ppermute | solution.py:177
  36.8 0.0 all-gather.2.cloned.1.call-update
  36.9 0.1 select_reduce_fusion
  37.0 2.5 %collective-permute-done = bf16[4,1024,128]{2,1,0:T(8,128)(2,1)} collective-permute-done((bf16[4,1024,128]{2,1,0:T(8,128)(2,1)}, bf16[4,1024,128]{2,1,0:T(8,128)(2,1)}, u32[]{:S(2)}, u32[]{:S(2)}) %collective-permute-start) | collective-permute-done | bytes 1048608 | tf_op jit(solution)/shard_map/ppermute | solution.py:177
  39.5 1.6 %add_convert_fusion = bf16[4,1024,128]{2,1,0:T(8,128)(2,1)S(1)} fusion(bf16[4,1024,128]{2,1,0:T(8,128)(2,1)} %collective-permute-done, bf16[4,1024,128]{2,1,0:T(8,128)(2,1)S(1)} %get-tuple-element.19), kind=kLoop, calls=%fused_computation.1 | loop fusion | flops 2097152 | bytes 3145728 | tf_op jit(solution)/shard_map/convert_element_type | solution.py:264
  41.1 1.0 copy-done.4
  42.0 0.1 dynamic-slice_bitcast_fusion
  42.1 3.1 %collective-permute-start.1 = (bf16[1024,128]{1,0:T(8,128)(2,1)S(1)}, bf16[1024,128]{1,0:T(8,128)(2,1)S(1)}, u32[]{:S(2)}, u32[]{:S(2)}) collective-permute-start(bf16[1024,128]{1,0:T(8,128)(2,1)S(1)} %get-tuple-element.34), channel_id=1, source_target_pairs={{0,256},{256,512},{512,768},{768,0},{1,257},{257,513},{513,769},{7... | collective-permute-start | bytes 786440 | tf_op jit(solution)/shard_map/ppermute | solution.py:177
  45.2 4.5 %collective-permute-start.2 = (bf16[1024,128]{1,0:T(8,128)(2,1)S(1)}, bf16[1024,128]{1,0:T(8,128)(2,1)S(1)}, u32[]{:S(2)}, u32[]{:S(2)}) collective-permute-start(bf16[1024,128]{1,0:T(8,128)(2,1)S(1)} %get-tuple-element.33), channel_id=1, source_target_pairs={{0,512},{256,768},{512,0},{768,256},{1,513},{257,769},{513,1},{769... | collective-permute-start | bytes 786440 | tf_op jit(solution)/shard_map/ppermute | solution.py:177
  49.8 3.0 %collective-permute-start.3 = (bf16[1024,128]{1,0:T(8,128)(2,1)S(1)}, bf16[1024,128]{1,0:T(8,128)(2,1)}, u32[]{:S(2)}, u32[]{:S(2)}) collective-permute-start(bf16[1024,128]{1,0:T(8,128)(2,1)S(1)} %get-tuple-element.32), channel_id=1, source_target_pairs={{0,768},{256,0},{512,256},{768,512},{1,769},{257,1},{513,257},{769... | collective-permute-start | bytes 786440 | tf_op jit(solution)/shard_map/ppermute | solution.py:177
  52.8 10.2 %all-to-all-done = bf16[64,16,640]{2,1,0:T(8,128)(2,1)} async-done(((bf16[64,16,640]{2,1,0:T(8,128)(2,1)}), bf16[64,16,640]{2,1,0:T(8,128)(2,1)}, u32[]{:S(2)}, u32[]{:S(2)}) %all-to-all-start) | async-done | bytes 1310752 | tf_op jit(solution)/shard_map/all_to_all | solution.py:220
  63.0 3.1 %gather_fusion = bf16[64,16,640]{2,1,0:T(8,128)(2,1)} fusion(bf16[64,16,640]{2,1,0:T(8,128)(2,1)} %all-to-all-done, s32[1024]{0:T(1024)S(1)} %pad_clamp_fusion), kind=kCustom, calls=%fused_computation | custom fusion | bytes 2621696 | tf_op jit(solution)/shard_map/gather | solution.py:265
  66.1 0.0 collective-permute-done.1
  66.1 0.5 collective-permute-done.2
  66.6 1.9 %fusion.2 = bf16[1024,128]{1,0:T(8,128)(2,1)} fusion(bf16[1024,128]{1,0:T(8,128)(2,1)} %collective-permute-done.3, bf16[1024,128]{1,0:T(8,128)(2,1)S(1)} %collective-permute-done.2, bf16[1024,128]{1,0:T(8,128)(2,1)S(1)} %collective-permute-done.1, bf16[4,1024,128]{2,1,0:T(8,128)(2,1)} %copy-done.4, s32[]{:T(128)S(6)} %select_n.64), kind=kLoop, calls=%fused_computation.5 | loop fusion | flops 1048576 | bytes 1310724 | tf_op jit(solution)/shard_map/convert_element_type | solution.py:195
  68.5 9.8 %all-to-all-start.1 = ((bf16[64,16,640]{2,1,0:T(8,128)(2,1)}), bf16[64,16,640]{2,1,0:T(8,128)(2,1)S(1)}, u32[]{:S(2)}, u32[]{:S(2)}) async-start(bf16[64,16,640]{2,1,0:T(8,128)(2,1)} %gather_fusion), calls=%async_computation.1 | async-start | bytes 2621440 | tf_op jit(solution)/shard_map/all_to_all | solution.py:220
  78.3 1.6 %dynamic-slice_bitcast_fusion.5 = (bf16[4,64,128]{2,1,0:T(8,128)(2,1)S(1)}, bf16[4,64,128]{2,1,0:T(8,128)(2,1)}, bf16[4,64,128]{2,1,0:T(8,128)(2,1)}) fusion(bf16[4,4,64,128]{3,2,1,0:T(8,128)(2,1)} %bitcast.39, s32[]{:T(128)S(6)} %select_n.71, s32[]{:T(128)S(6)} %select_n.73, s32[]{:T(128)S(6)} %select_n.72), kind=kLoop, calls=%fused_computation.17 | loop fusion | bytes 393228 | tf_op jit(solution)/shard_map/jit(dynamic_index_in_dim)/squeeze | solution.py:181
  79.8 1.9 %collective-permute-start.6 = (bf16[4,64,128]{2,1,0:T(8,128)(2,1)}, bf16[4,64,128]{2,1,0:T(8,128)(2,1)S(1)}, u32[]{:S(2)}, u32[]{:S(2)}) collective-permute-start(bf16[4,64,128]{2,1,0:T(8,128)(2,1)} %get-tuple-element.36), channel_id=1, source_target_pairs={{0,3},{1,0},{2,1},{3,2},{4,7},{5,4},{6,5},{7,6},{8,11},{9,8},{10,9... | collective-permute-start | bytes 196616 | tf_op jit(solution)/shard_map/ppermute | solution.py:177
  81.8 1.9 %collective-permute-start.5 = (bf16[4,64,128]{2,1,0:T(8,128)(2,1)}, bf16[4,64,128]{2,1,0:T(8,128)(2,1)S(1)}, u32[]{:S(2)}, u32[]{:S(2)}) collective-permute-start(bf16[4,64,128]{2,1,0:T(8,128)(2,1)} %get-tuple-element.37), channel_id=1, source_target_pairs={{0,2},{1,3},{2,0},{3,1},{4,6},{5,7},{6,4},{7,5},{8,10},{9,11},{10,... | collective-permute-start | bytes 196616 | tf_op jit(solution)/shard_map/ppermute | solution.py:177
  83.7 3.4 %collective-permute-start.4 = (bf16[4,64,128]{2,1,0:T(8,128)(2,1)S(1)}, bf16[4,64,128]{2,1,0:T(8,128)(2,1)}, u32[]{:S(2)}, u32[]{:S(2)}) collective-permute-start(bf16[4,64,128]{2,1,0:T(8,128)(2,1)S(1)} %get-tuple-element.35), channel_id=1, source_target_pairs={{0,1},{1,2},{2,3},{3,0},{4,5},{5,6},{6,7},{7,4},{8,9},{9,10},{10,1... | collective-permute-start | bytes 196616 | tf_op jit(solution)/shard_map/ppermute | solution.py:177
  87.1 4.0 %collective-permute-done.5 = bf16[4,64,128]{2,1,0:T(8,128)(2,1)S(1)} collective-permute-done((bf16[4,64,128]{2,1,0:T(8,128)(2,1)}, bf16[4,64,128]{2,1,0:T(8,128)(2,1)S(1)}, u32[]{:S(2)}, u32[]{:S(2)}) %collective-permute-start.5) | collective-permute-done | bytes 65568 | tf_op jit(solution)/shard_map/ppermute | solution.py:177
  91.1 1.7 %collective-permute-done.4 = bf16[4,64,128]{2,1,0:T(8,128)(2,1)} collective-permute-done((bf16[4,64,128]{2,1,0:T(8,128)(2,1)S(1)}, bf16[4,64,128]{2,1,0:T(8,128)(2,1)}, u32[]{:S(2)}, u32[]{:S(2)}) %collective-permute-start.4) | collective-permute-done | bytes 65568 | tf_op jit(solution)/shard_map/ppermute | solution.py:177
  92.8 0.9 fusion.5
  93.8 11.9 %collective-permute-start.9 = (bf16[64,128]{1,0:T(8,128)(2,1)S(1)}, bf16[64,128]{1,0:T(8,128)(2,1)S(1)}, u32[]{:S(2)}, u32[]{:S(2)}) collective-permute-start(bf16[64,128]{1,0:T(8,128)(2,1)S(1)} %get-tuple-element.39), channel_id=1, source_target_pairs={{0,12},{1,13},{2,14},{3,15},{4,0},{5,1},{6,2},{7,3},{8,4},{9,5},{1... | collective-permute-start | bytes 49160 | tf_op jit(solution)/shard_map/ppermute | solution.py:177
  105.7 4.0 %collective-permute-start.8 = (bf16[64,128]{1,0:T(8,128)(2,1)S(1)}, bf16[64,128]{1,0:T(8,128)(2,1)S(1)}, u32[]{:S(2)}, u32[]{:S(2)}) collective-permute-start(bf16[64,128]{1,0:T(8,128)(2,1)S(1)} %get-tuple-element.40), channel_id=1, source_target_pairs={{0,8},{1,9},{2,10},{3,11},{4,12},{5,13},{6,14},{7,15},{8,0},{9,1},... | collective-permute-start | bytes 49160 | tf_op jit(solution)/shard_map/ppermute | solution.py:177
  109.7 7.3 %collective-permute-start.7 = (bf16[64,128]{1,0:T(8,128)(2,1)S(1)}, bf16[64,128]{1,0:T(8,128)(2,1)S(1)}, u32[]{:S(2)}, u32[]{:S(2)}) collective-permute-start(bf16[64,128]{1,0:T(8,128)(2,1)S(1)} %get-tuple-element.38), channel_id=1, source_target_pairs={{0,4},{1,5},{2,6},{3,7},{4,8},{5,9},{6,10},{7,11},{8,12},{9,13},{1... | collective-permute-start | bytes 49160 | tf_op jit(solution)/shard_map/ppermute | solution.py:177
  117.0 2.0 %collective-permute-done.8 = bf16[64,128]{1,0:T(8,128)(2,1)S(1)} collective-permute-done((bf16[64,128]{1,0:T(8,128)(2,1)S(1)}, bf16[64,128]{1,0:T(8,128)(2,1)S(1)}, u32[]{:S(2)}, u32[]{:S(2)}) %collective-permute-start.8) | collective-permute-done | bytes 16416 | tf_op jit(solution)/shard_map/ppermute | solution.py:177
  119.1 0.7 broadcast_in_dim.20
  119.7 6.4 %all-to-all-start.2 = ((bf16[8,64,128]{2,1,0:T(8,128)(2,1)}), bf16[8,64,128]{2,1,0:T(8,128)(2,1)S(1)}, u32[]{:S(2)}, u32[]{:S(2)}) async-start(bf16[8,64,128]{2,1,0:T(8,128)(2,1)} %broadcast_in_dim.20), calls=%async_computation.2 | async-start | bytes 262144 | tf_op jit(solution)/shard_map/all_to_all | solution.py:220
  126.1 0.1 copy.27.lengths_ref
  126.2 1.6 %copy-done.2 = bf16[1024,1024]{1,0:T(8,128)(2,1)S(1)} copy-done((bf16[1024,1024]{1,0:T(8,128)(2,1)S(1)}, bf16[1024,1024]{1,0:T(8,128)(2,1)}, u32[]{:S(2)}) %copy-start.2) | copy-done | bytes 2097176
  127.8 5.0 %back.1 = bf16[192,4096]{1,0:T(8,128)(2,1)} custom-call(s32[1,3]{1,0:T(1,128)S(1)} %copy.27.lengths_ref, bf16[192,4096]{1,0:T(8,128)(2,1)S(1)} %copy-done, bf16[192,1024]{1,0:T(8,128)(2,1)S(1)} %copy-done.1, bf16[64,16,640]{2,1,0:T(8,128)(2,1)S(1)} %all-to-all-done.1.came_ref, bf16[1024,1024]{1,0:T(8,128)(2,1)S(1)} %copy-done.2, ...), custom_call_target="tpu_custom_call" | custom-call | flops 1610612736 | bytes 8388608 | tf_op jit(solution)/shard_map/back/pallas_call | solution.py:272
  132.8 1.2 all-to-all-done.2
  134.1 14.3 %all_to_all.20 = bf16[8,64,128]{2,1,0:T(8,128)(2,1)S(1)} all-to-all(bf16[8,64,128]{2,1,0:T(8,128)(2,1)S(1)} %broadcast_in_dim.21), channel_id=1, replica_groups=mesh['x'=4,'y'=8,'core'=2,'z'=16] {'x','core'}, dimensions={0} | all-to-all | bytes 262144 | tf_op jit(solution)/shard_map/all_to_all | solution.py:220
  148.4 0.2 copy.25
  148.6 0.8 reshape.46
  (20 shorter events, 0.1 us)
Async XLA Ops:
  9.6 19.3 %copy-start.5 = (s32[64]{0:T(128)S(1)}, s32[64]{0:T(128)}, u32[]{:S(2)}) copy-start(s32[64]{0:T(128)} %param.11) | copy-start | bytes 772
  9.6 21.4 %copy-start.3 = (s32[1,64]{1,0:T(1,128)S(1)}, s32[1,64]{1,0:T(1,128)}, u32[]{:S(2)}) copy-start(s32[1,64]{1,0:T(1,128)} %seg_row_ref.3) | copy-start | bytes 772
  9.6 21.5 %copy-start = (bf16[192,4096]{1,0:T(8,128)(2,1)S(1)}, bf16[192,4096]{1,0:T(8,128)(2,1)}, u32[]{:S(2)}) copy-start(bf16[192,4096]{1,0:T(8,128)(2,1)} %x_ref.3) | copy-start | bytes 4718596
  9.7 21.5 %copy-start.1 = (bf16[192,1024]{1,0:T(8,128)(2,1)S(1)}, bf16[192,1024]{1,0:T(8,128)(2,1)}, u32[]{:S(2)}) copy-start(bf16[192,1024]{1,0:T(8,128)(2,1)} %g_ref.3) | copy-start | bytes 1179652
  9.7 53.3 %all-to-all-start = ((bf16[64,16,640]{2,1,0:T(8,128)(2,1)}), bf16[64,16,640]{2,1,0:T(8,128)(2,1)}, u32[]{:S(2)}, u32[]{:S(2)}) async-start(bf16[64,16,640]{2,1,0:T(8,128)(2,1)} %pack.1), calls=%async_computation | async-start | bytes 2621440 | tf_op jit(solution)/shard_map/all_to_all | solution.py:220
  28.8 97.3 %all-gather.2.cloned.1.call-start = ((), (), s32[]{:S(2)}) async-start(), calls=%async_computation.4 | async-start | bytes 2228224 | tf_op jit(solution)/shard_map/all_gather | solution.py:233
  34.3 5.1 %collective-permute-start = (bf16[4,1024,128]{2,1,0:T(8,128)(2,1)}, bf16[4,1024,128]{2,1,0:T(8,128)(2,1)}, u32[]{:S(2)}, u32[]{:S(2)}) collective-permute-start(bf16[4,1024,128]{2,1,0:T(8,128)(2,1)} %get-tuple-element.20), channel_id=1, source_target_pairs={{0,16},{16,0},{1,17},{17,1},{2,18},{18,2},{3,19},{19,3},{4,20},{20... | collective-permute-start | bytes 3145736 | tf_op jit(solution)/shard_map/ppermute | solution.py:177
  41.0 1.0 copy-start.4
  42.1 24.0 %collective-permute-start.1 = (bf16[1024,128]{1,0:T(8,128)(2,1)S(1)}, bf16[1024,128]{1,0:T(8,128)(2,1)S(1)}, u32[]{:S(2)}, u32[]{:S(2)}) collective-permute-start(bf16[1024,128]{1,0:T(8,128)(2,1)S(1)} %get-tuple-element.34), channel_id=1, source_target_pairs={{0,256},{256,512},{512,768},{768,0},{1,257},{257,513},{513,769},{7... | collective-permute-start | bytes 786440 | tf_op jit(solution)/shard_map/ppermute | solution.py:177
  45.2 21.3 %collective-permute-start.2 = (bf16[1024,128]{1,0:T(8,128)(2,1)S(1)}, bf16[1024,128]{1,0:T(8,128)(2,1)S(1)}, u32[]{:S(2)}, u32[]{:S(2)}) collective-permute-start(bf16[1024,128]{1,0:T(8,128)(2,1)S(1)} %get-tuple-element.33), channel_id=1, source_target_pairs={{0,512},{256,768},{512,0},{768,256},{1,513},{257,769},{513,1},{769... | collective-permute-start | bytes 786440 | tf_op jit(solution)/shard_map/ppermute | solution.py:177
  49.8 16.8 %collective-permute-start.3 = (bf16[1024,128]{1,0:T(8,128)(2,1)S(1)}, bf16[1024,128]{1,0:T(8,128)(2,1)}, u32[]{:S(2)}, u32[]{:S(2)}) collective-permute-start(bf16[1024,128]{1,0:T(8,128)(2,1)S(1)} %get-tuple-element.32), channel_id=1, source_target_pairs={{0,768},{256,0},{512,256},{768,512},{1,769},{257,1},{513,257},{769... | collective-permute-start | bytes 786440 | tf_op jit(solution)/shard_map/ppermute | solution.py:177
  68.5 50.6 %all-to-all-start.1 = ((bf16[64,16,640]{2,1,0:T(8,128)(2,1)}), bf16[64,16,640]{2,1,0:T(8,128)(2,1)S(1)}, u32[]{:S(2)}, u32[]{:S(2)}) async-start(bf16[64,16,640]{2,1,0:T(8,128)(2,1)} %gather_fusion), calls=%async_computation.1 | async-start | bytes 2621440 | tf_op jit(solution)/shard_map/all_to_all | solution.py:220
  79.8 7.2 %collective-permute-start.6 = (bf16[4,64,128]{2,1,0:T(8,128)(2,1)}, bf16[4,64,128]{2,1,0:T(8,128)(2,1)S(1)}, u32[]{:S(2)}, u32[]{:S(2)}) collective-permute-start(bf16[4,64,128]{2,1,0:T(8,128)(2,1)} %get-tuple-element.36), channel_id=1, source_target_pairs={{0,3},{1,0},{2,1},{3,2},{4,7},{5,4},{6,5},{7,6},{8,11},{9,8},{10,9... | collective-permute-start | bytes 196616 | tf_op jit(solution)/shard_map/ppermute | solution.py:177
  81.8 9.3 %collective-permute-start.5 = (bf16[4,64,128]{2,1,0:T(8,128)(2,1)}, bf16[4,64,128]{2,1,0:T(8,128)(2,1)S(1)}, u32[]{:S(2)}, u32[]{:S(2)}) collective-permute-start(bf16[4,64,128]{2,1,0:T(8,128)(2,1)} %get-tuple-element.37), channel_id=1, source_target_pairs={{0,2},{1,3},{2,0},{3,1},{4,6},{5,7},{6,4},{7,5},{8,10},{9,11},{10,... | collective-permute-start | bytes 196616 | tf_op jit(solution)/shard_map/ppermute | solution.py:177
  83.7 9.1 %collective-permute-start.4 = (bf16[4,64,128]{2,1,0:T(8,128)(2,1)S(1)}, bf16[4,64,128]{2,1,0:T(8,128)(2,1)}, u32[]{:S(2)}, u32[]{:S(2)}) collective-permute-start(bf16[4,64,128]{2,1,0:T(8,128)(2,1)S(1)} %get-tuple-element.35), channel_id=1, source_target_pairs={{0,1},{1,2},{2,3},{3,0},{4,5},{5,6},{6,7},{7,4},{8,9},{9,10},{10,1... | collective-permute-start | bytes 196616 | tf_op jit(solution)/shard_map/ppermute | solution.py:177
  93.8 23.2 %collective-permute-start.9 = (bf16[64,128]{1,0:T(8,128)(2,1)S(1)}, bf16[64,128]{1,0:T(8,128)(2,1)S(1)}, u32[]{:S(2)}, u32[]{:S(2)}) collective-permute-start(bf16[64,128]{1,0:T(8,128)(2,1)S(1)} %get-tuple-element.39), channel_id=1, source_target_pairs={{0,12},{1,13},{2,14},{3,15},{4,0},{5,1},{6,2},{7,3},{8,4},{9,5},{1... | collective-permute-start | bytes 49160 | tf_op jit(solution)/shard_map/ppermute | solution.py:177
  105.7 13.4 %collective-permute-start.8 = (bf16[64,128]{1,0:T(8,128)(2,1)S(1)}, bf16[64,128]{1,0:T(8,128)(2,1)S(1)}, u32[]{:S(2)}, u32[]{:S(2)}) collective-permute-start(bf16[64,128]{1,0:T(8,128)(2,1)S(1)} %get-tuple-element.40), channel_id=1, source_target_pairs={{0,8},{1,9},{2,10},{3,11},{4,12},{5,13},{6,14},{7,15},{8,0},{9,1},... | collective-permute-start | bytes 49160 | tf_op jit(solution)/shard_map/ppermute | solution.py:177
  109.7 9.3 %collective-permute-start.7 = (bf16[64,128]{1,0:T(8,128)(2,1)S(1)}, bf16[64,128]{1,0:T(8,128)(2,1)S(1)}, u32[]{:S(2)}, u32[]{:S(2)}) collective-permute-start(bf16[64,128]{1,0:T(8,128)(2,1)S(1)} %get-tuple-element.38), channel_id=1, source_target_pairs={{0,4},{1,5},{2,6},{3,7},{4,8},{5,9},{6,10},{7,11},{8,12},{9,13},{1... | collective-permute-start | bytes 49160 | tf_op jit(solution)/shard_map/ppermute | solution.py:177
  119.7 14.3 %all-to-all-start.2 = ((bf16[8,64,128]{2,1,0:T(8,128)(2,1)}), bf16[8,64,128]{2,1,0:T(8,128)(2,1)S(1)}, u32[]{:S(2)}, u32[]{:S(2)}) async-start(bf16[8,64,128]{2,1,0:T(8,128)(2,1)} %broadcast_in_dim.20), calls=%async_computation.2 | async-start | bytes 262144 | tf_op jit(solution)/shard_map/all_to_all | solution.py:220
  126.2 1.6 %copy-start.2 = (bf16[1024,1024]{1,0:T(8,128)(2,1)S(1)}, bf16[1024,1024]{1,0:T(8,128)(2,1)}, u32[]{:S(2)}) copy-start(bf16[1024,1024]{1,0:T(8,128)(2,1)} %all-gather.2.cloned.1.call-done.w_ref) | copy-start | bytes 6291460
Sparse Core Ops, SparseCore 0:
  37.0 70.3 all-gather.1
